TPU v7x, 128 devices: a whole 4x4x4 slice. The times are simulated.
128 devices in a mesh: row: 16 (over x, z), col: 8 (over y, core).
Axes of the slice: x: 4, y: 4, z: 4, core: 2. Of those that a mesh axis runs over, the one named last changes fastest.
Arguments:
- trailing: float32 [20480, 20480], P('row', 'col'), may hold values from -28 to 28
- panel_block: float32 [20480, 256], P('row', 'col'), as said below
Outputs:
- updated: float32 [20480, 20480], P('row', 'col')
Inputs may be any that keep to these rules, and one draw needn't show every extreme that they name: `panel_block`: entry (j, j) of each of the first 256 rows is 2 * sqrt(20480) plus a term within 7 of zero; every other entry lies within 7 of zero.
All inputs are finite; a program needn't handle non-finite values.
Results may differ from a plain program's by a relative error of at most 0.000064.
Values sent between devices are 32-bit elements; how exact they have to be, the bound alone decides.
No kernel may reach another device: no remote copies, remote signals or barrier semaphores. Data moves between devices by JAX's collectives and lax.ppermute only.
A program may use at most 128 MiB of HBM per device.

v0:
```python
import jax
import jax.numpy as jnp
from jax import lax
from jax.sharding import PartitionSpec as P


def from_root(block, axis, holder):
    block = jnp.where(lax.axis_index(axis) == holder, block, jnp.zeros_like(block))
    return lax.psum(block, axis)


def invert_small(matrix):
    highest = lax.Precision.HIGHEST
    normal_gram = jnp.dot(matrix.T, matrix, precision=highest)
    lower_factor = jnp.linalg.cholesky(normal_gram)
    return jax.scipy.linalg.cho_solve((lower_factor, True), matrix.T)


def shards(trailing, panel_block):
    highest = lax.Precision.HIGHEST
    row_index = lax.axis_index("row")
    col_index = lax.axis_index("col")
    ratio = lax.axis_size("row") // lax.axis_size("col")
    gathered = lax.all_gather(panel_block, "col", axis=1, tiled=True)
    local_rows = gathered.shape[0]
    width = gathered.shape[1]
    local_gram = jnp.dot(gathered.T, gathered, precision=highest)
    top_piece = jnp.where(row_index == 0, gathered[:width], jnp.zeros((width, width), jnp.float32))
    panel_gram, top_rows = lax.psum((local_gram, top_piece), "row")
    factor = jnp.linalg.cholesky(panel_gram)
    local_basis = jax.scipy.linalg.solve_triangular(factor, gathered.T, lower=True).T
    top_basis = jax.scipy.linalg.solve_triangular(factor, top_rows.T, lower=True).T
    global_rows = row_index * local_rows + lax.broadcasted_iota(jnp.int32, (local_rows, width), 0)
    column_ids = lax.broadcasted_iota(jnp.int32, (local_rows, width), 1)
    reflect_rows = local_basis + jnp.where(global_rows == column_ids, 1.0, 0.0).astype(jnp.float32)
    leading = top_basis + jnp.eye(width, dtype=jnp.float32)
    coupling = invert_small(leading).T
    pieces = []
    for offset in range(ratio):
        pieces.append(from_root(reflect_rows, "row", col_index * ratio + offset))
    reflect_cols = jnp.concatenate(pieces, axis=0)
    partial_rows = jnp.dot(trailing, reflect_cols, precision=highest)
    summed_rows = lax.psum(partial_rows, "col")
    products_rows = jnp.dot(summed_rows, coupling, precision=highest)
    cross_term = lax.psum(jnp.dot(reflect_rows.T, products_rows, precision=highest), "row")
    inner_map = jnp.dot(coupling.T, cross_term, precision=highest)
    adjust_rows = products_rows - 0.5 * jnp.dot(reflect_rows, inner_map, precision=highest)
    adjust_pieces = []
    for offset in range(ratio):
        adjust_pieces.append(from_root(adjust_rows, "row", col_index * ratio + offset))
    adjust_cols = jnp.concatenate(adjust_pieces, axis=0)
    first_term = jnp.dot(reflect_rows, adjust_cols.T, precision=highest)
    second_term = jnp.dot(adjust_rows, reflect_cols.T, precision=highest)
    return trailing - first_term - second_term


def solution(mesh):
    in_specs = (P("row", "col"), P("row", "col"))
    out_specs = P("row", "col")
    return jax.shard_map(shards, mesh=mesh, in_specs=in_specs, out_specs=out_specs, check_vma=False)
```

profile of v0, /device:TPU:1, one launch (start us, length us, event | category | flops | bytes accessed | tf_op | source)
XLA Modules:
  0.0 666.6 jit_solution(9710948631904089730)
XLA Ops:
  6.5 0.7 all-gather.2.cloned.1.call-update
  7.3 29.5 %all-gather.2.cloned.1.call-done = f32[1280,256]{0,1:T(8,128)} async-done(((f32[1280,32]{0,1:T(8,128)}), f32[1280,256]{0,1:T(8,128)}) %all-gather.2.cloned.1.call-update) | async-done | bytes 1310736 | tf_op jit(solution)/shard_map/all_gather | solution.py:24
  36.8 3.7 fusion.42
  40.8 0.7 select_bitcast_fusion
  41.5 81.8 %all-reduce.9.cloned.1.call-done = f32[256,256]{0,1:T(8,128)} async-done(((f32[256,256]{0,1:T(8,128)}), f32[256,256]{0,1:T(8,128)}) %all-reduce.9.cloned.1.call-update) | async-done | bytes 262160 | tf_op jit(solution)/shard_map/psum | solution.py:29
  123.3 1.1 copy.10
  124.4 1.0 fusion.9
  125.4 11.7 %cholesky.130 = f32[128,128]{1,0:T(8,128)S(1)} custom-call(f32[128,128]{1,0:T(8,128)S(1)} %cholesky.194), custom_call_target="Cholesky" | custom-call | tf_op jit(solution)/shard_map/jit(cholesky)/cholesky | solution.py:30
  137.1 9.8 %custom-call.23 = f32[1,128,128]{1,2,0:T(8,128)S(1)} custom-call(f32[1,128,128]{2,1,0:T(8,128)S(1)} %get-tuple-element.75), custom_call_target="InvertDiagBlocksLowerTriangular" | custom-call | tf_op jit(solution)/shard_map/jit(cholesky)/cholesky | solution.py:30
  147.5 11.7 %cholesky.147 = f32[128,128]{1,0:T(8,128)S(1)} custom-call(f32[128,128]{1,0:T(8,128)S(1)} %convolution_subtract_fusion.7), custom_call_target="Cholesky" | custom-call | tf_op jit(solution)/shard_map/jit(cholesky)/cholesky | solution.py:30
  159.2 0.7 compare_reduce_fusion.2
  161.3 4.2 while.6
  162.1 1.3 bitcast_dynamic-update-slice_fusion.4
  164.1 1.3 bitcast_dynamic-update-slice_fusion.4
  165.5 19.7 %custom-call.19 = f32[2,128,128]{1,2,0:T(8,128)S(1)} custom-call(f32[2,128,128]{2,1,0:T(8,128)S(1)} %get-tuple-element.22), custom_call_target="InvertDiagBlocksLowerTriangular" | custom-call | tf_op jit(solution)/shard_map/jit(_solve_triangular)/triangular_solve | solution.py:31
  185.2 0.7 fusion.5
  185.9 0.7 convolution_subtract_fusion.2
  186.6 0.7 fusion.24
  187.3 1.7 broadcast_select_fusion.2
  189.1 94.9 %all-reduce.17.cloned.1.call-done = (f32[1280,256]{0,1:T(8,128)}, f32[1280,256]{0,1:T(8,128)}, f32[256,256]{0,1:T(8,128)}) async-done(((f32[1280,256]{0,1:T(8,128)}, f32[1280,256]{0,1:T(8,128)}, f32[256,256]{0,1:T(8,128)}), (f32[1280,256]{0,1:T(8,128)}, f32[1280,256]{0,1:T(8,128)}, f32[256,256]{0,1:T(8,128)})) %all-reduce.17.cloned.1.call-update) | async-done | bytes 2883600 | tf_op jit(solution)/shard_map/psum | solution.py:9
  284.1 1.2 fusion.15
  285.3 1.3 convolution_subtract_fusion.5
  287.5 11.7 %cholesky.164 = f32[128,128]{1,0:T(8,128)S(1)} custom-call(f32[128,128]{1,0:T(8,128)S(1)} %cholesky.197), custom_call_target="Cholesky" | custom-call | tf_op jit(solution)/shard_map/jit(cholesky)/cholesky | solution.py:15
  299.3 0.6 compare_reduce_fusion.1
  299.9 9.8 %custom-call.25 = f32[1,128,128]{1,2,0:T(8,128)S(1)} custom-call(f32[1,128,128]{2,1,0:T(8,128)S(1)} %get-tuple-element.71), custom_call_target="InvertDiagBlocksLowerTriangular" | custom-call | tf_op jit(solution)/shard_map/jit(cholesky)/cholesky | solution.py:15
  310.3 11.7 %cholesky.181 = f32[128,128]{1,0:T(8,128)S(1)} custom-call(f32[128,128]{1,0:T(8,128)S(1)} %convolution_subtract_fusion.6), custom_call_target="Cholesky" | custom-call | tf_op jit(solution)/shard_map/jit(cholesky)/cholesky | solution.py:15
  322.0 0.6 compare_reduce_fusion
  323.9 14.6 %while.7 = (s32[]{:T(128)}, f32[256,256]{1,0:T(8,128)S(1)}, s32[2,2]{1,0:T(2,128)S(1)}, f32[2,128,128]{2,1,0:T(8,128)S(1)}, s32[]{:T(128)}) while((s32[]{:T(128)}, f32[256,256]{1,0:T(8,128)S(1)}, s32[2,2]{1,0:T(2,128)S(1)}, f32[2,128,128]{2,1,0:T(8,128)S(1)}, s32[]{:T(128)}) %tuple.72), condition=%wide.while_cond.2, body=%wide.while_body.2.sunk | while | flops 2 | bytes 131189 | solution.py:16
  335.3 1.3 bitcast_dynamic-update-slice_fusion.5
  337.2 1.3 bitcast_dynamic-update-slice_fusion.5
  338.6 19.7 %custom-call.20 = f32[2,128,128]{1,2,0:T(8,128)S(1)} custom-call(f32[2,128,128]{2,1,0:T(8,128)S(1)} %get-tuple-element.30), custom_call_target="InvertDiagBlocksLowerTriangular" | custom-call | tf_op jit(solution)/shard_map/jit(_cho_solve)/triangular_solve | solution.py:16
  358.8 1.0 fusion.26
  359.8 1.6 constant_dynamic-update-slice_fusion.1
  361.7 15.2 %convolution_bitcast_fusion = f32[1280,256]{0,1:T(8,128)} fusion(f32[2560,256]{0,1:T(8,128)S(1)} %constant_dynamic-update-slice_fusion, f32[1280,2560]{1,0:T(8,128)} %param.5), kind=kOutput, calls=%fused_computation.8 | convolution fusion | flops 10066329600 | bytes 17039360 | tf_op jit(solution)/shard_map/dot_general | solution.py:42
  376.9 1.2 fusion.27
  378.2 1.1 convolution_subtract_fusion.3
  379.3 1.1 fusion.25
  380.4 57.3 %all-reduce.11.cloned.1.call-done = f32[1280,256]{0,1:T(8,128)} async-done(((f32[1280,256]{0,1:T(8,128)}), f32[1280,256]{0,1:T(8,128)}) %all-reduce.11.cloned.1.call-update) | async-done | bytes 1310736 | tf_op jit(solution)/shard_map/psum | solution.py:43
  437.7 3.6 fusion.12
  441.3 1.0 copy-done.3
  442.4 2.1 fusion.38
  444.5 2.8 copy.14
  447.3 81.8 %all-reduce.13.cloned.1.call-done = f32[256,256]{1,0:T(8,128)} async-done(((f32[256,256]{1,0:T(8,128)}), f32[256,256]{1,0:T(8,128)}) %all-reduce.13.cloned.1.call-update) | async-done | bytes 262160 | tf_op jit(solution)/shard_map/psum | solution.py:45
  529.2 1.3 fusion.11
  530.5 5.0 broadcast_select_fusion.1
  535.5 93.4 %all-reduce.15.cloned.1.call-done = (f32[1280,256]{0,1:T(8,128)}, f32[1280,256]{0,1:T(8,128)}) async-done(((f32[1280,256]{0,1:T(8,128)}, f32[1280,256]{0,1:T(8,128)}), (f32[1280,256]{0,1:T(8,128)}, f32[1280,256]{0,1:T(8,128)})) %all-reduce.15.cloned.1.call-update) | async-done | bytes 2621456 | tf_op jit(solution)/shard_map/psum | solution.py:9
  628.9 15.9 %convolution_subtract_fusion.1 = f32[1280,2560]{1,0:T(8,128)S(1)} fusion(f32[1280,2560]{1,0:T(8,128)} %param.5, f32[1280,256]{0,1:T(8,128)} %get-tuple-element.55, f32[1280,256]{0,1:T(8,128)} %get-tuple-element.56, f32[128,1280]{1,0:T(8,128)} %copy-done, f32[128,1280]{1,0:T(8,128)S(1)} %fusion.5, s32[1280]{0:T(1024)S(1)} %iota_add_fusion), kind=kOutput, calls=%fused_computation.5 | convolution fusion | flops 10071572480 | bytes 30151680 | tf_op jit(solution)/shard_map/dot_general | solution.py:52
  644.8 14.6 %convolution_subtract_fusion = f32[1280,2560]{1,0:T(8,128)} fusion(f32[1280,2560]{1,0:T(8,128)S(1)} %convolution_subtract_fusion.1, f32[1280,256]{0,1:T(8,128)S(1)} %copy-done.4, f32[2560,256]{0,1:T(8,128)S(1)} %constant_dynamic-update-slice_fusion), kind=kOutput, calls=%fused_computation.4 | convolution fusion | flops 10069606400 | bytes 30146560 | tf_op jit(solution)/shard_map/dot_general | solution.py:53
  (64 shorter events, 5.9 us)
Async XLA Ops:
  6.5 30.3 %all-gather.2.cloned.1.call-start = ((), (), s32[]{:S(2)}) async-start(), calls=%async_computation | async-start | bytes 1474560 | tf_op jit(solution)/shard_map/all_gather | solution.py:24
  7.3 116.0 %all-reduce.9.cloned.1.call-start = ((), (), s32[]{:S(2)}) async-start(), calls=%async_computation.1 | async-start | bytes 524288 | tf_op jit(solution)/shard_map/psum | solution.py:29
  36.8 3.9 slice-start
  40.6 243.5 %all-reduce.17.cloned.1.call-start = ((), (), s32[]{:S(2)}) async-start(), calls=%async_computation.5 | async-start | bytes 5767168 | tf_op jit(solution)/shard_map/psum | solution.py:9
  137.1 48.1 %copy-start.2 = (f32[1280,256]{0,1:T(8,128)S(1)}, f32[1280,256]{0,1:T(8,128)}, u32[]{:S(2)}) copy-start(f32[1280,256]{0,1:T(8,128)} %all-gather.2.cloned.1.call-done) | copy-start | bytes 3932164
  187.3 1.7 copy-start
  189.1 248.6 %all-reduce.11.cloned.1.call-start = ((), (), s32[]{:S(2)}) async-start(), calls=%async_computation.2 | async-start | bytes 2621440 | tf_op jit(solution)/shard_map/psum | solution.py:43
  338.5 21.3 %copy-start.5 = (f32[256,256]{1,0:T(8,128)}, f32[256,256]{1,0:T(8,128)S(1)}, u32[]{:S(2)}) copy-start(f32[256,256]{1,0:T(8,128)S(1)} %get-tuple-element.195) | copy-start | bytes 786436
  358.2 1.6 copy-start.7
  359.8 1.7 copy-start.6
  376.9 152.3 %all-reduce.13.cloned.1.call-start = ((), (), s32[]{:S(2)}) async-start(), calls=%async_computation.3 | async-start | bytes 524288 | tf_op jit(solution)/shard_map/psum | solution.py:45
  437.7 4.7 copy-start.1
  441.3 1.1 copy-start.3
  444.5 184.4 %all-reduce.15.cloned.1.call-start = ((), (), s32[]{:S(2)}) async-start(), calls=%async_computation.4 | async-start | bytes 5242880 | tf_op jit(solution)/shard_map/psum | solution.py:9
  628.9 15.9 %copy-start.4 = (f32[1280,256]{0,1:T(8,128)S(1)}, f32[1280,256]{0,1:T(8,128)}, u32[]{:S(2)}) copy-start(f32[1280,256]{0,1:T(8,128)} %get-tuple-element.80) | copy-start | bytes 3932164
Sparse Core Ops, SparseCore 0:
  9.0 27.6 all-gather.1
  40.7 82.5 all-reduce.8
  189.2 94.8 all-reduce.16
  377.0 60.6 all-reduce.10
  444.6 84.4 all-reduce.12
  535.6 93.2 all-reduce.14
where the time goes:
time: 676 us; the launch traced here: 667 us
  waiting for transfers between devices  439 us (65%)
  other arithmetic  111 us (16%)
  matrix products  72.7 us (11%)
  between operations  16.7 us (2%)
  local copies, waits for them, and re-layouts  14.8 us (2%)
  loops' own time  11.2 us (2%)
    psum x2, waiting for transfers between devices, from_root(): return lax.psum(block, axis)  188 us
    psum x1, waiting for transfers between devices, shards(): lax.psum(jnp.dot(reflect_rows.T, products_rows, precision=highest), 'row')  81.8 us
    psum x1, waiting for transfers between devices, shards(): panel_gram, top_rows = lax.psum((local_gram, top_piece), 'row')  81.8 us
    psum x1, waiting for transfers between devices, shards(): summed_rows = lax.psum(partial_rows, 'col')  57.3 us
    another operation x7, other arithmetic, invert_small(): lower_factor = jnp.linalg.cholesky(normal_gram)  34.6 us
    another operation x6, other arithmetic, shards(): factor = jnp.linalg.cholesky(panel_gram)  34 us
    all_gather x1, waiting for transfers between devices, shards(): gathered = lax.all_gather(panel_block, 'col', axis=1, tiled=True)  29.5 us
    another operation x3, other arithmetic, shards(): jax.scipy.linalg.solve_triangular(factor, gathered.T, lower=True)  19.7 us
  transfers between devices with their start and end apart: 6, of which 6 were waited for; matrix products, arithmetic and copies ran while one was open for 1% of the time, Pallas kernels for 0%

commit v1 on v0

v1 whole, which is shorter than its diff:
```python
import jax
import jax.numpy as jnp
from jax import lax
from jax.experimental import pallas as pl
from jax.experimental.pallas import tpu as pltpu
from jax.sharding import PartitionSpec as P

W = 256
H = 128
BOTH = ("row", "col")
HIGHEST = lax.Precision.HIGHEST
HIGH = lax.Precision.HIGH


def lane(x, l):
    if x.shape[0] == 1:
        return lane(jnp.broadcast_to(x, (8, H)), l)[0:1]
    return jnp.take_along_axis(x, jnp.full(x.shape, l, jnp.int32), axis=1, mode="promise_in_bounds")


def factor_kernel(gram_ref, top_ref, lt_ref, tt_ref, gw, vr, lt):
    ri = lax.broadcasted_iota(jnp.int32, (W, W), 0)
    ci = lax.broadcasted_iota(jnp.int32, (W, W), 1)
    g = gram_ref[...]
    scale = 1.0 / jnp.max(jnp.where(ri == ci, g, 0.0), keepdims=True)
    root = jnp.sqrt(scale)
    t = top_ref[...] * root
    g = g * scale
    for h in range(2):
        gw[h] = g[:, h * H : (h + 1) * H]
        vr[h] = t[:, h * H : (h + 1) * H]
    li = lax.broadcasted_iota(jnp.int32, (1, H), 1)

    def chol_step(j, h, row0):
        l = j - h * H
        rows = [gw[k, pl.ds(j, 1), :] for k in range(2)]
        d = lane(rows[h], l)
        rs = lax.rsqrt(d)
        rs = rs * (1.5 - 0.5 * d * rs * rs)
        inv = rs * rs
        mod = [r * inv for r in rows]
        mod[h] = jnp.where(li == l, 1.0 + inv, mod[h])
        col = lane(gw[h, row0:, :], l)
        for k in range(2):
            gw[k, row0:, :] = gw[k, row0:, :] - col * mod[k]
        scaled = [r * rs for r in rows]
        for k in range(2):
            lt[k, pl.ds(j, 1), :] = jnp.where(li + k * H >= j, scaled[k], 0.0)
        return (rs, scaled[0], scaled[1])

    def jordan_step(j, h, carry):
        rs, s0, s1 = carry
        l = j - h * H
        rows = [vr[0, pl.ds(j, 1), :] + s0, vr[1, pl.ds(j, 1), :] + s1]
        q = 1.0 / lane(rows[h], l)
        here = li == l
        norm = [r * q for r in rows]
        mod = list(norm)
        mod[h] = jnp.where(here, 1.0 + rs * q, norm[h])
        norm[h] = jnp.where(here, rs * q, norm[h])
        col = lane(vr[h], l)
        for k in range(2):
            vr[k] = vr[k] - col * mod[k]
        for k in range(2):
            vr[k, pl.ds(j, 1), :] = norm[k]

    seg = 64
    carry = chol_step(0, 0, 0)
    for s in range(W // seg):
        h = s * seg // H
        start = s * seg

        def body(j, carry, h=h, start=start):
            new = chol_step(j, h, start)
            jordan_step(j - 1, h, carry)
            return new

        first = start
        if start % H == 0:
            if s > 0:
                new = chol_step(start, h, start)
                jordan_step(start - 1, h - 1, carry)
                carry = new
            first += 1
        carry = lax.fori_loop(first, start + seg, body, carry)
    jordan_step(W - 1, 1, carry)
    unroot = 1.0 / root
    for k in range(2):
        lt_ref[:, k * H : (k + 1) * H] = lt[k] * unroot
        tt_ref[:, k * H : (k + 1) * H] = vr[k] * scale


def factor(gram, top):
    vmem = pl.BlockSpec(memory_space=pltpu.VMEM)
    return pl.pallas_call(
        factor_kernel,
        out_shape=[jax.ShapeDtypeStruct((W, W), jnp.float32)] * 2,
        in_specs=[vmem] * 2,
        out_specs=[vmem] * 2,
        scratch_shapes=[pltpu.VMEM((2, W, H), jnp.float32)] * 3,
        cost_estimate=pl.CostEstimate(flops=2 * W**3, bytes_accessed=16 * W * W, transcendentals=0),
    )(gram, top)


def to_tiles(x):
    rows, cols = x.shape
    return x.reshape(rows // 8, 8, cols // H, H).transpose(0, 2, 1, 3).reshape(rows * cols // (8 * H), 8, H)


def from_tiles(x, rows, cols):
    return x.reshape(rows // 8, cols // H, 8, H).transpose(0, 2, 1, 3).reshape(rows, cols)


def sum_all(x, axes, parts):
    pieces = x.reshape((parts, -1) + x.shape[1:])
    mine = jnp.sum(lax.all_to_all(pieces, axes, 0, 0, tiled=True), axis=0)
    full = lax.all_to_all(jnp.broadcast_to(mine[None], (parts,) + mine.shape), axes, 0, 0, tiled=True)
    return full.reshape(x.shape)


def shards(trailing, panel_block):
    r = lax.axis_index("row")
    c = lax.axis_index("col")
    nr = lax.axis_size("row")
    nc = lax.axis_size("col")
    ratio = nr // nc
    perm = [(i * nc + j, ((i % ratio) * nc + j) * nc + i // ratio) for i in range(nr) for j in range(nc)]
    rows = panel_block.shape[0]
    part = rows // nc
    panel_t = panel_block.T
    slab = lax.all_to_all(panel_block, "col", 0, 1, tiled=True)
    local_gram = jnp.dot(slab.T, slab, precision=HIGHEST)
    full = jnp.zeros((rows, W), jnp.float32)
    placed = lax.dynamic_update_slice(full, slab, (c * part, 0))[:W]
    placed = jnp.where(r == 0, placed, jnp.zeros_like(placed))
    both = to_tiles(jnp.concatenate([local_gram, placed], axis=1))
    both = from_tiles(sum_all(both, BOTH, nr * nc), W, 2 * W)
    panel_rows = lax.all_gather(panel_t, "col", axis=0, tiled=True)
    moved = lax.ppermute(panel_t, BOTH, perm)
    panel_cols = lax.all_gather(moved, "row", axis=0, tiled=True).reshape(ratio, W, rows)
    factor_t, coupling_t = factor(both[:, :W], both[:, W:])
    lower = factor_t.T
    add_rows = jnp.where(r == 0, lower, jnp.zeros_like(lower))
    add_cols = jnp.where(c == 0, lower, jnp.zeros_like(lower))
    reflect_rows = panel_rows + jnp.pad(add_rows, ((0, 0), (0, rows - W)))
    reflect_cols = jnp.concatenate([panel_cols[i] for i in range(ratio)], axis=1)
    reflect_cols = reflect_cols + jnp.pad(add_cols, ((0, 0), (0, ratio * rows - W)))
    partial = lax.dot_general(trailing, reflect_cols, (((1,), (1,)), ((), ())), precision=HIGH)
    inner = jnp.dot(reflect_rows, partial, precision=HIGH)
    pieces = lax.all_to_all(partial.reshape(nc, part, W), "col", 0, 0, tiled=True)
    mine = jnp.sum(pieces, axis=0)
    mine = lax.dot_general(mine, coupling_t, (((1,), (1,)), ((), ())), precision=HIGHEST)
    moved = lax.ppermute(mine, BOTH, perm)
    weight_cols = lax.all_gather(moved, "row", axis=0, tiled=True)
    weight_rows = lax.all_gather(mine, "col", axis=0, tiled=True)
    inner = sum_all(inner, BOTH, nr * nc)
    inner = jnp.dot(coupling_t, inner, precision=HIGHEST)
    inner = lax.dot_general(inner, coupling_t, (((1,), (1,)), ((), ())), precision=HIGHEST) * 0.5
    weight_cols = weight_cols - lax.dot_general(reflect_cols, inner, (((0,), (0,)), ((), ())), precision=HIGH)
    weight_rows = weight_rows - lax.dot_general(reflect_rows, inner, (((0,), (0,)), ((), ())), precision=HIGH)
    first = lax.dot_general(reflect_rows, weight_cols, (((0,), (1,)), ((), ())), precision=HIGH)
    second = jnp.dot(weight_rows, reflect_cols, precision=HIGH)
    return trailing - first - second


def solution(mesh):
    return jax.shard_map(shards, mesh=mesh, in_specs=(P("row", "col"), P("row", "col")), out_specs=P("row", "col"), check_vma=False)
```

time: 676 us -> 273 us (0.40); the launches traced: 667 us -> 272 us
  waiting for transfers between devices: 439 us -> 33 us
  other arithmetic: 111 us -> 4.41 us
  blocking collectives: 0 us -> 83.6 us
  Pallas kernels: 0 us -> 36 us
  starting transfers between devices: 0.21 us -> 27.9 us
  matrix products: 72.7 us -> 55 us
  loops' own time: 11.2 us -> 0 us
    psum x5 -> x0, waiting for transfers between devices: 409 us -> none  [the longest x2 188 us: from_root(): return lax.psum(block, axis)]
    another operation x18 -> x0, other arithmetic: 108 us -> none  [the longest x7 34.6 us: invert_small(): lower_factor = jnp.linalg.cholesky(normal_gram)]
    all_to_all x0 -> x4, blocking collectives: none -> 83.6 us  [the longest x2 45.2 us: sum_all(): mine = jnp.sum(lax.all_to_all(pieces, axes, 0, 0, tiled=True), axis=0)]
    pallas_call x0 -> x1, Pallas kernels: none -> 36 us  [factor(): pl.pallas_call(factor_kernel, out_shape=[jax.ShapeDtypeStruct((W, W), jnp...]
    all_gather x1 -> x4, waiting for transfers between devices: 29.5 us -> 0.05 us  [the longest x1 0.02 us: shards(): lax.all_gather(moved, 'row', axis=0, tiled=True).reshape(ratio, W, rows)]
    all_to_all x0 -> x2, waiting for transfers between devices: none -> 20.6 us  [the longest x1 14.1 us: sum_all(): lax.all_to_all(jnp.broadcast_to(mine[None], (parts,) + mine.shape), axes,...]
    all_to_all x0 -> x2, starting transfers between devices: none -> 19.1 us  [the longest x1 14.3 us: shards(): slab = lax.all_to_all(panel_block, 'col', 0, 1, tiled=True)]
    ppermute x0 -> x2, waiting for transfers between devices: none -> 11.7 us  [the longest x1 6.06 us: shards(): moved = lax.ppermute(mine, BOTH, perm)]
  transfers between devices with their start and end apart: 6 -> 8, of which waited for: 6 -> 4; matrix products, arithmetic and copies ran while one was open for 1% -> 22% of each run, Pallas kernels for 0% -> 13%
where the time goes in v1:
time: 273 us; the launch traced here: 272 us
  blocking collectives  83.6 us (31%)
  matrix products  55 us (20%)
  Pallas kernels  36 us (13%)
  waiting for transfers between devices  33 us (12%)
  starting transfers between devices  27.9 us (10%)
  local copies, waits for them, and re-layouts  18.7 us (7%)
  between operations  13.3 us (5%)
  other arithmetic  4.41 us (2%)
    all_to_all x2, blocking collectives, sum_all(): mine = jnp.sum(lax.all_to_all(pieces, axes, 0, 0, tiled=True), axis=0)  45.2 us
    pallas_call x1, Pallas kernels, factor(): pl.pallas_call(factor_kernel, out_shape=[jax.ShapeDtypeStruct((W, W), jnp...  36 us
    all_to_all x1, blocking collectives, shards(): lax.all_to_all(partial.reshape(nc, part, W), 'col', 0, 0, tiled=True)  23 us
    dot_general x1, matrix products, shards(): lax.dot_general(reflect_rows, weight_cols, (((0,), (1,)), ((), ())), prec...  17.6 us
    all_to_all x1, blocking collectives, sum_all(): lax.all_to_all(jnp.broadcast_to(mine[None], (parts,) + mine.shape), axes,...  15.4 us
    dot_general x1, matrix products, shards(): lax.dot_general(trailing, reflect_cols, (((1,), (1,)), ((), ())), precisi...  14.9 us
    all_to_all x1, starting transfers between devices, shards(): slab = lax.all_to_all(panel_block, 'col', 0, 1, tiled=True)  14.3 us
    all_to_all x1, waiting for transfers between devices, sum_all(): lax.all_to_all(jnp.broadcast_to(mine[None], (parts,) + mine.shape), axes,...  14.1 us
  transfers between devices with their start and end apart: 8, of which 4 were waited for; matrix products, arithmetic and copies ran while one was open for 22% of the time, Pallas kernels for 13%

profile of v1, /device:TPU:1, one launch (start us, length us, event | category | flops | bytes accessed | tf_op | source)
XLA Modules:
  0.0 271.9 jit_solution(5698929348416065706)
XLA Ops:
  6.5 4.9 %collective-permute-start = (f32[32,1280]{1,0:T(8,128)}, f32[32,1280]{1,0:T(8,128)S(1)}, u32[]{:S(2)}, u32[]{:S(2)}) collective-permute-start(f32[32,1280]{1,0:T(8,128)} %bitcast.41), channel_id=1, source_target_pairs={{0,0},{1,8},{2,16},{3,24},{4,32},{5,40},{6,48},{7,56},{8,64},{9,72... | collective-permute-start | bytes 491528 | tf_op jit(solution)/shard_map/ppermute | solution.py:139
  11.5 5.6 %collective-permute-done = f32[32,1280]{1,0:T(8,128)S(1)} collective-permute-done((f32[32,1280]{1,0:T(8,128)}, f32[32,1280]{1,0:T(8,128)S(1)}, u32[]{:S(2)}, u32[]{:S(2)}) %collective-permute-start) | collective-permute-done | bytes 163872 | tf_op jit(solution)/shard_map/ppermute | solution.py:139
  17.1 0.7 copy-done.1
  17.8 1.1 all_to_all.29
  18.9 0.8 copy.11
  19.6 14.3 %all-to-all-start = ((f32[8,160,32]{1,2,0:T(8,128)}), f32[8,160,32]{1,2,0:T(8,128)S(1)}, u32[]{:S(2)}, u32[]{:S(2)}) async-start(f32[8,160,32]{1,2,0:T(8,128)} %copy.11), calls=%async_computation | async-start | bytes 524288 | tf_op jit(solution)/shard_map/all_to_all | solution.py:131
  34.0 6.5 %all-to-all-done = f32[8,160,32]{1,2,0:T(8,128)S(1)} async-done(((f32[8,160,32]{1,2,0:T(8,128)}), f32[8,160,32]{1,2,0:T(8,128)S(1)}, u32[]{:S(2)}, u32[]{:S(2)}) %all-to-all-start) | async-done | bytes 163872 | tf_op jit(solution)/shard_map/all_to_all | solution.py:131
  40.5 0.1 copy.12
  40.6 0.1 broadcast_in_dim.6
  40.7 0.4 fusion.17
  41.2 0.1 pad_maximum_fusion
  41.2 19.8 %all_to_all.44 = f32[128,1,8,128]{3,2,1,0:T(8,128)S(1)} all-to-all(f32[128,1,8,128]{3,2,1,0:T(8,128)S(1)} %bitcast.40), channel_id=1, replica_groups=mesh['row'=16,'col'=8] {'row','col'}, dimensions={0} | all-to-all | bytes 1048576 | tf_op jit(solution)/shard_map/all_to_all | solution.py:116
  61.0 0.1 reduce_sum.27
  61.2 0.8 broadcast_in_dim.7
  62.0 4.8 %all-to-all-start.2 = ((f32[128,1,8,128]{3,2,1,0:T(8,128)}), f32[128,1,8,128]{3,2,1,0:T(8,128)S(1)}, u32[]{:S(2)}, u32[]{:S(2)}) async-start(f32[128,1,8,128]{3,2,1,0:T(8,128)} %broadcast_in_dim.7), calls=%async_computation.2 | async-start | bytes 1048576 | tf_op jit(solution)/shard_map/all_to_all | solution.py:117
  66.8 0.0 all-gather.5.cloned.1.call-start
  66.8 0.7 all-gather.5.cloned.1.call-update
  67.5 0.0 all-gather.11.cloned.1.call-start
  67.6 14.1 %all-to-all-done.2 = f32[128,1,8,128]{3,2,1,0:T(8,128)S(1)} async-done(((f32[128,1,8,128]{3,2,1,0:T(8,128)}), f32[128,1,8,128]{3,2,1,0:T(8,128)S(1)}, u32[]{:S(2)}, u32[]{:S(2)}) %all-to-all-start.2) | async-done | bytes 524320 | tf_op jit(solution)/shard_map/all_to_all | solution.py:117
  81.6 0.8 fusion.16
  82.5 36.0 %shard_map.28 = (f32[256,256]{1,0:T(8,128)}, f32[256,256]{1,0:T(8,128)}) custom-call(f32[256,256]{1,0:T(8,128)} %get-tuple-element.12.gram_ref, f32[256,256]{1,0:T(8,128)} %get-tuple-element.11.top_ref), custom_call_target="tpu_custom_call" | custom-call | flops 33554432 | bytes 1048576 | tf_op jit(solution)/shard_map/pallas_call | solution.py:95
  118.5 1.0 select_bitcast_fusion.1
  119.5 0.0 all-gather.7.cloned.1.call-done
  119.5 2.9 %fusion.15 = (f32[256,1280]{1,0:T(8,128)S(1)}, f32[256,1280]{1,0:T(8,128)}) fusion(f32[512,1280]{1,0:T(8,128)} %all-gather.7.cloned.1.call-done), kind=kLoop, calls=%fused_computation.25 | loop fusion | bytes 5242880 | tf_op jit(solution)/shard_map/slice | solution.py:146
  122.4 0.4 copy.19
  122.8 1.7 copy.20
  124.6 14.9 %fusion.4 = f32[256,1280]{1,0:T(8,128)} fusion(f32[1280,2560]{1,0:T(8,128)} %param.2, f32[256,1280]{0,1:T(8,128)S(1)} %copy.20, f32[256,1280]{0,1:T(8,128)S(1)} %copy.19, f32[256,256]{0,1:T(8,128)S(1)} %get-tuple-element.14), kind=kOutput, calls=%fused_computation.9 | convolution fusion | flops 5034475520 | bytes 17301504 | tf_op jit(solution)/shard_map/dot_general | solution.py:148
  139.5 2.8 %copy.17 = f32[1280,256]{1,0:T(8,128)} copy(f32[1280,256]{0,1:T(8,128)} %bitcast.35) | data formatting | bytes 2621440 | tf_op jit(solution)/shard_map/dot_general | solution.py:148
  142.3 23.0 %all_to_all.45 = f32[8,160,256]{2,1,0:T(8,128)} all-to-all(f32[8,160,256]{2,1,0:T(8,128)} %bitcast.36), channel_id=1, replica_groups=mesh['row'=16,'col'=8] {'col'}, dimensions={0} | all-to-all | bytes 2621440 | tf_op jit(solution)/shard_map/all_to_all | solution.py:150
  165.2 2.1 reduce_sum.28
  167.3 2.0 fusion.18
  169.4 0.0 all-gather.9.cloned.1.call-start
  169.4 3.7 %collective-permute-start.1 = (f32[160,256]{1,0:T(8,128)}, f32[160,256]{1,0:T(8,128)}, u32[]{:S(2)}, u32[]{:S(2)}) collective-permute-start(f32[160,256]{1,0:T(8,128)} %fusion.18), channel_id=1, source_target_pairs={{0,0},{1,8},{2,16},{3,24},{4,32},{5,40},{6,48},{7,56},{8,64},{9,72... | collective-permute-start | bytes 491528 | tf_op jit(solution)/shard_map/ppermute | solution.py:153
  173.1 6.1 %collective-permute-done.1 = f32[160,256]{1,0:T(8,128)} collective-permute-done((f32[160,256]{1,0:T(8,128)}, f32[160,256]{1,0:T(8,128)}, u32[]{:S(2)}, u32[]{:S(2)}) %collective-permute-start.1) | collective-permute-done | bytes 163872 | tf_op jit(solution)/shard_map/ppermute | solution.py:153
  179.3 2.8 %copy.14 = f32[256,1280]{0,1:T(8,128)} copy(f32[256,1280]{1,0:T(8,128)} %all-gather.5.cloned.1.call-done) | data formatting | bytes 2621440 | tf_op jit(solution)/shard_map/all_gather | solution.py:138
  182.0 3.6 %fusion.5 = f32[256,256]{1,0:T(8,128)} fusion(f32[256,1280]{1,0:T(8,128)} %fusion.4, f32[256,1280]{0,1:T(8,128)} %copy.14, f32[256,256]{0,1:T(8,128)S(1)} %get-tuple-element.13), kind=kOutput, calls=%fused_computation.10 | convolution fusion | flops 503644160 | bytes 3145728 | tf_op jit(solution)/shard_map/dot_general | solution.py:149
  185.7 1.8 reshape.32
  187.5 25.4 %all_to_all.46 = f32[128,2,256]{2,1,0:T(2,128)} all-to-all(f32[128,2,256]{2,1,0:T(2,128)} %reshape.32), channel_id=1, replica_groups=mesh['row'=16,'col'=8] {'row','col'}, dimensions={0} | all-to-all | bytes 524288 | tf_op jit(solution)/shard_map/all_to_all | solution.py:116
  212.9 1.1 reduce_sum.29
  214.0 0.1 broadcast_in_dim.8
  214.0 15.4 %all_to_all.47 = f32[128,2,256]{2,1,0:T(2,128)} all-to-all(f32[128,2,256]{2,1,0:T(2,128)S(1)} %broadcast_in_dim.8), channel_id=1, replica_groups=mesh['row'=16,'col'=8] {'row','col'}, dimensions={0} | all-to-all | bytes 524288 | tf_op jit(solution)/shard_map/all_to_all | solution.py:117
  229.5 1.8 reshape.33
  231.3 1.3 fusion.19
  232.7 1.4 convolution_multiply_fusion
  234.0 2.7 %fusion.3 = f32[2560,256]{1,0:T(8,128)} fusion(f32[256,256]{1,0:T(8,128)S(1)} %convolution_multiply_fusion, f32[256,1280]{0,1:T(8,128)S(1)} %copy.20, f32[256,1280]{0,1:T(8,128)S(1)} %copy.19, f32[256,256]{0,1:T(8,128)S(1)} %get-tuple-element.14), kind=kOutput, calls=%fused_computation.8 | convolution fusion | flops 1007943680 | bytes 5767168 | tf_op jit(solution)/shard_map/dot_general | solution.py:159
  236.8 2.4 convolution_subtract_fusion.1
  239.2 8.6 %fusion.2 = f32[1280,2560]{1,0:T(8,128)} fusion(f32[1280,256]{1,0:T(8,128)S(1)} %convolution_subtract_fusion.1, f32[256,1280]{0,1:T(8,128)S(1)} %copy.20, f32[256,1280]{0,1:T(8,128)S(1)} %copy.19, f32[256,256]{0,1:T(8,128)S(1)} %get-tuple-element.14), kind=kOutput, calls=%fused_computation.7 | convolution fusion | flops 5034475520 | bytes 17301504 | tf_op jit(solution)/shard_map/dot_general | solution.py:162
  247.8 17.6 %fusion = f32[1280,2560]{1,0:T(8,128)} fusion(f32[1280,2560]{1,0:T(8,128)} %fusion.2, f32[1280,2560]{1,0:T(8,128)} %param.2, f32[2560,256]{1,0:T(8,128)} %all-gather.9.cloned.1.call-done, f32[2560,256]{1,0:T(8,128)} %fusion.3, f32[256,1280]{0,1:T(8,128)} %copy.14, f32[256,256]{0,1:T(8,128)S(1)} %get-tuple-element.13), kind=kOutput, calls=%fused_computation.1 | convolution fusion | flops 5040701440 | bytes 46137344 | tf_op jit(solution)/shard_map/dot_general | solution.py:161
  (12 shorter events, 0.1 us)
Async XLA Ops:
  6.5 113.0 %all-gather.7.cloned.1.call-start = ((), (), s32[]{:S(2)}) async-start(), calls=%async_computation.7 | async-start | bytes 2785280 | tf_op jit(solution)/shard_map/all_gather | solution.py:140
  6.5 10.6 %collective-permute-start = (f32[32,1280]{1,0:T(8,128)}, f32[32,1280]{1,0:T(8,128)S(1)}, u32[]{:S(2)}, u32[]{:S(2)}) collective-permute-start(f32[32,1280]{1,0:T(8,128)} %bitcast.41), channel_id=1, source_target_pairs={{0,0},{1,8},{2,16},{3,24},{4,32},{5,40},{6,48},{7,56},{8,64},{9,72... | collective-permute-start | bytes 491528 | tf_op jit(solution)/shard_map/ppermute | solution.py:139
  17.1 0.7 copy-start.1
  19.6 20.8 %all-to-all-start = ((f32[8,160,32]{1,2,0:T(8,128)}), f32[8,160,32]{1,2,0:T(8,128)S(1)}, u32[]{:S(2)}, u32[]{:S(2)}) async-start(f32[8,160,32]{1,2,0:T(8,128)} %copy.11), calls=%async_computation | async-start | bytes 524288 | tf_op jit(solution)/shard_map/all_to_all | solution.py:131
  62.0 19.6 %all-to-all-start.2 = ((f32[128,1,8,128]{3,2,1,0:T(8,128)}), f32[128,1,8,128]{3,2,1,0:T(8,128)S(1)}, u32[]{:S(2)}, u32[]{:S(2)}) async-start(f32[128,1,8,128]{3,2,1,0:T(8,128)} %broadcast_in_dim.7), calls=%async_computation.2 | async-start | bytes 1048576 | tf_op jit(solution)/shard_map/all_to_all | solution.py:117
  66.8 112.5 %all-gather.5.cloned.1.call-start = ((), (), s32[]{:S(2)}) async-start(), calls=%async_computation.6 | async-start | bytes 1474560 | tf_op jit(solution)/shard_map/all_gather | solution.py:138
  67.5 169.2 %all-gather.11.cloned.1.call-start = ((), (), s32[]{:S(2)}) async-start(), calls=%async_computation.9 | async-start | bytes 1474560 | tf_op jit(solution)/shard_map/all_gather | solution.py:155
  165.2 2.1 copy-start
  169.4 78.5 %all-gather.9.cloned.1.call-start = ((), (), s32[]{:S(2)}) async-start(), calls=%async_computation.8 | async-start | bytes 2785280 | tf_op jit(solution)/shard_map/all_gather | solution.py:154
  169.4 9.8 %collective-permute-start.1 = (f32[160,256]{1,0:T(8,128)}, f32[160,256]{1,0:T(8,128)}, u32[]{:S(2)}, u32[]{:S(2)}) collective-permute-start(f32[160,256]{1,0:T(8,128)} %fusion.18), channel_id=1, source_target_pairs={{0,0},{1,8},{2,16},{3,24},{4,32},{5,40},{6,48},{7,56},{8,64},{9,72... | collective-permute-start | bytes 491528 | tf_op jit(solution)/shard_map/ppermute | solution.py:153
Sparse Core Ops, SparseCore 0:
  17.9 58.7 all-gather.6
  78.4 24.8 all-gather.4
  169.5 24.7 all-gather.10
  196.3 46.2 all-gather.8

commit v2 on v1

--- a/solution.py
+++ b/solution.py
@@ -118,6 +118,139 @@
     return full.reshape(x.shape)
 
 
+def split(x):
+    high = x.astype(jnp.bfloat16)
+    return high, (x - high.astype(jnp.float32)).astype(jnp.bfloat16)
+
+
+def dot3(a, b, contract):
+    dims = (contract, ((), ()))
+    a_high, a_low = split(a)
+    b_high, b_low = split(b)
+
+    def dot(x, y):
+        return lax.dot_general(x, y, dims, preferred_element_type=jnp.float32)
+
+    return dot(a_high, b_high) + (dot(a_high, b_low) + dot(a_low, b_high))
+
+
+NN = ((1,), (0,))
+NT = ((1,), (1,))
+VMEM_BYTES = 50 * 1024 * 1024
+
+
+def product_kernel(place_ref, a_ref, cols_ref, rows_ref, lt_ref, out_ref, inner_ref, acc):
+    step = pl.program_id(0)
+    steps = pl.num_programs(0)
+    lower = lt_ref[...].T
+
+    @pl.when(step == 0)
+    def _():
+        own = (place_ref[1] == 0).astype(jnp.float32)
+        first = cols_ref[0, :, :W] + own * lower
+        rest = cols_ref[0, :, W:]
+        acc[...] = dot3(a_ref[:, :W], first, NT) + dot3(a_ref[:, W:], rest, NT)
+
+    @pl.when(step > 0)
+    def _():
+        acc[...] += dot3(a_ref[...], cols_ref[0], NT)
+
+    @pl.when(step == steps - 1)
+    def _():
+        total = acc[...]
+        out_ref[...] = total
+        own = (place_ref[0] == 0).astype(jnp.float32)
+        inner = dot3(rows_ref[:, :W] + own * lower, total[:W], NN)
+        inner_ref[...] = inner + dot3(rows_ref[:, W:], total[W:], NN)
+
+
+def product(place, trailing, panel_cols, panel_rows, factor_t):
+    rows, cols = trailing.shape
+    half = panel_cols.shape[2]
+    tile = 640
+    per = half // tile
+    return pl.pallas_call(
+        product_kernel,
+        grid=(cols // tile,),
+        out_shape=[jax.ShapeDtypeStruct((rows, W), jnp.float32), jax.ShapeDtypeStruct((W, W), jnp.float32)],
+        in_specs=[
+            pl.BlockSpec(memory_space=pltpu.SMEM),
+            pl.BlockSpec((rows, tile), lambda i: (0, i)),
+            pl.BlockSpec((1, W, tile), lambda i: (i // per, 0, i % per)),
+            pl.BlockSpec((W, rows), lambda i: (0, 0)),
+            pl.BlockSpec((W, W), lambda i: (0, 0)),
+        ],
+        out_specs=[pl.BlockSpec((rows, W), lambda i: (0, 0)), pl.BlockSpec((W, W), lambda i: (0, 0))],
+        scratch_shapes=[pltpu.VMEM((rows, W), jnp.float32)],
+        compiler_params=pltpu.CompilerParams(vmem_limit_bytes=VMEM_BYTES),
+        cost_estimate=pl.CostEstimate(flops=6 * rows * cols * W, bytes_accessed=4 * rows * cols, transcendentals=0),
+    )(place, trailing, panel_cols, panel_rows, factor_t)
+
+
+def update_kernel(place_ref, a_ref, cols_ref, wcols_ref, rows_ref, wrows_ref, lt_ref, tt_ref, inner_ref, out_ref,
+                  half_ref, vh, vl, zh, zl):
+    step = pl.program_id(0)
+
+    def dot(x, y, contract):
+        return lax.dot_general(x, y, (contract, ((), ())), preferred_element_type=jnp.float32)
+
+    @pl.when(step == 0)
+    def _():
+        t = tt_ref[...]
+        mid = jnp.dot(t, inner_ref[...], precision=HIGHEST, preferred_element_type=jnp.float32)
+        half_ref[...] = 0.5 * lax.dot_general(mid, t, (NT, ((), ())), precision=HIGHEST, preferred_element_type=jnp.float32)
+        own = (place_ref[0] == 0).astype(jnp.float32)
+        lt = lt_ref[...] * own
+        reflect = rows_ref[...].T
+        vh[...], vl[...] = split(reflect)
+        vh[:W], vl[:W] = split(reflect[:W] + lt)
+        zh[...], zl[...] = split(wrows_ref[...] - dot3(reflect, half_ref[...], NN))
+        zh[:W], zl[:W] = split(wrows_ref[:W] - dot3(reflect[:W] + lt, half_ref[...], NN))
+
+    own = jnp.logical_and(place_ref[1] == 0, step == 0).astype(jnp.float32)
+    lower = lt_ref[...].T * own
+    cols = cols_ref[0]
+    if cols.shape[1] > W:
+        cols = jnp.concatenate([cols[:, :W] + lower, cols[:, W:]], axis=1)
+    else:
+        cols = cols + lower
+    ch, cl = split(cols)
+    fix = dot3(half_ref[...], cols, NN)
+    weights = wcols_ref[...].T - fix
+    wh, wl = split(weights)
+    first = dot(vh[...], wh, NN) + (dot(vh[...], wl, NN) + dot(vl[...], wh, NN))
+    second = dot(zh[...], ch, NN) + (dot(zh[...], cl, NN) + dot(zl[...], ch, NN))
+    out_ref[...] = a_ref[...] - first - second
+
+
+def update(place, trailing, panel_cols, weight_cols, panel_rows, weight_rows, factor_t, coupling_t, inner):
+    rows, cols = trailing.shape
+    half = panel_cols.shape[2]
+    tile = 256
+    per = half // tile
+    square = pl.BlockSpec((W, W), lambda i: (0, 0))
+    return pl.pallas_call(
+        update_kernel,
+        grid=(cols // tile,),
+        out_shape=jax.ShapeDtypeStruct((rows, cols), jnp.float32),
+        in_specs=[
+            pl.BlockSpec(memory_space=pltpu.SMEM),
+            pl.BlockSpec((rows, tile), lambda i: (0, i)),
+            pl.BlockSpec((1, W, tile), lambda i: (i // per, 0, i % per)),
+            pl.BlockSpec((tile, W), lambda i: (i, 0)),
+            pl.BlockSpec((W, rows), lambda i: (0, 0)),
+            pl.BlockSpec((rows, W), lambda i: (0, 0)),
+            square,
+            square,
+            square,
+        ],
+        out_specs=pl.BlockSpec((rows, tile), lambda i: (0, i)),
+        scratch_shapes=[pltpu.VMEM((W, W), jnp.float32)] + [pltpu.VMEM((rows, W), jnp.bfloat16)] * 4,
+        compiler_params=pltpu.CompilerParams(vmem_limit_bytes=VMEM_BYTES),
+        cost_estimate=pl.CostEstimate(flops=12 * rows * cols * W, bytes_accessed=8 * rows * cols, transcendentals=0),
+    )(place, trailing, panel_cols, weight_cols, panel_rows, weight_rows, factor_t, coupling_t, inner)
+
+
 def shards(trailing, panel_block):
     r = lax.axis_index("row")
     c = lax.axis_index("col")
@@ -125,42 +258,35 @@
     nc = lax.axis_size("col")
     ratio = nr // nc
     perm = [(i * nc + j, ((i % ratio) * nc + j) * nc + i // ratio) for i in range(nr) for j in range(nc)]
-    rows = panel_block.shape[0]
+    pair = [(j, j ^ 1) for j in range(nc)]
+    lines = [list(range(k, nc, 2)) for k in range(2)]
+    place = jnp.stack([r, c]).astype(jnp.int32)
+    rows, width = panel_block.shape
     part = rows // nc
     panel_t = panel_block.T
-    slab = lax.all_to_all(panel_block, "col", 0, 1, tiled=True)
-    local_gram = jnp.dot(slab.T, slab, precision=HIGHEST)
-    full = jnp.zeros((rows, W), jnp.float32)
-    placed = lax.dynamic_update_slice(full, slab, (c * part, 0))[:W]
-    placed = jnp.where(r == 0, placed, jnp.zeros_like(placed))
-    both = to_tiles(jnp.concatenate([local_gram, placed], axis=1))
-    both = from_tiles(sum_all(both, BOTH, nr * nc), W, 2 * W)
-    panel_rows = lax.all_gather(panel_t, "col", axis=0, tiled=True)
     moved = lax.ppermute(panel_t, BOTH, perm)
+    line = lax.all_gather(panel_t, "col", axis=0, axis_index_groups=lines)
+    other = lax.ppermute(line, "col", pair)
+    even = c % 2 == 0
+    panel_rows = jnp.stack([jnp.where(even, line, other), jnp.where(even, other, line)], axis=1).reshape(W, rows)
     panel_cols = lax.all_gather(moved, "row", axis=0, tiled=True).reshape(ratio, W, rows)
-    factor_t, coupling_t = factor(both[:, :W], both[:, W:])
-    lower = factor_t.T
-    add_rows = jnp.where(r == 0, lower, jnp.zeros_like(lower))
-    add_cols = jnp.where(c == 0, lower, jnp.zeros_like(lower))
-    reflect_rows = panel_rows + jnp.pad(add_rows, ((0, 0), (0, rows - W)))
-    reflect_cols = jnp.concatenate([panel_cols[i] for i in range(ratio)], axis=1)
-    reflect_cols = reflect_cols + jnp.pad(add_cols, ((0, 0), (0, ratio * rows - W)))
-    partial = lax.dot_general(trailing, reflect_cols, (((1,), (1,)), ((), ())), precision=HIGH)
-    inner = jnp.dot(reflect_rows, partial, precision=HIGH)
+    strip = lax.dot_general(panel_t, panel_rows, (((1,), (1,)), ((), ())), precision=HIGHEST)
+    top = jnp.where(r == 0, panel_t[:, :W], jnp.zeros((width, W), jnp.float32))
+    pieces = to_tiles(jnp.concatenate([strip, top], axis=1))
+    mine = jnp.sum(lax.all_to_all(pieces, "row", 0, 0, tiled=True), axis=0)
+    full = lax.all_to_all(jnp.broadcast_to(mine[None], (nr * nc,) + mine.shape), BOTH, 0, 0, tiled=True)
+    tr, tc = width // 8, 2 * W // H
+    full = full.reshape(tr, tc, nc, 8, H).transpose(2, 0, 3, 1, 4).reshape(W, 2 * W)
+    factor_t, coupling_t = factor(full[:, :W], full[:, W:].T)
+    partial, inner = product(place, trailing, panel_cols, panel_rows, factor_t)
     pieces = lax.all_to_all(partial.reshape(nc, part, W), "col", 0, 0, tiled=True)
     mine = jnp.sum(pieces, axis=0)
     mine = lax.dot_general(mine, coupling_t, (((1,), (1,)), ((), ())), precision=HIGHEST)
     moved = lax.ppermute(mine, BOTH, perm)
     weight_cols = lax.all_gather(moved, "row", axis=0, tiled=True)
     weight_rows = lax.all_gather(mine, "col", axis=0, tiled=True)
-    inner = sum_all(inner, BOTH, nr * nc)
-    inner = jnp.dot(coupling_t, inner, precision=HIGHEST)
-    inner = lax.dot_general(inner, coupling_t, (((1,), (1,)), ((), ())), precision=HIGHEST) * 0.5
-    weight_cols = weight_cols - lax.dot_general(reflect_cols, inner, (((0,), (0,)), ((), ())), precision=HIGH)
-    weight_rows = weight_rows - lax.dot_general(reflect_rows, inner, (((0,), (0,)), ((), ())), precision=HIGH)
-    first = lax.dot_general(reflect_rows, weight_cols, (((0,), (1,)), ((), ())), precision=HIGH)
-    second = jnp.dot(weight_rows, reflect_cols, precision=HIGH)
-    return trailing - first - second
+    inner = from_tiles(sum_all(to_tiles(inner).reshape(nr * nc, 4, H), BOTH, nr * nc).reshape(-1, 8, H), W, W)
+    return update(place, trailing, panel_cols, weight_cols, panel_rows, weight_rows, factor_t, coupling_t, inner)
 
 
 def solution(mesh):

time: 273 us -> 261 us (0.956)
  matrix products: 55 us -> 3.22 us
  Pallas kernels: 36 us -> 69.1 us
  waiting for transfers between devices: 33 us -> 53.9 us
  starting transfers between devices: 27.9 us -> 13.9 us
  blocking collectives: 83.6 us -> 97.2 us
  local copies, waits for them, and re-layouts: 18.7 us -> 7.11 us
    dot_general x9 -> x1, matrix products: 53 us -> 1.22 us  [shards(): lax.dot_general(panel_t, panel_rows, (((1,), (1,)), ((), ())), precision=...]
    pallas_call x0 -> x2, Pallas kernels: none -> 33.1 us  [the longest x1 22.5 us: update(): pl.pallas_call(update_kernel, grid=(cols // tile,), out_shape=jax.ShapeDt...]
    all_gather x1, waiting for transfers between devices: 0.01 us -> 23.2 us  [shards(): weight_cols = lax.all_gather(moved, 'row', axis=0, tiled=True)]
    all_gather x0 -> x1, blocking collectives: none -> 21.5 us  [shards(): line = lax.all_gather(panel_t, 'col', axis=0, axis_index_groups=lines)]
    all_to_all x2 -> x1, blocking collectives: 45.2 us -> 24.7 us  [sum_all(): mine = jnp.sum(lax.all_to_all(pieces, axes, 0, 0, tiled=True), axis=0)]
    all_to_all x0 -> x1, blocking collectives: none -> 13.7 us  [shards(): mine = jnp.sum(lax.all_to_all(pieces, 'row', 0, 0, tiled=True), axis=0)]
    all_to_all x2 -> x1, starting transfers between devices: 19.1 us -> 5.79 us  [shards(): lax.all_to_all(jnp.broadcast_to(mine[None], (nr * nc,) + mine.shape), BOT...]
    all_to_all x2 -> x1, waiting for transfers between devices: 20.6 us -> 16.9 us  [shards(): lax.all_to_all(jnp.broadcast_to(mine[None], (nr * nc,) + mine.shape), BOT...]
  transfers between devices with their start and end apart: 8 -> 7, of which waited for: 4 -> 5; matrix products, arithmetic and copies ran while one was open for 22% -> 2% of each run, Pallas kernels for 13% -> 14%
where the time goes in v2:
time: 261 us; the launch traced here: 260 us
  blocking collectives  97.2 us (37%)
  Pallas kernels  69.1 us (26%)
  waiting for transfers between devices  53.9 us (21%)
  starting transfers between devices  13.9 us (5%)
  between operations  13.2 us (5%)
  local copies, waits for them, and re-layouts  7.11 us (3%)
  matrix products  3.22 us (1%)
    pallas_call x1, Pallas kernels, factor(): pl.pallas_call(factor_kernel, out_shape=[jax.ShapeDtypeStruct((W, W), jnp...  36.1 us
    all_to_all x1, blocking collectives, sum_all(): mine = jnp.sum(lax.all_to_all(pieces, axes, 0, 0, tiled=True), axis=0)  24.7 us
    all_gather x1, waiting for transfers between devices, shards(): weight_cols = lax.all_gather(moved, 'row', axis=0, tiled=True)  23.2 us
    pallas_call x1, Pallas kernels, update(): pl.pallas_call(update_kernel, grid=(cols // tile,), out_shape=jax.ShapeDt...  22.5 us
    all_gather x1, blocking collectives, shards(): line = lax.all_gather(panel_t, 'col', axis=0, axis_index_groups=lines)  21.5 us
    all_to_all x1, blocking collectives, shards(): lax.all_to_all(partial.reshape(nc, part, W), 'col', 0, 0, tiled=True)  21.2 us
    all_to_all x1, waiting for transfers between devices, shards(): lax.all_to_all(jnp.broadcast_to(mine[None], (nr * nc,) + mine.shape), BOT...  16.9 us
    all_to_all x1, blocking collectives, sum_all(): lax.all_to_all(jnp.broadcast_to(mine[None], (parts,) + mine.shape), axes,...  16.1 us
  transfers between devices with their start and end apart: 7, of which 5 were waited for; matrix products, arithmetic and copies ran while one was open for 2% of the time, Pallas kernels for 14%

profile of v2, /device:TPU:1, one launch (start us, length us, event | category | flops | bytes accessed | tf_op | source)
XLA Modules:
  0.0 259.8 jit_solution(1521200304599300973)
XLA Ops:
  6.5 0.0 all-gather.5.cloned.1.call-start
  6.5 4.9 %collective-permute-start = (f32[32,1280]{1,0:T(8,128)}, f32[32,1280]{1,0:T(8,128)S(1)}, u32[]{:S(2)}, u32[]{:S(2)}) collective-permute-start(f32[32,1280]{1,0:T(8,128)} %bitcast.50), channel_id=1, source_target_pairs={{0,0},{1,8},{2,16},{3,24},{4,32},{5,40},{6,48},{7,56},{8,64},{9,72... | collective-permute-start | bytes 491528 | tf_op jit(solution)/shard_map/ppermute | solution.py:267
  11.5 5.6 %collective-permute-done = f32[32,1280]{1,0:T(8,128)S(1)} collective-permute-done((f32[32,1280]{1,0:T(8,128)}, f32[32,1280]{1,0:T(8,128)S(1)}, u32[]{:S(2)}, u32[]{:S(2)}) %collective-permute-start) | collective-permute-done | bytes 163872 | tf_op jit(solution)/shard_map/ppermute | solution.py:267
  17.1 0.0 copy-start.5
  17.1 0.7 copy-done.5
  17.8 0.0 all-gather.5.cloned.1.call-update
  17.8 21.5 %all-gather = f32[128,1280]{1,0:T(8,128)S(1)} all-gather(f32[32,1280]{1,0:T(8,128)} %bitcast.51), channel_id=2, replica_groups={{0,2,4,6},{1,3,5,7},{8,10,12,14},{9,11,13,15},{16,18,20,22},{17,19,21,2..., dimensions={0}, use_global_device_ids=true | all-gather | bytes 819200 | tf_op jit(solution)/shard_map/all_gather | solution.py:268
  39.3 0.0 collective-permute-start.1
  39.3 0.8 slice_select_fusion
  40.1 1.3 collective-permute-done.1
  41.4 0.1 select_bitcast_fusion.1
  41.6 0.0 copy-start.4
  41.6 0.1 pad_maximum_fusion
  41.7 0.8 copy-done.4
  42.5 1.2 convolution_bitcast_fusion
  43.7 13.7 %all_to_all.25 = f32[16,8,128]{2,1,0:T(8,128)S(1)} all-to-all(f32[16,8,128]{2,1,0:T(8,128)S(1)} %bitcast.53), channel_id=1, replica_groups=mesh['row'=16,'col'=8] {'row'}, dimensions={0} | all-to-all | bytes 131072 | tf_op jit(solution)/shard_map/all_to_all | solution.py:276
  57.5 0.8 broadcast_in_dim.7
  58.3 5.8 %all-to-all-start.1 = ((f32[128,8,128]{2,1,0:T(8,128)}), f32[128,8,128]{2,1,0:T(8,128)S(1)}, u32[]{:S(2)}, u32[]{:S(2)}) async-start(f32[128,8,128]{2,1,0:T(8,128)} %broadcast_in_dim.7), calls=%async_computation.1 | async-start | bytes 1048576 | tf_op jit(solution)/shard_map/all_to_all | solution.py:277
  64.1 0.0 all-gather.9.cloned.1.call-start
  64.2 0.1 pad_add_fusion.place_ref
  64.2 16.9 %all-to-all-done.1 = f32[128,8,128]{2,1,0:T(8,128)S(1)} async-done(((f32[128,8,128]{2,1,0:T(8,128)}), f32[128,8,128]{2,1,0:T(8,128)S(1)}, u32[]{:S(2)}, u32[]{:S(2)}) %all-to-all-start.1) | async-done | bytes 524320 | tf_op jit(solution)/shard_map/all_to_all | solution.py:277
  81.1 0.1 copy.9
  81.2 0.7 fusion
  81.9 0.8 copy.11
  82.8 36.1 %shard_map.28 = (f32[256,256]{1,0:T(8,128)}, f32[256,256]{1,0:T(8,128)}) custom-call(f32[256,256]{1,0:T(8,128)} %get-tuple-element.16.gram_ref, f32[256,256]{1,0:T(8,128)} %bitcast.49), custom_call_target="tpu_custom_call" | custom-call | flops 33554432 | bytes 1048576 | tf_op jit(solution)/shard_map/pallas_call | solution.py:95
  118.8 0.0 all-gather.5.cloned.1.call-done
  118.8 0.9 copy-done.2
  119.8 10.6 %shard_map.29 = (f32[1280,256]{1,0:T(8,128)S(1)}, f32[256,256]{1,0:T(8,128)S(1)}) custom-call(s32[2]{0:T(128)S(1)} %pad_add_fusion.place_ref, f32[1280,2560]{1,0:T(8,128)} %a_ref.3, f32[2,256,1280]{2,1,0:T(8,128)} %bitcast.54, f32[256,1280]{1,0:T(8,128)S(1)} %bitcast.40, f32[256,256]{1,0:T(8,128)S(1)} %copy-done.2), custom_call_target="tpu_custom_call" | custom-call | flops 5033164800 | bytes 13107200 | tf_op jit(solution)/shard_map/pallas_call | solution.py:172
  130.4 21.2 %all_to_all.26 = f32[8,160,256]{2,1,0:T(8,128)S(1)} all-to-all(f32[8,160,256]{2,1,0:T(8,128)S(1)} %bitcast.42), channel_id=1, replica_groups=mesh['row'=16,'col'=8] {'col'}, dimensions={0} | all-to-all | bytes 2621440 | tf_op jit(solution)/shard_map/all_to_all | solution.py:282
  151.6 0.0 copy-start
  151.6 0.8 reduce_sum.28
  152.4 0.2 copy-done
  152.6 2.0 fusion.1
  154.6 0.0 all-gather.9.cloned.1.call-update
  154.6 0.0 all-gather.7.cloned.1.call-start
  154.6 3.1 %collective-permute-start.2 = (f32[160,256]{1,0:T(8,128)}, f32[160,256]{1,0:T(8,128)S(1)}, u32[]{:S(2)}, u32[]{:S(2)}) collective-permute-start(f32[160,256]{1,0:T(8,128)} %fusion.1), channel_id=1, source_target_pairs={{0,0},{1,8},{2,16},{3,24},{4,32},{5,40},{6,48},{7,56},{8,64},{9,72... | collective-permute-start | bytes 491528 | tf_op jit(solution)/shard_map/ppermute | solution.py:285
  157.8 6.8 %collective-permute-done.2 = f32[160,256]{1,0:T(8,128)S(1)} collective-permute-done((f32[160,256]{1,0:T(8,128)}, f32[160,256]{1,0:T(8,128)S(1)}, u32[]{:S(2)}, u32[]{:S(2)}) %collective-permute-start.2) | collective-permute-done | bytes 163872 | tf_op jit(solution)/shard_map/ppermute | solution.py:285
  164.6 0.0 copy-start.6
  164.6 0.7 copy-done.6
  165.2 0.0 all-gather.7.cloned.1.call-update
  165.3 24.7 %all_to_all.27 = f32[128,1,4,128]{3,2,1,0:T(4,128)S(1)} all-to-all(f32[128,1,4,128]{3,2,1,0:T(4,128)S(1)} %bitcast.43), channel_id=1, replica_groups=mesh['row'=16,'col'=8] {'row','col'}, dimensions={0} | all-to-all | bytes 524288 | tf_op jit(solution)/shard_map/all_to_all | solution.py:116
  189.9 0.1 reduce_sum.29
  190.1 16.1 %all_to_all.28 = f32[128,1,4,128]{3,2,1,0:T(4,128)S(1)} all-to-all(f32[128,1,4,128]{3,2,1,0:T(4,128)S(1)} %broadcast_in_dim.8), channel_id=1, replica_groups=mesh['row'=16,'col'=8] {'row','col'}, dimensions={0} | all-to-all | bytes 524288 | tf_op jit(solution)/shard_map/all_to_all | solution.py:117
  206.2 23.2 %all-gather.7.cloned.1.call-done.wcols_ref = f32[2560,256]{1,0:T(8,128)} async-done(((f32[160,256]{1,0:T(8,128)}), f32[2560,256]{1,0:T(8,128)}) %all-gather.7.cloned.1.call-update) | async-done | bytes 2621456 | tf_op jit(solution)/shard_map/all_gather | solution.py:286
  229.4 0.0 copy-done.3
  229.4 0.0 copy-start.1
  229.4 1.3 copy-done.1
  230.7 22.5 %shard_map.30 = f32[1280,2560]{1,0:T(8,128)} custom-call(s32[2]{0:T(128)S(1)} %pad_add_fusion.place_ref, f32[1280,2560]{1,0:T(8,128)} %a_ref.3, f32[2,256,1280]{2,1,0:T(8,128)} %bitcast.55, f32[2560,256]{1,0:T(8,128)} %all-gather.7.cloned.1.call-done.wcols_ref, f32[256,1280]{1,0:T(8,128)S(1)} %bitcast.41, f32[1280,256]{1,0:T(8,128)S(1)} %copy-done.1, ...), custom_call_target="tpu_custom_call" | custom-call | flops 10066329600 | bytes 26214400 | tf_op jit(solution)/shard_map/pallas_call | solution.py:232
  (6 shorter events, 0.1 us)
Async XLA Ops:
  6.5 112.3 %all-gather.5.cloned.1.call-start = ((), (), s32[]{:S(2)}) async-start(), calls=%async_computation.5 | async-start | bytes 2785280 | tf_op jit(solution)/shard_map/all_gather | solution.py:272
  6.5 10.6 %collective-permute-start = (f32[32,1280]{1,0:T(8,128)}, f32[32,1280]{1,0:T(8,128)S(1)}, u32[]{:S(2)}, u32[]{:S(2)}) collective-permute-start(f32[32,1280]{1,0:T(8,128)} %bitcast.50), channel_id=1, source_target_pairs={{0,0},{1,8},{2,16},{3,24},{4,32},{5,40},{6,48},{7,56},{8,64},{9,72... | collective-permute-start | bytes 491528 | tf_op jit(solution)/shard_map/ppermute | solution.py:267
  17.1 0.7 copy-start.5
  39.3 2.1 collective-permute-start.1
  41.6 0.9 copy-start.4
  58.3 22.8 %all-to-all-start.1 = ((f32[128,8,128]{2,1,0:T(8,128)}), f32[128,8,128]{2,1,0:T(8,128)S(1)}, u32[]{:S(2)}, u32[]{:S(2)}) async-start(f32[128,8,128]{2,1,0:T(8,128)} %broadcast_in_dim.7), calls=%async_computation.1 | async-start | bytes 1048576 | tf_op jit(solution)/shard_map/all_to_all | solution.py:277
  64.1 142.1 %all-gather.9.cloned.1.call-start = ((), (), s32[]{:S(2)}) async-start(), calls=%async_computation.7 | async-start | bytes 1474560 | tf_op jit(solution)/shard_map/all_gather | solution.py:287
  118.8 1.0 copy-start.2
  151.6 1.0 copy-start
  152.4 77.0 %copy-start.3 = (f32[256,256]{1,0:T(8,128)S(1)}, f32[256,256]{1,0:T(8,128)}, u32[]{:S(2)}) copy-start(f32[256,256]{1,0:T(8,128)} %get-tuple-element.9.lt_ref) | copy-start | bytes 786436
  154.6 74.8 %all-gather.7.cloned.1.call-start = ((), (), s32[]{:S(2)}) async-start(), calls=%async_computation.6 | async-start | bytes 2785280 | tf_op jit(solution)/shard_map/all_gather | solution.py:286
  154.6 9.9 %collective-permute-start.2 = (f32[160,256]{1,0:T(8,128)}, f32[160,256]{1,0:T(8,128)S(1)}, u32[]{:S(2)}, u32[]{:S(2)}) collective-permute-start(f32[160,256]{1,0:T(8,128)} %fusion.1), channel_id=1, source_target_pairs={{0,0},{1,8},{2,16},{3,24},{4,32},{5,40},{6,48},{7,56},{8,64},{9,72... | collective-permute-start | bytes 491528 | tf_op jit(solution)/shard_map/ppermute | solution.py:285
  164.6 0.7 copy-start.6
  229.4 1.3 copy-start.1
Sparse Core Ops, SparseCore 0:
  17.9 59.9 all-gather.4
  154.7 24.6 all-gather.8
  181.6 47.8 all-gather.6

commit v3 on v2

v3 whole, which is shorter than its diff:
```python
import jax
import jax.numpy as jnp
from jax import lax
from jax.experimental import pallas as pl
from jax.experimental.pallas import tpu as pltpu
from jax.sharding import PartitionSpec as P

W = 256
H = 128
BOTH = ("row", "col")
HIGHEST = lax.Precision.HIGHEST
HIGH = lax.Precision.HIGH


def lane(x, l):
    if x.shape[0] == 1:
        return lane(jnp.broadcast_to(x, (8, H)), l)[0:1]
    return jnp.take_along_axis(x, jnp.full(x.shape, l, jnp.int32), axis=1, mode="promise_in_bounds")


def factor_kernel(gram_ref, top_ref, lt_ref, tt_ref, gw, vr, lt, lw):
    ri = lax.broadcasted_iota(jnp.int32, (W, W), 0)
    ci = lax.broadcasted_iota(jnp.int32, (W, W), 1)
    li = lax.broadcasted_iota(jnp.int32, (1, H), 1)
    g = gram_ref[...]
    scale = 1.0 / jnp.max(jnp.where(ri == ci, g, 0.0), keepdims=True)
    root = jnp.sqrt(scale)
    t = top_ref[...] * root
    g = g * scale

    def dot(x, y):
        return jnp.dot(x, y, precision=HIGHEST, preferred_element_type=jnp.float32)

    def chol_step(j, row):
        here = li == j
        d = lane(row, j)
        rs = lax.rsqrt(d)
        rs = rs * (1.5 - 0.5 * d * rs * rs)
        inv = rs * rs
        mod = jnp.where(here, 1.0 + inv, row * inv)
        old = gw[pl.ds(jnp.minimum(j + 1, H - 1), 1), :]
        ahead = old - lane(old, j) * mod
        gw[...] = gw[...] - lane(gw[...], j) * mod
        scaled = row * rs
        lt[pl.ds(j, 1), :] = jnp.where(li >= j, scaled, 0.0)
        lw[pl.ds(j, 1), :] = jnp.where(here, rs, jnp.where(li < j, scaled, 0.0))
        return ahead, rs, scaled

    def jordan_step(j, row, rs, scaled):
        here = li == j
        row = row + scaled
        q = 1.0 / lane(row, j)
        norm = row * q
        rq = rs * q
        mod = jnp.where(here, 1.0 + rq, norm)
        old = vr[pl.ds(jnp.minimum(j + 1, H - 1), 1), :]
        ahead = old - lane(old, j) * mod
        vr[...] = vr[...] - lane(vr[...], j) * mod
        vr[pl.ds(j, 1), :] = jnp.where(here, rq, norm)
        return ahead

    def block(gram, top):
        gw[...] = gram
        vr[...] = top

        def body(j, carry):
            row, rs, scaled, vrow = carry
            new = chol_step(j, row)
            vrow = jordan_step(j - 1, vrow, rs, scaled)
            return new + (vrow,)

        carry = chol_step(0, gram[0:1]) + (top[0:1],)
        row, rs, scaled, vrow = lax.fori_loop(1, H, body, carry)
        jordan_step(H - 1, vrow, rs, scaled)
        return lt[...], lw[...], vr[...]

    g12, g22 = g[:H, H:], g[H:, H:]
    l11t, w11, x11 = block(g[:H, :H], t[:H, :H])
    l21t = dot(w11, g12)
    l21 = l21t.T
    inv11 = dot(x11, l11t.T)
    v12 = t[:H, H:] + l21t
    k21 = dot(t[H:, :H], inv11)
    n12 = dot(inv11, v12)
    l22t, w22, x22 = block(g22 - dot(l21, l21t), t[H:, H:] - dot(k21, v12))
    t21 = -dot(x22, dot(l21 + dot(l22t.T, k21), w11))
    unroot = 1.0 / root
    lt_ref[:H, :H] = l11t * unroot
    lt_ref[:H, H:] = l21t * unroot
    lt_ref[H:, :H] = jnp.zeros((H, H), jnp.float32)
    lt_ref[H:, H:] = l22t * unroot
    tt_ref[:H, :H] = (x11 - dot(n12, t21)) * scale
    tt_ref[:H, H:] = -dot(n12, x22) * scale
    tt_ref[H:, :H] = t21 * scale
    tt_ref[H:, H:] = x22 * scale


def factor(gram, top):
    vmem = pl.BlockSpec(memory_space=pltpu.VMEM)
    return pl.pallas_call(
        factor_kernel,
        out_shape=[jax.ShapeDtypeStruct((W, W), jnp.float32)] * 2,
        in_specs=[vmem] * 2,
        out_specs=[vmem] * 2,
        scratch_shapes=[pltpu.VMEM((H, H), jnp.float32)] * 4,
        cost_estimate=pl.CostEstimate(flops=2 * W**3, bytes_accessed=16 * W * W, transcendentals=0),
    )(gram, top)


def to_tiles(x):
    rows, cols = x.shape
    return x.reshape(rows // 8, 8, cols // H, H).transpose(0, 2, 1, 3).reshape(rows * cols // (8 * H), 8, H)


def from_tiles(x, rows, cols):
    return x.reshape(rows // 8, cols // H, 8, H).transpose(0, 2, 1, 3).reshape(rows, cols)


def sum_all(x, axes, parts):
    pieces = x.reshape((parts, -1) + x.shape[1:])
    mine = jnp.sum(lax.all_to_all(pieces, axes, 0, 0, tiled=True), axis=0)
    full = lax.all_to_all(jnp.broadcast_to(mine[None], (parts,) + mine.shape), axes, 0, 0, tiled=True)
    return full.reshape(x.shape)


def split(x):
    high = x.astype(jnp.bfloat16)
    return high, (x - high.astype(jnp.float32)).astype(jnp.bfloat16)


NN = ((1,), (0,))
NT = ((1,), (1,))
VMEM_BYTES = 50 * 1024 * 1024


def stack3(a, b, axis):
    a_high, a_low = split(a)
    b_high, b_low = split(b)
    return jnp.concatenate([a_high, a_high, a_low], axis=axis[0]), jnp.concatenate([b_high, b_low, b_high], axis=axis[1])


def dots(a, b, contract):
    left, right = stack3(a, b, (contract[0][0], contract[1][0]))
    return lax.dot_general(left, right, (contract, ((), ())), preferred_element_type=jnp.float32)


def product_kernel(place_ref, a_ref, cols_ref, rows_ref, lt_ref, out_ref, inner_ref, acc):
    step = pl.program_id(0)
    steps = pl.num_programs(0)
    lower = lt_ref[...].T

    @pl.when(step == 0)
    def _():
        own = (place_ref[1] == 0).astype(jnp.float32)
        first = cols_ref[0, :, :W] + own * lower
        rest = cols_ref[0, :, W:]
        acc[...] = dots(a_ref[:, :W], first, NT) + dots(a_ref[:, W:], rest, NT)

    @pl.when(step > 0)
    def _():
        acc[...] += dots(a_ref[...], cols_ref[0], NT)

    @pl.when(step == steps - 1)
    def _():
        total = acc[...]
        out_ref[...] = total
        own = (place_ref[0] == 0).astype(jnp.float32)
        inner = dots(rows_ref[:, :W] + own * lower, total[:W], NN)
        inner_ref[...] = inner + dots(rows_ref[:, W:], total[W:], NN)


def product(place, trailing, panel_cols, panel_rows, factor_t):
    rows, cols = trailing.shape
    half = panel_cols.shape[2]
    tile = 640
    per = half // tile
    return pl.pallas_call(
        product_kernel,
        grid=(cols // tile,),
        out_shape=[jax.ShapeDtypeStruct((rows, W), jnp.float32), jax.ShapeDtypeStruct((W, W), jnp.float32)],
        in_specs=[
            pl.BlockSpec(memory_space=pltpu.SMEM),
            pl.BlockSpec((rows, tile), lambda i: (0, i)),
            pl.BlockSpec((1, W, tile), lambda i: (i // per, 0, i % per)),
            pl.BlockSpec((W, rows), lambda i: (0, 0)),
            pl.BlockSpec((W, W), lambda i: (0, 0)),
        ],
        out_specs=[pl.BlockSpec((rows, W), lambda i: (0, 0)), pl.BlockSpec((W, W), lambda i: (0, 0))],
        scratch_shapes=[pltpu.VMEM((rows, W), jnp.float32)],
        compiler_params=pltpu.CompilerParams(vmem_limit_bytes=VMEM_BYTES),
        cost_estimate=pl.CostEstimate(flops=6 * rows * cols * W, bytes_accessed=4 * rows * cols, transcendentals=0),
    )(place, trailing, panel_cols, panel_rows, factor_t)


def prepare_kernel(place_ref, cols_ref, rows_ref, wrows_ref, lt_ref, tt_ref, inner_ref, left_ref, right_ref):
    t = tt_ref[...]
    mid = jnp.dot(t, inner_ref[...], precision=HIGHEST, preferred_element_type=jnp.float32)
    square = lax.dot_general(mid, t, (NT, ((), ())), precision=HIGHEST, preferred_element_type=jnp.float32)
    own_rows = (place_ref[0] == 0).astype(jnp.float32)
    own_cols = (place_ref[1] == 0).astype(jnp.float32)
    lt = lt_ref[...]
    for i in range(rows_ref.shape[1] // W):
        at = slice(i * W, (i + 1) * W)
        reflect = rows_ref[:, at].T
        if i == 0:
            reflect = reflect + lt * own_rows
        weights = wrows_ref[at] - dots(reflect, square, NN)
        for k, x in enumerate((reflect, weights)):
            high, low = split(x)
            for p, part in enumerate((high, high, low)):
                left_ref[at, (3 * k + p) * W : (3 * k + p + 1) * W] = part
    half = cols_ref.shape[2]
    for h in range(cols_ref.shape[0]):
        for i in range(half // W):
            cols = cols_ref[h, :, i * W : (i + 1) * W]
            if h == 0 and i == 0:
                cols = cols + lt.T * own_cols
            high, low = split(cols)
            at = slice(h * half + i * W, h * half + (i + 1) * W)
            for p, part in enumerate((high, low, high)):
                right_ref[p * W : (p + 1) * W, at] = part


def prepare(place, panel_cols, panel_rows, weight_rows, factor_t, coupling_t, inner):
    rows = panel_rows.shape[1]
    cols = panel_cols.shape[0] * panel_cols.shape[2]
    vmem = pl.BlockSpec(memory_space=pltpu.VMEM)
    return pl.pallas_call(
        prepare_kernel,
        out_shape=[jax.ShapeDtypeStruct((rows, 6 * W), jnp.bfloat16), jax.ShapeDtypeStruct((3 * W, cols), jnp.bfloat16)],
        in_specs=[pl.BlockSpec(memory_space=pltpu.SMEM)] + [vmem] * 6,
        out_specs=[vmem] * 2,
        compiler_params=pltpu.CompilerParams(vmem_limit_bytes=VMEM_BYTES),
        cost_estimate=pl.CostEstimate(flops=6 * rows * W * W, bytes_accessed=16 * rows * W, transcendentals=0),
    )(place, panel_cols, panel_rows, weight_rows, factor_t, coupling_t, inner)


def update_kernel(a_ref, left_ref, right_ref, weights_ref, out_ref):
    high, low = split(weights_ref[...].T)
    right = jnp.concatenate([high, low, high], axis=0)
    first = jnp.dot(left_ref[:, : 3 * W], right, preferred_element_type=jnp.float32)
    second = jnp.dot(left_ref[:, 3 * W :], right_ref[...], preferred_element_type=jnp.float32)
    out_ref[...] = a_ref[...] - (first + second)


def update(trailing, left, right, weight_cols):
    rows, cols = trailing.shape
    tile = 512
    return pl.pallas_call(
        update_kernel,
        grid=(cols // tile,),
        out_shape=jax.ShapeDtypeStruct((rows, cols), jnp.float32),
        in_specs=[
            pl.BlockSpec((rows, tile), lambda i: (0, i)),
            pl.BlockSpec((rows, 6 * W), lambda i: (0, 0)),
            pl.BlockSpec((3 * W, tile), lambda i: (0, i)),
            pl.BlockSpec((tile, W), lambda i: (i, 0)),
        ],
        out_specs=pl.BlockSpec((rows, tile), lambda i: (0, i)),
        compiler_params=pltpu.CompilerParams(vmem_limit_bytes=VMEM_BYTES),
        cost_estimate=pl.CostEstimate(flops=12 * rows * cols * W, bytes_accessed=8 * rows * cols, transcendentals=0),
    )(trailing, left, right, weight_cols)


def shards(trailing, panel_block):
    r = lax.axis_index("row")
    c = lax.axis_index("col")
    nr = lax.axis_size("row")
    nc = lax.axis_size("col")
    ratio = nr // nc
    perm = [(i * nc + j, ((i % ratio) * nc + j) * nc + i // ratio) for i in range(nr) for j in range(nc)]
    pair = [(j, j ^ 1) for j in range(nc)]
    lines = [list(range(k, nc, 2)) for k in range(2)]
    place = jnp.stack([r, c]).astype(jnp.int32)
    rows, width = panel_block.shape
    part = rows // nc
    panel_t = panel_block.T

    def gather_col(x):
        line = lax.all_gather(x, "col", axis=0, axis_index_groups=lines)
        other = lax.ppermute(line, "col", pair)
        even = c % 2 == 0
        both = jnp.stack([jnp.where(even, line, other), jnp.where(even, other, line)], axis=1)
        return both.reshape((-1,) + x.shape[1:])

    panel_rows = gather_col(panel_t)
    panel_rows, later = lax.optimization_barrier((panel_rows, panel_t))
    moved = lax.ppermute(later, BOTH, perm)
    panel_cols = lax.all_gather(moved, "row", axis=0, tiled=True).reshape(ratio, W, rows)
    strip = lax.dot_general(panel_t, panel_rows, (((1,), (1,)), ((), ())), precision=HIGHEST)
    top = jnp.where(r == 0, panel_t[:, :W], jnp.zeros((width, W), jnp.float32))
    pieces = to_tiles(jnp.concatenate([strip, top], axis=1))
    mine = jnp.sum(lax.all_to_all(pieces, "row", 0, 0, tiled=True), axis=0)
    full = lax.all_to_all(jnp.broadcast_to(mine[None], (nr * nc,) + mine.shape), BOTH, 0, 0, tiled=True)
    tr, tc = width // 8, 2 * W // H
    full = full.reshape(tr, tc, nc, 8, H).transpose(2, 0, 3, 1, 4).reshape(W, 2 * W)
    factor_t, coupling_t = factor(full[:, :W], full[:, W:].T)
    partial, inner = product(place, trailing, panel_cols, panel_rows, factor_t)
    pieces = lax.all_to_all(partial.reshape(nc, part, W), "col", 0, 0, tiled=True)
    mine = jnp.sum(pieces, axis=0)
    mine = lax.dot_general(mine, coupling_t, (((1,), (1,)), ((), ())), precision=HIGHEST)
    moved = lax.ppermute(mine, BOTH, perm)
    weight_cols = lax.all_gather(moved, "row", axis=0, tiled=True)
    weight_rows = gather_col(mine)
    inner = from_tiles(sum_all(to_tiles(inner).reshape(nr * nc, 4, H), BOTH, nr * nc).reshape(-1, 8, H), W, W)
    left, right = prepare(place, panel_cols, panel_rows, weight_rows, factor_t, coupling_t, inner)
    return update(trailing, left, right, weight_cols)


def solution(mesh):
    return jax.shard_map(shards, mesh=mesh, in_specs=(P("row", "col"), P("row", "col")), out_specs=P("row", "col"), check_vma=False)
```

time: 261 us -> 247 us (0.946)
  waiting for transfers between devices: 53.9 us -> 38.9 us
  starting transfers between devices: 13.9 us -> 22.7 us
  blocking collectives: 97.2 us -> 93 us
    all_gather x1, waiting for transfers between devices: 23.2 us -> 0.01 us  [shards(): weight_cols = lax.all_gather(moved, 'row', axis=0, tiled=True)]
    all_to_all x1 -> x0, blocking collectives: 16.1 us -> none  [sum_all(): lax.all_to_all(jnp.broadcast_to(mine[None], (parts,) + mine.shape), axes,...]
    all_to_all x0 -> x1, waiting for transfers between devices: none -> 13.1 us  [sum_all(): lax.all_to_all(jnp.broadcast_to(mine[None], (parts,) + mine.shape), axes,...]
    all_gather x1 -> x2, blocking collectives: 21.5 us -> 32.4 us  [gather_col(): line = lax.all_gather(x, 'col', axis=0, axis_index_groups=lines)]
    all_to_all x1, blocking collectives: 13.7 us -> 21.5 us  [shards(): mine = jnp.sum(lax.all_to_all(pieces, 'row', 0, 0, tiled=True), axis=0)]
    all_to_all x1, blocking collectives: 24.7 us -> 17.8 us  [sum_all(): mine = jnp.sum(lax.all_to_all(pieces, axes, 0, 0, tiled=True), axis=0)]
    pallas_call x0 -> x1, Pallas kernels: none -> 6.6 us  [prepare(): pl.pallas_call(prepare_kernel, out_shape=[jax.ShapeDtypeStruct((rows, 6 *...]
    pallas_call x1, Pallas kernels: 22.5 us -> 17.1 us  [update(): pl.pallas_call(update_kernel, grid=(cols // tile,), out_shape=jax.ShapeDt...]
  transfers between devices with their start and end apart: 7 -> 8, of which waited for: 5 -> 5; matrix products, arithmetic and copies ran while one was open for 2% -> 2% of each run, Pallas kernels for 14% -> 16%
where the time goes in v3:
time: 247 us
  blocking collectives  93 us (38%)
  Pallas kernels  67.2 us (27%)
  waiting for transfers between devices  38.9 us (16%)
  starting transfers between devices  22.7 us (9%)
  between operations  13.6 us (6%)
  local copies, waits for them, and re-layouts  8.88 us (4%)
    pallas_call x1, Pallas kernels, factor(): pl.pallas_call(factor_kernel, out_shape=[jax.ShapeDtypeStruct((W, W), jnp...  33.3 us
    all_gather x2, blocking collectives, gather_col(): line = lax.all_gather(x, 'col', axis=0, axis_index_groups=lines)  32.4 us
    all_to_all x1, blocking collectives, shards(): mine = jnp.sum(lax.all_to_all(pieces, 'row', 0, 0, tiled=True), axis=0)  21.5 us
    all_to_all x1, blocking collectives, shards(): lax.all_to_all(partial.reshape(nc, part, W), 'col', 0, 0, tiled=True)  21.4 us
    all_to_all x1, blocking collectives, sum_all(): mine = jnp.sum(lax.all_to_all(pieces, axes, 0, 0, tiled=True), axis=0)  17.8 us
    pallas_call x1, Pallas kernels, update(): pl.pallas_call(update_kernel, grid=(cols // tile,), out_shape=jax.ShapeDt...  17.1 us
    all_to_all x1, waiting for transfers between devices, shards(): lax.all_to_all(jnp.broadcast_to(mine[None], (nr * nc,) + mine.shape), BOT...  13.5 us
    all_to_all x1, waiting for transfers between devices, sum_all(): lax.all_to_all(jnp.broadcast_to(mine[None], (parts,) + mine.shape), axes,...  13.1 us
  transfers between devices with their start and end apart: 8, of which 5 were waited for; matrix products, arithmetic and copies ran while one was open for 2% of the time, Pallas kernels for 16%

profile of v3, /device:TPU:1, one launch (start us, length us, event | category | flops | bytes accessed | tf_op | source)
XLA Modules:
  0.0 246.6 jit_solution(17660908091417335044)
XLA Ops:
  6.5 0.0 all-gather.5.cloned.1.call-start
  6.5 13.2 %all-gather = f32[128,1280]{1,0:T(8,128)S(1)} all-gather(f32[32,1280]{1,0:T(8,128)} %bitcast.63), channel_id=2, replica_groups={{0,2,4,6},{1,3,5,7},{8,10,12,14},{9,11,13,15},{16,18,20,22},{17,19,21,2..., dimensions={0}, use_global_device_ids=true | all-gather | bytes 819200 | tf_op jit(solution)/shard_map/all_gather | solution.py:280
  19.7 2.1 collective-permute-start
  21.8 1.7 collective-permute-done
  23.5 0.1 select_bitcast_fusion.3
  23.6 0.0 copy-start.4
  23.7 0.1 pad_maximum_fusion
  23.8 0.8 copy-done.4
  24.6 3.8 %collective-permute-start.1 = (f32[32,1280]{1,0:T(8,128)S(1)}, f32[32,1280]{1,0:T(8,128)S(1)}, u32[]{:S(2)}, u32[]{:S(2)}) collective-permute-start(f32[32,1280]{1,0:T(8,128)S(1)} %bitcast.64), channel_id=1, source_target_pairs={{0,0},{1,8},{2,16},{3,24},{4,32},{5,40},{6,48},{7,56},{8,64},{9,72... | collective-permute-start | bytes 491528 | tf_op jit(solution)/shard_map/ppermute | solution.py:288
  28.4 5.0 %collective-permute-done.1 = f32[32,1280]{1,0:T(8,128)S(1)} collective-permute-done((f32[32,1280]{1,0:T(8,128)S(1)}, f32[32,1280]{1,0:T(8,128)S(1)}, u32[]{:S(2)}, u32[]{:S(2)}) %collective-permute-start.1) | collective-permute-done | bytes 163872 | tf_op jit(solution)/shard_map/ppermute | solution.py:288
  33.4 0.7 copy-done.5
  34.1 0.0 all-gather.5.cloned.1.call-update
  34.1 1.2 convolution_bitcast_fusion
  35.3 21.5 %all_to_all.25 = f32[16,8,128]{2,1,0:T(8,128)S(1)} all-to-all(f32[16,8,128]{2,1,0:T(8,128)S(1)} %bitcast.66), channel_id=1, replica_groups=mesh['row'=16,'col'=8] {'row'}, dimensions={0} | all-to-all | bytes 131072 | tf_op jit(solution)/shard_map/all_to_all | solution.py:293
  56.8 0.8 broadcast_in_dim.7
  57.7 6.8 %all-to-all-start.1 = ((f32[128,8,128]{2,1,0:T(8,128)}), f32[128,8,128]{2,1,0:T(8,128)S(1)}, u32[]{:S(2)}, u32[]{:S(2)}) async-start(f32[128,8,128]{2,1,0:T(8,128)} %broadcast_in_dim.7), calls=%async_computation.1 | async-start | bytes 1048576 | tf_op jit(solution)/shard_map/all_to_all | solution.py:294
  64.4 0.0 all-gather.7.cloned.1.call-start
  64.5 0.1 pad_add_fusion.place_ref
  64.6 13.5 %all-to-all-done.1 = f32[128,8,128]{2,1,0:T(8,128)S(1)} async-done(((f32[128,8,128]{2,1,0:T(8,128)}), f32[128,8,128]{2,1,0:T(8,128)S(1)}, u32[]{:S(2)}, u32[]{:S(2)}) %all-to-all-start.1) | async-done | bytes 524320 | tf_op jit(solution)/shard_map/all_to_all | solution.py:294
  78.0 0.1 copy.11
  78.1 0.7 fusion
  78.8 0.8 copy.14
  79.6 33.3 %shard_map.28 = (f32[256,256]{1,0:T(8,128)}, f32[256,256]{1,0:T(8,128)}) custom-call(f32[256,256]{1,0:T(8,128)} %get-tuple-element.26.gram_ref, f32[256,256]{1,0:T(8,128)} %bitcast.62), custom_call_target="tpu_custom_call" | custom-call | flops 33554432 | bytes 1048576 | tf_op jit(solution)/shard_map/pallas_call | solution.py:100
  113.0 0.9 copy-done.1
  113.9 10.2 %shard_map.29 = (f32[1280,256]{1,0:T(8,128)S(1)}, f32[256,256]{1,0:T(8,128)S(1)}) custom-call(s32[2]{0:T(128)S(1)} %pad_add_fusion.place_ref, f32[1280,2560]{1,0:T(8,128)} %a_ref.3, f32[2,256,1280]{2,1,0:T(8,128)} %bitcast.54, f32[256,1280]{1,0:T(8,128)S(1)} %bitcast.48, f32[256,256]{1,0:T(8,128)S(1)} %copy-done.1), custom_call_target="tpu_custom_call" | custom-call | flops 5033164800 | bytes 13107200 | tf_op jit(solution)/shard_map/pallas_call | solution.py:177
  124.1 21.4 %all_to_all.26 = f32[8,160,256]{2,1,0:T(8,128)S(1)} all-to-all(f32[8,160,256]{2,1,0:T(8,128)S(1)} %bitcast.51), channel_id=1, replica_groups=mesh['row'=16,'col'=8] {'col'}, dimensions={0} | all-to-all | bytes 2621440 | tf_op jit(solution)/shard_map/all_to_all | solution.py:299
  145.5 0.1 reduce_sum.28
  145.6 0.9 copy-done
  146.5 0.4 fusion.1
  146.9 3.5 %collective-permute-start.3 = (f32[160,256]{1,0:T(8,128)S(1)}, f32[160,256]{1,0:T(8,128)S(1)}, u32[]{:S(2)}, u32[]{:S(2)}) collective-permute-start(f32[160,256]{1,0:T(8,128)S(1)} %fusion.1), channel_id=1, source_target_pairs={{0,0},{1,8},{2,16},{3,24},{4,32},{5,40},{6,48},{7,56},{8,64},{9,72... | collective-permute-start | bytes 491528 | tf_op jit(solution)/shard_map/ppermute | solution.py:302
  150.3 5.6 %collective-permute-done.3 = f32[160,256]{1,0:T(8,128)S(1)} collective-permute-done((f32[160,256]{1,0:T(8,128)S(1)}, f32[160,256]{1,0:T(8,128)S(1)}, u32[]{:S(2)}, u32[]{:S(2)}) %collective-permute-start.3) | collective-permute-done | bytes 163872 | tf_op jit(solution)/shard_map/ppermute | solution.py:302
  155.9 0.7 copy-done.6
  156.6 0.0 all-gather.7.cloned.1.call-update
  156.6 19.2 %all-gather.1 = f32[640,256]{1,0:T(8,128)S(1)} all-gather(f32[160,256]{1,0:T(8,128)S(1)} %fusion.1), channel_id=3, replica_groups={{0,2,4,6},{1,3,5,7},{8,10,12,14},{9,11,13,15},{16,18,20,22},{17,19,21,2..., dimensions={0}, use_global_device_ids=true | all-gather | bytes 819200 | tf_op jit(solution)/shard_map/all_gather | solution.py:280
  175.8 1.9 collective-permute-start.2
  177.7 17.8 %all_to_all.27 = f32[128,1,4,128]{3,2,1,0:T(4,128)S(1)} all-to-all(f32[128,1,4,128]{3,2,1,0:T(4,128)S(1)} %bitcast.53), channel_id=1, replica_groups=mesh['row'=16,'col'=8] {'row','col'}, dimensions={0} | all-to-all | bytes 524288 | tf_op jit(solution)/shard_map/all_to_all | solution.py:121
  195.5 0.1 reduce_sum.29
  195.6 0.7 broadcast_in_dim.8
  196.3 4.7 %all-to-all-start.4 = ((f32[128,1,4,128]{3,2,1,0:T(4,128)}), f32[128,1,4,128]{3,2,1,0:T(4,128)S(1)}, u32[]{:S(2)}, u32[]{:S(2)}) async-start(f32[128,1,4,128]{3,2,1,0:T(4,128)} %broadcast_in_dim.8), calls=%async_computation.4 | async-start | bytes 524288 | tf_op jit(solution)/shard_map/all_to_all | solution.py:122
  201.0 0.0 collective-permute-done.2
  201.0 0.1 select_bitcast_fusion.1
  201.1 0.0 copy-start.2
  201.1 0.1 pad_maximum_fusion.1
  201.2 13.1 %all-to-all-done.4 = f32[128,1,4,128]{3,2,1,0:T(4,128)S(1)} async-done(((f32[128,1,4,128]{3,2,1,0:T(4,128)}), f32[128,1,4,128]{3,2,1,0:T(4,128)S(1)}, u32[]{:S(2)}, u32[]{:S(2)}) %all-to-all-start.4) | async-done | bytes 262176 | tf_op jit(solution)/shard_map/all_to_all | solution.py:122
  214.3 0.0 copy-done.2
  214.3 6.6 %shard_map.30 = (bf16[1280,1536]{1,0:T(8,128)(2,1)}, bf16[768,2560]{1,0:T(8,128)(2,1)}) custom-call(s32[2]{0:T(128)S(1)} %pad_add_fusion.place_ref, f32[2,256,1280]{2,1,0:T(8,128)} %bitcast.55, f32[256,1280]{1,0:T(8,128)S(1)} %bitcast.49, f32[1280,256]{1,0:T(8,128)S(1)} %bitcast.50, f32[256,256]{1,0:T(8,128)S(1)} %copy-done.2, f32[256,256]{1,0:T(8,128)S(1)} %copy-done, ...), custom_call_target="tpu_custom_call" | custom-call | flops 503316480 | bytes 5242880 | tf_op jit(solution)/shard_map/pallas_call | solution.py:228
  220.9 1.7 copy-done.3
  222.7 17.1 %shard_map.31 = f32[1280,2560]{1,0:T(8,128)} custom-call(f32[1280,2560]{1,0:T(8,128)} %a_ref.3, bf16[1280,1536]{1,0:T(8,128)(2,1)} %get-tuple-element.19.left_ref, bf16[768,2560]{1,0:T(8,128)(2,1)} %get-tuple-element.20.right_ref, f32[2560,256]{1,0:T(8,128)S(1)} %copy-done.3), custom_call_target="tpu_custom_call" | custom-call | flops 10066329600 | bytes 26214400 | tf_op jit(solution)/shard_map/pallas_call | solution.py:249
  (10 shorter events, 0.0 us)
Async XLA Ops:
  6.5 106.4 %all-gather.5.cloned.1.call-start = ((), (), s32[]{:S(2)}) async-start(), calls=%async_computation.5 | async-start | bytes 2785280 | tf_op jit(solution)/shard_map/all_gather | solution.py:289
  19.7 3.8 %collective-permute-start = (f32[4,32,1280]{2,1,0:T(8,128)S(1)}, f32[4,32,1280]{2,1,0:T(8,128)S(1)}, u32[]{:S(2)}, u32[]{:S(2)}) collective-permute-start(f32[4,32,1280]{2,1,0:T(8,128)S(1)} %bitcast.56), channel_id=1, source_target_pairs={{0,1},{1,0},{2,3},{3,2},{4,5},{5,4},{6,7},{7,6},{8,9},{9,8},{10,11... | collective-permute-start | bytes 1966088 | tf_op jit(solution)/shard_map/ppermute | solution.py:281
  23.6 0.9 copy-start.4
  24.6 8.8 %collective-permute-start.1 = (f32[32,1280]{1,0:T(8,128)S(1)}, f32[32,1280]{1,0:T(8,128)S(1)}, u32[]{:S(2)}, u32[]{:S(2)}) collective-permute-start(f32[32,1280]{1,0:T(8,128)S(1)} %bitcast.64), channel_id=1, source_target_pairs={{0,0},{1,8},{2,16},{3,24},{4,32},{5,40},{6,48},{7,56},{8,64},{9,72... | collective-permute-start | bytes 491528 | tf_op jit(solution)/shard_map/ppermute | solution.py:288
  33.4 0.7 copy-start.5
  57.7 20.4 %all-to-all-start.1 = ((f32[128,8,128]{2,1,0:T(8,128)}), f32[128,8,128]{2,1,0:T(8,128)S(1)}, u32[]{:S(2)}, u32[]{:S(2)}) async-start(f32[128,8,128]{2,1,0:T(8,128)} %broadcast_in_dim.7), calls=%async_computation.1 | async-start | bytes 1048576 | tf_op jit(solution)/shard_map/all_to_all | solution.py:294
  64.4 156.5 %all-gather.7.cloned.1.call-start = ((), (), s32[]{:S(2)}) async-start(), calls=%async_computation.6 | async-start | bytes 2785280 | tf_op jit(solution)/shard_map/all_gather | solution.py:303
  113.0 1.0 copy-start.1
  145.5 1.0 copy-start
  146.9 9.0 %collective-permute-start.3 = (f32[160,256]{1,0:T(8,128)S(1)}, f32[160,256]{1,0:T(8,128)S(1)}, u32[]{:S(2)}, u32[]{:S(2)}) collective-permute-start(f32[160,256]{1,0:T(8,128)S(1)} %fusion.1), channel_id=1, source_target_pairs={{0,0},{1,8},{2,16},{3,24},{4,32},{5,40},{6,48},{7,56},{8,64},{9,72... | collective-permute-start | bytes 491528 | tf_op jit(solution)/shard_map/ppermute | solution.py:302
  155.9 0.7 copy-start.6
  175.8 25.2 %collective-permute-start.2 = (f32[4,160,256]{2,1,0:T(8,128)S(1)}, f32[4,160,256]{2,1,0:T(8,128)S(1)}, u32[]{:S(2)}, u32[]{:S(2)}) collective-permute-start(f32[4,160,256]{2,1,0:T(8,128)S(1)} %bitcast.58), channel_id=1, source_target_pairs={{0,1},{1,0},{2,3},{3,2},{4,5},{5,4},{6,7},{7,6},{8,9},{9,8},{10,11... | collective-permute-start | bytes 1966088 | tf_op jit(solution)/shard_map/ppermute | solution.py:281
  196.3 18.0 %all-to-all-start.4 = ((f32[128,1,4,128]{3,2,1,0:T(4,128)}), f32[128,1,4,128]{3,2,1,0:T(4,128)S(1)}, u32[]{:S(2)}, u32[]{:S(2)}) async-start(f32[128,1,4,128]{3,2,1,0:T(4,128)} %broadcast_in_dim.8), calls=%async_computation.4 | async-start | bytes 524288 | tf_op jit(solution)/shard_map/all_to_all | solution.py:122
  201.1 13.2 %copy-start.2 = (f32[256,256]{1,0:T(8,128)S(1)}, f32[256,256]{1,0:T(8,128)}, u32[]{:S(2)}) copy-start(f32[256,256]{1,0:T(8,128)} %get-tuple-element.15.lt_ref) | copy-start | bytes 786436
  220.9 1.7 copy-start.3
Sparse Core Ops, SparseCore 0:
  34.2 54.9 all-gather.4
  156.7 54.4 all-gather.6

commit v4 on v3

--- a/solution.py
+++ b/solution.py
@@ -7,9 +7,9 @@
 
 W = 256
 H = 128
+PANEL = 8
 BOTH = ("row", "col")
 HIGHEST = lax.Precision.HIGHEST
-HIGH = lax.Precision.HIGH
 
 
 def lane(x, l):
@@ -18,7 +18,37 @@
     return jnp.take_along_axis(x, jnp.full(x.shape, l, jnp.int32), axis=1, mode="promise_in_bounds")
 
 
-def factor_kernel(gram_ref, top_ref, lt_ref, tt_ref, gw, vr, lt, lw):
+def panel_step(solo, rows, at):
+    li = lax.broadcasted_iota(jnp.int32, (1, H), 1)
+    sub = lax.broadcasted_iota(jnp.int32, (PANEL, H), 0)
+    cols = [lane(rows, at + k) for k in range(PANEL)]
+    mods, ratios, marks = [], [], []
+    for a in range(PANEL):
+        here = li == at + a
+        row = rows[a : a + 1]
+        tops = [cols[k][a : a + 1] for k in range(PANEL)]
+        mod, ratio, final, mark = solo(a, here, row, tops)
+        mods.append(mod)
+        ratios.append(ratio)
+        marks.append(mark)
+        own = sub == a
+        rows = jnp.where(own, final, rows - cols[a] * mod)
+        for k in range(a + 1, PANEL):
+            cols[k] = jnp.where(own, ratio[k], cols[k] - cols[a] * ratio[k])
+    for a in range(PANEL - 2, -1, -1):
+        for k in range(a + 1, PANEL):
+            mods[a] = mods[a] - ratios[a][k] * mods[k]
+    return rows, mods, marks
+
+
+def update_rows(mat, cols, mods):
+    new = mat[...]
+    for col, mod in zip(cols, mods):
+        new = new - col * mod
+    mat[...] = new
+
+
+def factor_kernel(gram_ref, top_ref, lt_ref, tt_ref, gw, vr, lt, lw, spread):
     ri = lax.broadcasted_iota(jnp.int32, (W, W), 0)
     ci = lax.broadcasted_iota(jnp.int32, (W, W), 1)
     li = lax.broadcasted_iota(jnp.int32, (1, H), 1)
@@ -31,47 +61,63 @@
     def dot(x, y):
         return jnp.dot(x, y, precision=HIGHEST, preferred_element_type=jnp.float32)
 
-    def chol_step(j, row):
-        here = li == j
-        d = lane(row, j)
-        rs = lax.rsqrt(d)
-        rs = rs * (1.5 - 0.5 * d * rs * rs)
-        inv = rs * rs
-        mod = jnp.where(here, 1.0 + inv, row * inv)
-        old = gw[pl.ds(jnp.minimum(j + 1, H - 1), 1), :]
-        ahead = old - lane(old, j) * mod
-        gw[...] = gw[...] - lane(gw[...], j) * mod
-        scaled = row * rs
-        lt[pl.ds(j, 1), :] = jnp.where(li >= j, scaled, 0.0)
-        lw[pl.ds(j, 1), :] = jnp.where(here, rs, jnp.where(li < j, scaled, 0.0))
-        return ahead, rs, scaled
-
-    def jordan_step(j, row, rs, scaled):
-        here = li == j
-        row = row + scaled
-        q = 1.0 / lane(row, j)
-        norm = row * q
-        rq = rs * q
-        mod = jnp.where(here, 1.0 + rq, norm)
-        old = vr[pl.ds(jnp.minimum(j + 1, H - 1), 1), :]
-        ahead = old - lane(old, j) * mod
-        vr[...] = vr[...] - lane(vr[...], j) * mod
-        vr[pl.ds(j, 1), :] = jnp.where(here, rq, norm)
-        return ahead
+    def chol_panel(at):
+        old = [lane(gw[...], at + k) for k in range(PANEL)]
+
+        def solo(a, here, row, tops):
+            d = tops[a]
+            inv = 1.0 / d
+            rs = lax.rsqrt(d)
+            rs = rs * (1.5 - 0.5 * d * rs * rs)
+            scaled = row * rs
+            mod = jnp.where(here, 1.0 + inv, row * inv)
+            ratio = [top * inv for top in tops]
+            upper = jnp.where(li >= at + a, scaled, 0.0)
+            lower = jnp.where(here, rs, jnp.where(li < at + a, scaled, 0.0))
+            marks = [rs, scaled] + [top * rs for top in tops]
+            return mod, ratio, row, (upper, lower, marks)
+
+        _, mods, marks = panel_step(solo, gw[pl.ds(at, PANEL), :], at)
+        update_rows(gw, old, mods)
+        lt[pl.ds(at, PANEL), :] = jnp.concatenate([m[0] for m in marks], axis=0)
+        lw[pl.ds(at, PANEL), :] = jnp.concatenate([m[1] for m in marks], axis=0)
+        for a in range(PANEL):
+            for i, x in enumerate(marks[a][2]):
+                if i < 2 or i - 2 >= a:
+                    spread[a, i : i + 1, :] = x
+
+    def jordan_panel(at):
+        old = [lane(vr[...], at + k) for k in range(PANEL)]
+        marks = [[spread[a, i : i + 1, :] for i in range(PANEL + 2)] for a in range(PANEL)]
+
+        def solo(a, here, row, tops):
+            rs, scaled = marks[a][:2]
+            row = row + scaled
+            q = 1.0 / (tops[a] + marks[a][2 + a])
+            norm = row * q
+            rq = rs * q
+            mod = jnp.where(here, 1.0 + rq, norm)
+            final = jnp.where(here, rq, norm)
+            ratio = [(tops[k] + marks[a][2 + k]) * q if k > a else None for k in range(PANEL)]
+            return mod, ratio, final, None
+
+        rows, mods, _ = panel_step(solo, vr[pl.ds(at, PANEL), :], at)
+        update_rows(vr, old, mods)
+        vr[pl.ds(at, PANEL), :] = rows
 
     def block(gram, top):
         gw[...] = gram
         vr[...] = top
-
-        def body(j, carry):
-            row, rs, scaled, vrow = carry
-            new = chol_step(j, row)
-            vrow = jordan_step(j - 1, vrow, rs, scaled)
-            return new + (vrow,)
-
-        carry = chol_step(0, gram[0:1]) + (top[0:1],)
-        row, rs, scaled, vrow = lax.fori_loop(1, H, body, carry)
-        jordan_step(H - 1, vrow, rs, scaled)
+        chol_panel(0)
+
+        def body(i, _):
+            at = pl.multiple_of(i * PANEL, PANEL)
+            jordan_panel(at - PANEL)
+            chol_panel(at)
+            return 0
+
+        lax.fori_loop(1, H // PANEL, body, 0)
+        jordan_panel(H - PANEL)
         return lt[...], lw[...], vr[...]
 
     g12, g22 = g[:H, H:], g[H:, H:]
@@ -102,7 +148,7 @@
         out_shape=[jax.ShapeDtypeStruct((W, W), jnp.float32)] * 2,
         in_specs=[vmem] * 2,
         out_specs=[vmem] * 2,
-        scratch_shapes=[pltpu.VMEM((H, H), jnp.float32)] * 4,
+        scratch_shapes=[pltpu.VMEM((H, H), jnp.float32)] * 4 + [pltpu.VMEM((PANEL, PANEL + 2, H), jnp.float32)],
         cost_estimate=pl.CostEstimate(flops=2 * W**3, bytes_accessed=16 * W * W, transcendentals=0),
     )(gram, top)
 
@@ -114,13 +160,6 @@
 
 def from_tiles(x, rows, cols):
     return x.reshape(rows // 8, cols // H, 8, H).transpose(0, 2, 1, 3).reshape(rows, cols)
-
-
-def sum_all(x, axes, parts):
-    pieces = x.reshape((parts, -1) + x.shape[1:])
-    mine = jnp.sum(lax.all_to_all(pieces, axes, 0, 0, tiled=True), axis=0)
-    full = lax.all_to_all(jnp.broadcast_to(mine[None], (parts,) + mine.shape), axes, 0, 0, tiled=True)
-    return full.reshape(x.shape)
 
 
 def split(x):
@@ -144,7 +183,7 @@
     return lax.dot_general(left, right, (contract, ((), ())), preferred_element_type=jnp.float32)
 
 
-def product_kernel(place_ref, a_ref, cols_ref, rows_ref, lt_ref, out_ref, inner_ref, acc):
+def product_kernel(place_ref, a_ref, cols_ref, rows_ref, lt_ref, out_ref, acc):
     step = pl.program_id(0)
     steps = pl.num_programs(0)
     lower = lt_ref[...].T
@@ -163,13 +202,17 @@
     @pl.when(step == steps - 1)
     def _():
         total = acc[...]
-        out_ref[...] = total
         own = (place_ref[0] == 0).astype(jnp.float32)
         inner = dots(rows_ref[:, :W] + own * lower, total[:W], NN)
-        inner_ref[...] = inner + dots(rows_ref[:, W:], total[W:], NN)
-
-
-def product(place, trailing, panel_cols, panel_rows, factor_t):
+        inner = inner + dots(rows_ref[:, W:], total[W:], NN)
+        parts = out_ref.shape[0]
+        part = total.shape[0] // parts
+        for q in range(parts):
+            out_ref[q, :part] = total[q * part : (q + 1) * part]
+            out_ref[q, part:] = inner[q * W // parts : (q + 1) * W // parts]
+
+
+def product(place, trailing, panel_cols, panel_rows, factor_t, parts):
     rows, cols = trailing.shape
     half = panel_cols.shape[2]
     tile = 640
@@ -177,7 +220,7 @@
     return pl.pallas_call(
         product_kernel,
         grid=(cols // tile,),
-        out_shape=[jax.ShapeDtypeStruct((rows, W), jnp.float32), jax.ShapeDtypeStruct((W, W), jnp.float32)],
+        out_shape=jax.ShapeDtypeStruct((parts, (rows + W) // parts, W), jnp.float32),
         in_specs=[
             pl.BlockSpec(memory_space=pltpu.SMEM),
             pl.BlockSpec((rows, tile), lambda i: (0, i)),
@@ -185,7 +228,7 @@
             pl.BlockSpec((W, rows), lambda i: (0, 0)),
             pl.BlockSpec((W, W), lambda i: (0, 0)),
         ],
-        out_specs=[pl.BlockSpec((rows, W), lambda i: (0, 0)), pl.BlockSpec((W, W), lambda i: (0, 0))],
+        out_specs=pl.BlockSpec((parts, (rows + W) // parts, W), lambda i: (0, 0, 0)),
         scratch_shapes=[pltpu.VMEM((rows, W), jnp.float32)],
         compiler_params=pltpu.CompilerParams(vmem_limit_bytes=VMEM_BYTES),
         cost_estimate=pl.CostEstimate(flops=6 * rows * cols * W, bytes_accessed=4 * rows * cols, transcendentals=0),
@@ -276,16 +319,18 @@
     part = rows // nc
     panel_t = panel_block.T
 
-    def gather_col(x):
-        line = lax.all_gather(x, "col", axis=0, axis_index_groups=lines)
+    def gather_line(x):
+        return lax.all_gather(x, "col", axis=0, axis_index_groups=lines)
+
+    def join_cores(line):
         other = lax.ppermute(line, "col", pair)
         even = c % 2 == 0
         both = jnp.stack([jnp.where(even, line, other), jnp.where(even, other, line)], axis=1)
-        return both.reshape((-1,) + x.shape[1:])
-
-    panel_rows = gather_col(panel_t)
-    panel_rows, later = lax.optimization_barrier((panel_rows, panel_t))
-    moved = lax.ppermute(later, BOTH, perm)
+        return both.reshape((-1,) + line.shape[2:])
+
+    moved = lax.ppermute(panel_t, BOTH, perm)
+    line, moved = lax.optimization_barrier((gather_line(panel_t), moved))
+    panel_rows = join_cores(line)
     panel_cols = lax.all_gather(moved, "row", axis=0, tiled=True).reshape(ratio, W, rows)
     strip = lax.dot_general(panel_t, panel_rows, (((1,), (1,)), ((), ())), precision=HIGHEST)
     top = jnp.where(r == 0, panel_t[:, :W], jnp.zeros((width, W), jnp.float32))
@@ -295,14 +340,18 @@
     tr, tc = width // 8, 2 * W // H
     full = full.reshape(tr, tc, nc, 8, H).transpose(2, 0, 3, 1, 4).reshape(W, 2 * W)
     factor_t, coupling_t = factor(full[:, :W], full[:, W:].T)
-    partial, inner = product(place, trailing, panel_cols, panel_rows, factor_t)
-    pieces = lax.all_to_all(partial.reshape(nc, part, W), "col", 0, 0, tiled=True)
-    mine = jnp.sum(pieces, axis=0)
+    partial = product(place, trailing, panel_cols, panel_rows, factor_t, nc)
+    pieces = jnp.sum(lax.all_to_all(partial, "col", 0, 0, tiled=True), axis=0)
+    mine, inner = pieces[:part], pieces[part:]
     mine = lax.dot_general(mine, coupling_t, (((1,), (1,)), ((), ())), precision=HIGHEST)
     moved = lax.ppermute(mine, BOTH, perm)
     weight_cols = lax.all_gather(moved, "row", axis=0, tiled=True)
-    weight_rows = gather_col(mine)
-    inner = from_tiles(sum_all(to_tiles(inner).reshape(nr * nc, 4, H), BOTH, nr * nc).reshape(-1, 8, H), W, W)
+    weight_rows = join_cores(gather_line(mine))
+    half = (nr, 8 * W * W // (8 * H * nr * nc), H)
+    inner = jnp.sum(lax.all_to_all(to_tiles(inner).reshape(half), "row", 0, 0, tiled=True), axis=0)
+    inner = jnp.broadcast_to(inner[None], (nr * nc,) + inner.shape)
+    inner = lax.all_to_all(inner, BOTH, 0, 0, tiled=True).reshape((nr, nc) + inner.shape[1:])
+    inner = from_tiles(inner.transpose(1, 0, 2, 3).reshape(-1, 8, H), W, W)
     left, right = prepare(place, panel_cols, panel_rows, weight_rows, factor_t, coupling_t, inner)
     return update(trailing, left, right, weight_cols)
 

time: 247 us -> 224 us (0.907)
  waiting for transfers between devices: 38.9 us -> 20 us
  blocking collectives: 93 us -> 107 us
  Pallas kernels: 67.2 us -> 53.5 us
  starting transfers between devices: 22.7 us -> 17.2 us
    all_to_all x2 -> x3, blocking collectives: 39.1 us -> 55.3 us  [the longest x1 24.3 us: shards(): pieces = jnp.sum(lax.all_to_all(partial, 'col', 0, 0, tiled=True), axis=0)]
    pallas_call x1, Pallas kernels: 33.3 us -> 19.6 us  [factor(): pl.pallas_call(factor_kernel, out_shape=[jax.ShapeDtypeStruct((W, W), jnp...]
    all_to_all x1 -> x0, waiting for transfers between devices: 13.1 us -> none  [sum_all(): lax.all_to_all(jnp.broadcast_to(mine[None], (parts,) + mine.shape), axes,...]
    all_to_all x1, blocking collectives: 21.5 us -> 10.9 us  [shards(): mine = jnp.sum(lax.all_to_all(pieces, 'row', 0, 0, tiled=True), axis=0)]
    all_gather x2, blocking collectives: 32.4 us -> 40.8 us  [gather_line(): return lax.all_gather(x, 'col', axis=0, axis_index_groups=lines)]
    ppermute x3, waiting for transfers between devices: 6.75 us -> 0.97 us  [the longest x2 0.96 us: join_cores(): other = lax.ppermute(line, 'col', pair)]
    all_to_all x1 -> x0, starting transfers between devices: 4.65 us -> none  [sum_all(): lax.all_to_all(jnp.broadcast_to(mine[None], (parts,) + mine.shape), axes,...]
  transfers between devices with their start and end apart: 8 -> 7, of which waited for: 5 -> 3; matrix products, arithmetic and copies ran while one was open for 2% -> 2% of each run, Pallas kernels for 16% -> 12%
where the time goes in v4:
time: 224 us; the launch traced here: 223 us
  blocking collectives  107 us (48%)
  Pallas kernels  53.5 us (24%)
  waiting for transfers between devices  20 us (9%)
  starting transfers between devices  17.2 us (8%)
  between operations  13.5 us (6%)
  local copies, waits for them, and re-layouts  9.23 us (4%)
    all_gather x2, blocking collectives, gather_line(): return lax.all_gather(x, 'col', axis=0, axis_index_groups=lines)  40.8 us
    all_to_all x1, blocking collectives, shards(): pieces = jnp.sum(lax.all_to_all(partial, 'col', 0, 0, tiled=True), axis=0)  24.3 us
    pallas_call x1, Pallas kernels, factor(): pl.pallas_call(factor_kernel, out_shape=[jax.ShapeDtypeStruct((W, W), jnp...  19.6 us
    all_to_all x1, blocking collectives, shards(): lax.all_to_all(inner, BOTH, 0, 0, tiled=True)  18.7 us
    pallas_call x1, Pallas kernels, update(): pl.pallas_call(update_kernel, grid=(cols // tile,), out_shape=jax.ShapeDt...  17.1 us
    all_to_all x1, waiting for transfers between devices, shards(): lax.all_to_all(jnp.broadcast_to(mine[None], (nr * nc,) + mine.shape), BOT...  13.4 us
    all_to_all x1, blocking collectives, shards(): lax.all_to_all(to_tiles(inner).reshape(half), 'row', 0, 0, tiled=True)  12.3 us
    all_to_all x1, blocking collectives, shards(): mine = jnp.sum(lax.all_to_all(pieces, 'row', 0, 0, tiled=True), axis=0)  10.9 us
  transfers between devices with their start and end apart: 7, of which 3 were waited for; matrix products, arithmetic and copies ran while one was open for 2% of the time, Pallas kernels for 12%

profile of v4, /device:TPU:1, one launch (start us, length us, event | category | flops | bytes accessed | tf_op | source)
XLA Modules:
  0.0 223.4 jit_solution(2271220115117948234)
XLA Ops:
  6.5 0.0 all-gather.5.cloned.1.call-start
  6.5 4.9 %collective-permute-start = (f32[32,1280]{1,0:T(8,128)}, f32[32,1280]{1,0:T(8,128)S(1)}, u32[]{:S(2)}, u32[]{:S(2)}) collective-permute-start(f32[32,1280]{1,0:T(8,128)} %bitcast.65), channel_id=1, source_target_pairs={{0,0},{1,8},{2,16},{3,24},{4,32},{5,40},{6,48},{7,56},{8,64},{9,72... | collective-permute-start | bytes 491528 | tf_op jit(solution)/shard_map/ppermute | solution.py:331
  11.5 21.6 %all-gather = f32[128,1280]{1,0:T(8,128)S(1)} all-gather(f32[32,1280]{1,0:T(8,128)} %bitcast.66), channel_id=2, replica_groups={{0,2,4,6},{1,3,5,7},{8,10,12,14},{9,11,13,15},{16,18,20,22},{17,19,21,2..., dimensions={0}, use_global_device_ids=true | all-gather | bytes 819200 | tf_op jit(solution)/shard_map/all_gather | solution.py:323
  33.1 0.0 collective-permute-done
  33.1 0.0 copy-start.5
  33.1 0.7 copy-done.5
  33.7 0.0 all-gather.5.cloned.1.call-update
  33.8 1.1 collective-permute-start.1
  34.9 0.8 slice_select_fusion
  35.6 1.0 collective-permute-done.1
  36.6 0.1 select_bitcast_fusion.3
  36.7 0.0 copy-start.4
  36.7 0.1 pad_maximum_fusion
  36.8 0.8 copy-done.4
  37.6 1.2 convolution_bitcast_fusion
  38.9 10.9 %all_to_all.25 = f32[16,8,128]{2,1,0:T(8,128)S(1)} all-to-all(f32[16,8,128]{2,1,0:T(8,128)S(1)} %bitcast.68), channel_id=1, replica_groups=mesh['row'=16,'col'=8] {'row'}, dimensions={0} | all-to-all | bytes 131072 | tf_op jit(solution)/shard_map/all_to_all | solution.py:338
  49.8 0.8 broadcast_in_dim.7
  50.6 5.8 %all-to-all-start.1 = ((f32[128,8,128]{2,1,0:T(8,128)}), f32[128,8,128]{2,1,0:T(8,128)S(1)}, u32[]{:S(2)}, u32[]{:S(2)}) async-start(f32[128,8,128]{2,1,0:T(8,128)} %broadcast_in_dim.7), calls=%async_computation.1 | async-start | bytes 1048576 | tf_op jit(solution)/shard_map/all_to_all | solution.py:339
  56.4 0.0 all-gather.7.cloned.1.call-start
  56.5 0.1 pad_add_fusion.place_ref
  56.5 13.4 %all-to-all-done.1 = f32[128,8,128]{2,1,0:T(8,128)S(1)} async-done(((f32[128,8,128]{2,1,0:T(8,128)}), f32[128,8,128]{2,1,0:T(8,128)S(1)}, u32[]{:S(2)}, u32[]{:S(2)}) %all-to-all-start.1) | async-done | bytes 524320 | tf_op jit(solution)/shard_map/all_to_all | solution.py:339
  69.9 0.1 copy.28
  70.0 0.7 fusion.2
  70.7 0.8 copy.35
  71.6 19.6 %shard_map.28 = (f32[256,256]{1,0:T(8,128)}, f32[256,256]{1,0:T(8,128)}) custom-call(f32[256,256]{1,0:T(8,128)} %get-tuple-element.22.gram_ref, f32[256,256]{1,0:T(8,128)} %bitcast.63), custom_call_target="tpu_custom_call" | custom-call | flops 33554432 | bytes 1048576 | tf_op jit(solution)/shard_map/pallas_call | solution.py:146
  91.2 0.9 copy-done
  92.1 10.2 %shard_map.29 = f32[8,192,256]{2,1,0:T(8,128)S(1)} custom-call(s32[2]{0:T(128)S(1)} %pad_add_fusion.place_ref, f32[1280,2560]{1,0:T(8,128)} %a_ref.3, f32[2,256,1280]{2,1,0:T(8,128)} %bitcast.55, f32[256,1280]{1,0:T(8,128)S(1)} %bitcast.51, f32[256,256]{1,0:T(8,128)S(1)} %copy-done), custom_call_target="tpu_custom_call" | custom-call | flops 5033164800 | bytes 13107200 | tf_op jit(solution)/shard_map/pallas_call | solution.py:220
  102.3 24.3 %all_to_all.26 = f32[8,192,256]{2,1,0:T(8,128)S(1)} all-to-all(f32[8,192,256]{2,1,0:T(8,128)S(1)} %shard_map.29), channel_id=1, replica_groups=mesh['row'=16,'col'=8] {'col'}, dimensions={0} | all-to-all | bytes 3145728 | tf_op jit(solution)/shard_map/all_to_all | solution.py:344
  126.7 0.1 reduce_sum.28
  126.8 0.8 copy-done.2
  127.6 0.4 fusion
  128.0 3.4 %collective-permute-start.3 = (f32[160,256]{1,0:T(8,128)S(1)}, f32[160,256]{1,0:T(8,128)S(1)}, u32[]{:S(2)}, u32[]{:S(2)}) collective-permute-start(f32[160,256]{1,0:T(8,128)S(1)} %fusion), channel_id=1, source_target_pairs={{0,0},{1,8},{2,16},{3,24},{4,32},{5,40},{6,48},{7,56},{8,64},{9,72... | collective-permute-start | bytes 491528 | tf_op jit(solution)/shard_map/ppermute | solution.py:347
  131.5 5.6 %collective-permute-done.3 = f32[160,256]{1,0:T(8,128)S(1)} collective-permute-done((f32[160,256]{1,0:T(8,128)S(1)}, f32[160,256]{1,0:T(8,128)S(1)}, u32[]{:S(2)}, u32[]{:S(2)}) %collective-permute-start.3) | collective-permute-done | bytes 163872 | tf_op jit(solution)/shard_map/ppermute | solution.py:347
  137.0 0.7 copy-done.6
  137.7 0.0 all-gather.7.cloned.1.call-update
  137.7 19.2 %all-gather.1 = f32[640,256]{1,0:T(8,128)S(1)} all-gather(f32[160,256]{1,0:T(8,128)S(1)} %fusion), channel_id=3, replica_groups={{0,2,4,6},{1,3,5,7},{8,10,12,14},{9,11,13,15},{16,18,20,22},{17,19,21,2..., dimensions={0}, use_global_device_ids=true | all-gather | bytes 819200 | tf_op jit(solution)/shard_map/all_gather | solution.py:323
  156.9 1.9 collective-permute-start.2
  158.8 12.3 %all_to_all.27 = f32[16,4,128]{2,1,0:T(4,128)S(1)} all-to-all(f32[16,4,128]{2,1,0:T(4,128)S(1)} %bitcast.69), channel_id=1, replica_groups=mesh['row'=16,'col'=8] {'row'}, dimensions={0} | all-to-all | bytes 65536 | tf_op jit(solution)/shard_map/all_to_all | solution.py:351
  171.2 18.7 %all_to_all.28 = f32[128,4,128]{2,1,0:T(4,128)S(1)} all-to-all(f32[128,4,128]{2,1,0:T(4,128)S(1)} %broadcast_in_dim.8), channel_id=1, replica_groups=mesh['row'=16,'col'=8] {'row','col'}, dimensions={0} | all-to-all | bytes 524288 | tf_op jit(solution)/shard_map/all_to_all | solution.py:353
  189.9 0.2 copy.33
  190.1 0.0 collective-permute-done.2
  190.1 0.1 select_bitcast_fusion.1
  190.2 0.0 copy-start.1
  190.2 0.1 pad_maximum_fusion.1
  190.3 0.8 copy-done.1
  191.1 6.6 %shard_map.30 = (bf16[1280,1536]{1,0:T(8,128)(2,1)}, bf16[768,2560]{1,0:T(8,128)(2,1)}) custom-call(s32[2]{0:T(128)S(1)} %pad_add_fusion.place_ref, f32[2,256,1280]{2,1,0:T(8,128)} %bitcast.56, f32[256,1280]{1,0:T(8,128)S(1)} %bitcast.52, f32[1280,256]{1,0:T(8,128)S(1)} %bitcast.53, f32[256,256]{1,0:T(8,128)S(1)} %copy-done.1, f32[256,256]{1,0:T(8,128)S(1)} %copy-done.2, ...), custom_call_target="tpu_custom_call" | custom-call | flops 503316480 | bytes 5242880 | tf_op jit(solution)/shard_map/pallas_call | solution.py:271
  197.8 1.7 copy-done.3
  199.5 17.1 %shard_map.31 = f32[1280,2560]{1,0:T(8,128)} custom-call(f32[1280,2560]{1,0:T(8,128)} %a_ref.3, bf16[1280,1536]{1,0:T(8,128)(2,1)} %get-tuple-element.15.left_ref, bf16[768,2560]{1,0:T(8,128)(2,1)} %get-tuple-element.16.right_ref, f32[2560,256]{1,0:T(8,128)S(1)} %copy-done.3), custom_call_target="tpu_custom_call" | custom-call | flops 10066329600 | bytes 26214400 | tf_op jit(solution)/shard_map/pallas_call | solution.py:292
  (12 shorter events, 0.1 us)
Async XLA Ops:
  6.5 84.6 %all-gather.5.cloned.1.call-start = ((), (), s32[]{:S(2)}) async-start(), calls=%async_computation.5 | async-start | bytes 2785280 | tf_op jit(solution)/shard_map/all_gather | solution.py:334
  6.5 26.5 %collective-permute-start = (f32[32,1280]{1,0:T(8,128)}, f32[32,1280]{1,0:T(8,128)S(1)}, u32[]{:S(2)}, u32[]{:S(2)}) collective-permute-start(f32[32,1280]{1,0:T(8,128)} %bitcast.65), channel_id=1, source_target_pairs={{0,0},{1,8},{2,16},{3,24},{4,32},{5,40},{6,48},{7,56},{8,64},{9,72... | collective-permute-start | bytes 491528 | tf_op jit(solution)/shard_map/ppermute | solution.py:331
  33.1 0.7 copy-start.5
  33.8 2.8 %collective-permute-start.1 = (f32[4,32,1280]{2,1,0:T(8,128)S(1)}, f32[4,32,1280]{2,1,0:T(8,128)S(1)}, u32[]{:S(2)}, u32[]{:S(2)}) collective-permute-start(f32[4,32,1280]{2,1,0:T(8,128)S(1)} %bitcast.57), channel_id=1, source_target_pairs={{0,1},{1,0},{2,3},{3,2},{4,5},{5,4},{6,7},{7,6},{8,9},{9,8},{10,11... | collective-permute-start | bytes 1966088 | tf_op jit(solution)/shard_map/ppermute | solution.py:326
  36.7 0.9 copy-start.4
  50.6 19.3 %all-to-all-start.1 = ((f32[128,8,128]{2,1,0:T(8,128)}), f32[128,8,128]{2,1,0:T(8,128)S(1)}, u32[]{:S(2)}, u32[]{:S(2)}) async-start(f32[128,8,128]{2,1,0:T(8,128)} %broadcast_in_dim.7), calls=%async_computation.1 | async-start | bytes 1048576 | tf_op jit(solution)/shard_map/all_to_all | solution.py:339
  56.4 141.3 %all-gather.7.cloned.1.call-start = ((), (), s32[]{:S(2)}) async-start(), calls=%async_computation.6 | async-start | bytes 2785280 | tf_op jit(solution)/shard_map/all_gather | solution.py:348
  91.2 1.0 copy-start
  126.7 1.0 copy-start.2
  128.0 9.0 %collective-permute-start.3 = (f32[160,256]{1,0:T(8,128)S(1)}, f32[160,256]{1,0:T(8,128)S(1)}, u32[]{:S(2)}, u32[]{:S(2)}) collective-permute-start(f32[160,256]{1,0:T(8,128)S(1)} %fusion), channel_id=1, source_target_pairs={{0,0},{1,8},{2,16},{3,24},{4,32},{5,40},{6,48},{7,56},{8,64},{9,72... | collective-permute-start | bytes 491528 | tf_op jit(solution)/shard_map/ppermute | solution.py:347
  137.0 0.7 copy-start.6
  156.9 33.2 %collective-permute-start.2 = (f32[4,160,256]{2,1,0:T(8,128)S(1)}, f32[4,160,256]{2,1,0:T(8,128)S(1)}, u32[]{:S(2)}, u32[]{:S(2)}) collective-permute-start(f32[4,160,256]{2,1,0:T(8,128)S(1)} %bitcast.59), channel_id=1, source_target_pairs={{0,1},{1,0},{2,3},{3,2},{4,5},{5,4},{6,7},{7,6},{8,9},{9,8},{10,11... | collective-permute-start | bytes 1966088 | tf_op jit(solution)/shard_map/ppermute | solution.py:326
  190.2 1.0 copy-start.1
  197.7 1.7 copy-start.3
Sparse Core Ops, SparseCore 0:
  33.9 45.6 all-gather.4
  137.9 53.9 all-gather.6

commit v5 on v4

--- a/solution.py
+++ b/solution.py
@@ -169,31 +169,27 @@
 
 NN = ((1,), (0,))
 NT = ((1,), (1,))
-VMEM_BYTES = 50 * 1024 * 1024
-
-
-def stack3(a, b, axis):
+VMEM_BYTES = 60 * 1024 * 1024
+
+
+def dots(a, b, contract):
     a_high, a_low = split(a)
     b_high, b_low = split(b)
-    return jnp.concatenate([a_high, a_high, a_low], axis=axis[0]), jnp.concatenate([b_high, b_low, b_high], axis=axis[1])
-
-
-def dots(a, b, contract):
-    left, right = stack3(a, b, (contract[0][0], contract[1][0]))
+    left = jnp.concatenate([a_high, a_high, a_low], axis=contract[0][0])
+    right = jnp.concatenate([b_high, b_low, b_high], axis=contract[1][0])
     return lax.dot_general(left, right, (contract, ((), ())), preferred_element_type=jnp.float32)
 
 
-def product_kernel(place_ref, a_ref, cols_ref, rows_ref, lt_ref, out_ref, acc):
+def product_kernel(place_ref, a_ref, cols_ref, rows_ref, lt_ref, keep_ref, send_ref, acc):
     step = pl.program_id(0)
     steps = pl.num_programs(0)
-    lower = lt_ref[...].T
 
     @pl.when(step == 0)
     def _():
         own = (place_ref[1] == 0).astype(jnp.float32)
-        first = cols_ref[0, :, :W] + own * lower
-        rest = cols_ref[0, :, W:]
-        acc[...] = dots(a_ref[:, :W], first, NT) + dots(a_ref[:, W:], rest, NT)
+        cols = cols_ref[0]
+        cols = jnp.concatenate([cols[:, :W] + own * lt_ref[...].T, cols[:, W:]], axis=1)
+        acc[...] = dots(a_ref[...], cols, NT)
 
     @pl.when(step > 0)
     def _():
@@ -201,15 +197,22 @@
 
     @pl.when(step == steps - 1)
     def _():
-        total = acc[...]
         own = (place_ref[0] == 0).astype(jnp.float32)
-        inner = dots(rows_ref[:, :W] + own * lower, total[:W], NN)
-        inner = inner + dots(rows_ref[:, W:], total[W:], NN)
-        parts = out_ref.shape[0]
-        part = total.shape[0] // parts
-        for q in range(parts):
-            out_ref[q, :part] = total[q * part : (q + 1) * part]
-            out_ref[q, part:] = inner[q * W // parts : (q + 1) * W // parts]
+        inner = dots(rows_ref[:, :W] + own * lt_ref[...].T, acc[:W], NN)
+        inner = inner + dots(rows_ref[:, W:], acc[W:], NN)
+        odd = place_ref[1] % 2 == 1
+        lines = keep_ref.shape[0]
+        part = acc.shape[0] // (2 * lines)
+        size = W // (2 * lines)
+        for q in range(lines):
+            for k in range(2):
+                i = 2 * q + k
+                for target, mine in ((keep_ref, odd == (k == 1)), (send_ref, odd != (k == 1))):
+
+                    @pl.when(mine)
+                    def _(target=target, i=i, q=q):
+                        target[q, :part] = acc[i * part : (i + 1) * part]
+                        target[q, part:] = inner[i * size : (i + 1) * size]
 
 
 def product(place, trailing, panel_cols, panel_rows, factor_t, parts):
@@ -217,10 +220,12 @@
     half = panel_cols.shape[2]
     tile = 640
     per = half // tile
+    out = jax.ShapeDtypeStruct((parts // 2, (rows + W) // parts, W), jnp.float32)
+    out_spec = pl.BlockSpec(out.shape, lambda i: (0, 0, 0))
     return pl.pallas_call(
         product_kernel,
         grid=(cols // tile,),
-        out_shape=jax.ShapeDtypeStruct((parts, (rows + W) // parts, W), jnp.float32),
+        out_shape=[out, out],
         in_specs=[
             pl.BlockSpec(memory_space=pltpu.SMEM),
             pl.BlockSpec((rows, tile), lambda i: (0, i)),
@@ -228,54 +233,63 @@
             pl.BlockSpec((W, rows), lambda i: (0, 0)),
             pl.BlockSpec((W, W), lambda i: (0, 0)),
         ],
-        out_specs=pl.BlockSpec((parts, (rows + W) // parts, W), lambda i: (0, 0, 0)),
+        out_specs=[out_spec, out_spec],
         scratch_shapes=[pltpu.VMEM((rows, W), jnp.float32)],
         compiler_params=pltpu.CompilerParams(vmem_limit_bytes=VMEM_BYTES),
         cost_estimate=pl.CostEstimate(flops=6 * rows * cols * W, bytes_accessed=4 * rows * cols, transcendentals=0),
     )(place, trailing, panel_cols, panel_rows, factor_t)
 
 
-def prepare_kernel(place_ref, cols_ref, rows_ref, wrows_ref, lt_ref, tt_ref, inner_ref, left_ref, right_ref):
-    t = tt_ref[...]
-    mid = jnp.dot(t, inner_ref[...], precision=HIGHEST, preferred_element_type=jnp.float32)
-    square = lax.dot_general(mid, t, (NT, ((), ())), precision=HIGHEST, preferred_element_type=jnp.float32)
-    own_rows = (place_ref[0] == 0).astype(jnp.float32)
-    own_cols = (place_ref[1] == 0).astype(jnp.float32)
-    lt = lt_ref[...]
-    for i in range(rows_ref.shape[1] // W):
-        at = slice(i * W, (i + 1) * W)
-        reflect = rows_ref[:, at].T
-        if i == 0:
-            reflect = reflect + lt * own_rows
-        weights = wrows_ref[at] - dots(reflect, square, NN)
-        for k, x in enumerate((reflect, weights)):
-            high, low = split(x)
-            for p, part in enumerate((high, high, low)):
-                left_ref[at, (3 * k + p) * W : (3 * k + p + 1) * W] = part
+def prepare_kernel(place_ref, cols_ref, rows_ref, own_ref, other_ref, lt_ref, tt_ref, inner_ref, out_ref, right_ref, reflect):
     half = cols_ref.shape[2]
     for h in range(cols_ref.shape[0]):
         for i in range(half // W):
             cols = cols_ref[h, :, i * W : (i + 1) * W]
             if h == 0 and i == 0:
-                cols = cols + lt.T * own_cols
+                cols = cols + lt_ref[...].T * (place_ref[1] == 0).astype(jnp.float32)
             high, low = split(cols)
             at = slice(h * half + i * W, h * half + (i + 1) * W)
             for p, part in enumerate((high, low, high)):
                 right_ref[p * W : (p + 1) * W, at] = part
-
-
-def prepare(place, panel_cols, panel_rows, weight_rows, factor_t, coupling_t, inner):
+    for i in range(rows_ref.shape[1] // W):
+        at = slice(i * W, (i + 1) * W)
+        rows = rows_ref[:, at].T
+        if i == 0:
+            rows = rows + lt_ref[...] * (place_ref[0] == 0).astype(jnp.float32)
+        high, low = split(rows)
+        both = jnp.concatenate([high, high, low], axis=1)
+        reflect[at] = both
+        out_ref[at, : 3 * W] = both
+    t = tt_ref[...]
+    mid = jnp.dot(t, inner_ref[...], precision=HIGHEST, preferred_element_type=jnp.float32)
+    square = lax.dot_general(mid, t, (NT, ((), ())), precision=HIGHEST, preferred_element_type=jnp.float32)
+    high, low = split(square)
+    right = jnp.concatenate([high, low, high], axis=0)
+    core = place_ref[1] % 2
+    line = place_ref[1] // 2
+    lines, part = own_ref.shape[:2]
+    for s in range(lines):
+        before = (line + lines - s) % lines
+        for ref, k in ((own_ref, core), (other_ref, 1 - core)):
+            at = pl.multiple_of((2 * before + k) * part, 16)
+            weights = ref[s] - jnp.dot(reflect[pl.ds(at, part)], right, preferred_element_type=jnp.float32)
+            high, low = split(weights)
+            out_ref[pl.ds(at, part), 3 * W :] = jnp.concatenate([high, high, low], axis=1)
+
+
+def prepare(place, panel_cols, panel_rows, own, other, factor_t, coupling_t, inner):
     rows = panel_rows.shape[1]
     cols = panel_cols.shape[0] * panel_cols.shape[2]
     vmem = pl.BlockSpec(memory_space=pltpu.VMEM)
     return pl.pallas_call(
         prepare_kernel,
         out_shape=[jax.ShapeDtypeStruct((rows, 6 * W), jnp.bfloat16), jax.ShapeDtypeStruct((3 * W, cols), jnp.bfloat16)],
-        in_specs=[pl.BlockSpec(memory_space=pltpu.SMEM)] + [vmem] * 6,
+        in_specs=[pl.BlockSpec(memory_space=pltpu.SMEM)] + [vmem] * 7,
         out_specs=[vmem] * 2,
+        scratch_shapes=[pltpu.VMEM((rows, 3 * W), jnp.bfloat16)],
         compiler_params=pltpu.CompilerParams(vmem_limit_bytes=VMEM_BYTES),
-        cost_estimate=pl.CostEstimate(flops=6 * rows * W * W, bytes_accessed=16 * rows * W, transcendentals=0),
-    )(place, panel_cols, panel_rows, weight_rows, factor_t, coupling_t, inner)
+        cost_estimate=pl.CostEstimate(flops=6 * rows * W * W, bytes_accessed=20 * rows * W, transcendentals=0),
+    )(place, panel_cols, panel_rows, own, other, factor_t, coupling_t, inner)
 
 
 def update_kernel(a_ref, left_ref, right_ref, weights_ref, out_ref):
@@ -318,19 +332,12 @@
     rows, width = panel_block.shape
     part = rows // nc
     panel_t = panel_block.T
-
-    def gather_line(x):
-        return lax.all_gather(x, "col", axis=0, axis_index_groups=lines)
-
-    def join_cores(line):
-        other = lax.ppermute(line, "col", pair)
-        even = c % 2 == 0
-        both = jnp.stack([jnp.where(even, line, other), jnp.where(even, other, line)], axis=1)
-        return both.reshape((-1,) + line.shape[2:])
-
     moved = lax.ppermute(panel_t, BOTH, perm)
-    line, moved = lax.optimization_barrier((gather_line(panel_t), moved))
-    panel_rows = join_cores(line)
+    line = lax.all_gather(panel_t, "col", axis=0, axis_index_groups=lines)
+    line, moved = lax.optimization_barrier((line, moved))
+    other = lax.ppermute(line, "col", pair)
+    even = c % 2 == 0
+    panel_rows = jnp.stack([jnp.where(even, line, other), jnp.where(even, other, line)], axis=1).reshape(W, rows)
     panel_cols = lax.all_gather(moved, "row", axis=0, tiled=True).reshape(ratio, W, rows)
     strip = lax.dot_general(panel_t, panel_rows, (((1,), (1,)), ((), ())), precision=HIGHEST)
     top = jnp.where(r == 0, panel_t[:, :W], jnp.zeros((width, W), jnp.float32))
@@ -340,19 +347,22 @@
     tr, tc = width // 8, 2 * W // H
     full = full.reshape(tr, tc, nc, 8, H).transpose(2, 0, 3, 1, 4).reshape(W, 2 * W)
     factor_t, coupling_t = factor(full[:, :W], full[:, W:].T)
-    partial = product(place, trailing, panel_cols, panel_rows, factor_t, nc)
-    pieces = jnp.sum(lax.all_to_all(partial, "col", 0, 0, tiled=True), axis=0)
+    keep, send = product(place, trailing, panel_cols, panel_rows, factor_t, nc)
+    pieces = keep + lax.ppermute(send, "col", pair)
+    pieces = jnp.sum(lax.all_to_all(pieces, "col", 0, 0, tiled=True, axis_index_groups=lines), axis=0)
     mine, inner = pieces[:part], pieces[part:]
     mine = lax.dot_general(mine, coupling_t, (((1,), (1,)), ((), ())), precision=HIGHEST)
     moved = lax.ppermute(mine, BOTH, perm)
     weight_cols = lax.all_gather(moved, "row", axis=0, tiled=True)
-    weight_rows = join_cores(gather_line(mine))
+    shifts = [[(j, (j + 2 * s) % nc) for j in range(nc)] for s in range(1, nc // 2)]
+    line = jnp.stack([mine] + [lax.ppermute(mine, "col", shift) for shift in shifts])
+    other = lax.ppermute(line, "col", pair)
     half = (nr, 8 * W * W // (8 * H * nr * nc), H)
     inner = jnp.sum(lax.all_to_all(to_tiles(inner).reshape(half), "row", 0, 0, tiled=True), axis=0)
     inner = jnp.broadcast_to(inner[None], (nr * nc,) + inner.shape)
     inner = lax.all_to_all(inner, BOTH, 0, 0, tiled=True).reshape((nr, nc) + inner.shape[1:])
     inner = from_tiles(inner.transpose(1, 0, 2, 3).reshape(-1, 8, H), W, W)
-    left, right = prepare(place, panel_cols, panel_rows, weight_rows, factor_t, coupling_t, inner)
+    left, right = prepare(place, panel_cols, panel_rows, line, other, factor_t, coupling_t, inner)
     return update(trailing, left, right, weight_cols)
 
 

time: 224 us -> 213 us (0.951)
  blocking collectives: 107 us -> 72.4 us
  waiting for transfers between devices: 20 us -> 31.1 us
  starting transfers between devices: 17.2 us -> 27.9 us
  Pallas kernels: 53.5 us -> 56.6 us
  local copies, waits for them, and re-layouts: 9.23 us -> 6.39 us
    all_gather x2 -> x1, blocking collectives: 40.8 us -> 21.6 us  [shards(): line = lax.all_gather(panel_t, 'col', axis=0, axis_index_groups=lines)]
    ppermute x2 -> x6, waiting for transfers between devices: 0.96 us -> 12.9 us  [the longest x3 9.82 us: shards(): lax.ppermute(mine, 'col', shift)]
    ppermute x2 -> x6, starting transfers between devices: 2.99 us -> 13.5 us  [the longest x3 10.4 us: shards(): lax.ppermute(mine, 'col', shift)]
    all_to_all x1, blocking collectives: 24.3 us -> 14.6 us  [shards(): lax.all_to_all(pieces, 'col', 0, 0, tiled=True, axis_index_groups=lines)]
    unnamed x15, local copies, waits for them, and re-layouts: 7.37 us -> 3.83 us
    all_to_all x1, blocking collectives: 12.3 us -> 9.19 us  [shards(): lax.all_to_all(to_tiles(inner).reshape(half), 'row', 0, 0, tiled=True)]
    all_to_all x1, blocking collectives: 18.7 us -> 16.1 us  [shards(): lax.all_to_all(inner, BOTH, 0, 0, tiled=True)]
  transfers between devices with their start and end apart: 7 -> 11, of which waited for: 3 -> 6; matrix products, arithmetic and copies ran while one was open for 2% -> 3% of each run, Pallas kernels for 12% -> 13%
where the time goes in v5:
time: 213 us; the launch traced here: 212 us
  blocking collectives  72.4 us (34%)
  Pallas kernels  56.6 us (27%)
  waiting for transfers between devices  31.1 us (15%)
  starting transfers between devices  27.9 us (13%)
  between operations  13.6 us (6%)
  local copies, waits for them, and re-layouts  6.39 us (3%)
  other arithmetic  2.98 us (1%)
    all_gather x1, blocking collectives, shards(): line = lax.all_gather(panel_t, 'col', axis=0, axis_index_groups=lines)  21.6 us
    pallas_call x1, Pallas kernels, factor(): pl.pallas_call(factor_kernel, out_shape=[jax.ShapeDtypeStruct((W, W), jnp...  19.6 us
    pallas_call x1, Pallas kernels, update(): pl.pallas_call(update_kernel, grid=(cols // tile,), out_shape=jax.ShapeDt...  17.8 us
    all_to_all x1, blocking collectives, shards(): lax.all_to_all(inner, BOTH, 0, 0, tiled=True)  16.1 us
    all_to_all x1, blocking collectives, shards(): lax.all_to_all(pieces, 'col', 0, 0, tiled=True, axis_index_groups=lines)  14.6 us
    all_to_all x1, waiting for transfers between devices, shards(): lax.all_to_all(jnp.broadcast_to(mine[None], (nr * nc,) + mine.shape), BOT...  12.8 us
    pallas_call x1, Pallas kernels, product(): pl.pallas_call(product_kernel, grid=(cols // tile,), out_shape=[out, out]...  11.6 us
    all_to_all x1, blocking collectives, shards(): mine = jnp.sum(lax.all_to_all(pieces, 'row', 0, 0, tiled=True), axis=0)  10.9 us
  transfers between devices with their start and end apart: 11, of which 6 were waited for; matrix products, arithmetic and copies ran while one was open for 3% of the time, Pallas kernels for 13%

profile of v5, /device:TPU:1, one launch (start us, length us, event | category | flops | bytes accessed | tf_op | source)
XLA Modules:
  0.0 212.5 jit_solution(1363863272864552820)
XLA Ops:
  6.5 4.9 %collective-permute-start = (f32[32,1280]{1,0:T(8,128)}, f32[32,1280]{1,0:T(8,128)S(1)}, u32[]{:S(2)}, u32[]{:S(2)}) collective-permute-start(f32[32,1280]{1,0:T(8,128)} %bitcast.58), channel_id=1, source_target_pairs={{0,0},{1,8},{2,16},{3,24},{4,32},{5,40},{6,48},{7,56},{8,64},{9,72... | collective-permute-start | bytes 491528 | tf_op jit(solution)/shard_map/ppermute | solution.py:335
  11.5 21.6 %all-gather = f32[128,1280]{1,0:T(8,128)S(1)} all-gather(f32[32,1280]{1,0:T(8,128)} %bitcast.59), channel_id=2, replica_groups={{0,2,4,6},{1,3,5,7},{8,10,12,14},{9,11,13,15},{16,18,20,22},{17,19,21,2..., dimensions={0}, use_global_device_ids=true | all-gather | bytes 819200 | tf_op jit(solution)/shard_map/all_gather | solution.py:336
  33.1 0.0 collective-permute-done
  33.1 0.7 copy-done.5
  33.8 0.0 all-gather.4.cloned.1.call-update
  33.8 1.1 collective-permute-start.1
  34.9 0.8 slice_select_fusion
  35.6 1.0 collective-permute-done.1
  36.6 0.1 select_bitcast_fusion.1
  36.7 0.0 copy-start.3
  36.7 0.1 pad_maximum_fusion
  36.8 0.0 copy-start
  36.8 0.8 copy-done.3
  37.6 1.2 convolution_bitcast_fusion
  38.9 10.9 %all_to_all.25 = f32[16,8,128]{2,1,0:T(8,128)S(1)} all-to-all(f32[16,8,128]{2,1,0:T(8,128)S(1)} %bitcast.62), channel_id=1, replica_groups=mesh['row'=16,'col'=8] {'row'}, dimensions={0} | all-to-all | bytes 131072 | tf_op jit(solution)/shard_map/all_to_all | solution.py:345
  49.8 0.8 broadcast_in_dim.7
  50.6 5.8 %all-to-all-start.1 = ((f32[128,8,128]{2,1,0:T(8,128)}), f32[128,8,128]{2,1,0:T(8,128)S(1)}, u32[]{:S(2)}, u32[]{:S(2)}) async-start(f32[128,8,128]{2,1,0:T(8,128)} %broadcast_in_dim.7), calls=%async_computation.1 | async-start | bytes 1048576 | tf_op jit(solution)/shard_map/all_to_all | solution.py:346
  56.4 0.0 all-gather.6.cloned.1.call-start
  56.5 0.7 pad_add_fusion.place_ref
  57.1 12.8 %all-to-all-done.1 = f32[128,8,128]{2,1,0:T(8,128)S(1)} async-done(((f32[128,8,128]{2,1,0:T(8,128)}), f32[128,8,128]{2,1,0:T(8,128)S(1)}, u32[]{:S(2)}, u32[]{:S(2)}) %all-to-all-start.1) | async-done | bytes 524320 | tf_op jit(solution)/shard_map/all_to_all | solution.py:346
  70.0 0.1 copy.23
  70.0 0.7 fusion.2
  70.8 0.8 copy.29
  71.6 19.6 %shard_map.28 = (f32[256,256]{1,0:T(8,128)}, f32[256,256]{1,0:T(8,128)}) custom-call(f32[256,256]{1,0:T(8,128)} %get-tuple-element.24.gram_ref, f32[256,256]{1,0:T(8,128)} %bitcast.56), custom_call_target="tpu_custom_call" | custom-call | flops 33554432 | bytes 1048576 | tf_op jit(solution)/shard_map/pallas_call | solution.py:146
  91.2 11.6 %shard_map.29 = (f32[4,192,256]{2,1,0:T(8,128)}, f32[4,192,256]{2,1,0:T(8,128)}) custom-call(s32[2]{0:T(128)} %pad_add_fusion.place_ref, f32[1280,2560]{1,0:T(8,128)} %a_ref.3, f32[2,256,1280]{2,1,0:T(8,128)} %bitcast.49, f32[256,1280]{1,0:T(8,128)} %bitcast.47, f32[256,256]{1,0:T(8,128)} %get-tuple-element.15.lt_ref), custom_call_target="tpu_custom_call" | custom-call | flops 5033164800 | bytes 13107200 | tf_op jit(solution)/shard_map/pallas_call | solution.py:225
  102.7 1.1 collective-permute-start.2
  103.8 2.1 collective-permute-done.2
  106.0 1.2 add.8
  107.2 14.6 %all_to_all.26 = f32[4,192,256]{2,1,0:T(8,128)S(1)} all-to-all(f32[4,192,256]{2,1,0:T(8,128)S(1)} %add.8), channel_id=1, replica_groups={{0,2,4,6},{1,3,5,7},{8,10,12,14},{9,11,13,15},{16,18,20,22},{17,19,21,2..., dimensions={0} | all-to-all | bytes 1572864 | tf_op jit(solution)/shard_map/all_to_all | solution.py:352
  121.8 0.1 reduce_sum.28
  121.9 0.4 fusion
  122.3 3.6 %collective-permute-start.7 = (f32[160,256]{1,0:T(8,128)S(1)}, f32[160,256]{1,0:T(8,128)S(1)}, u32[]{:S(2)}, u32[]{:S(2)}) collective-permute-start(f32[160,256]{1,0:T(8,128)S(1)} %fusion), channel_id=1, source_target_pairs={{0,0},{1,8},{2,16},{3,24},{4,32},{5,40},{6,48},{7,56},{8,64},{9,72... | collective-permute-start | bytes 491528 | tf_op jit(solution)/shard_map/ppermute | solution.py:355
  125.9 5.3 %collective-permute-done.7 = f32[160,256]{1,0:T(8,128)S(1)} collective-permute-done((f32[160,256]{1,0:T(8,128)S(1)}, f32[160,256]{1,0:T(8,128)S(1)}, u32[]{:S(2)}, u32[]{:S(2)}) %collective-permute-start.7) | collective-permute-done | bytes 163872 | tf_op jit(solution)/shard_map/ppermute | solution.py:355
  131.2 0.7 copy-done.6
  131.8 0.0 all-gather.6.cloned.1.call-update
  131.9 9.7 %collective-permute-start.5 = (f32[160,256]{1,0:T(8,128)S(1)}, f32[160,256]{1,0:T(8,128)S(1)}, u32[]{:S(2)}, u32[]{:S(2)}) collective-permute-start(f32[160,256]{1,0:T(8,128)S(1)} %fusion), channel_id=1, source_target_pairs={{0,6},{1,7},{2,0},{3,1},{4,2},{5,3},{6,4},{7,5},{8,14},{9,15},{10,... | collective-permute-start | bytes 491528 | tf_op jit(solution)/shard_map/ppermute | solution.py:358
  141.6 0.0 collective-permute-start.4
  141.6 0.7 collective-permute-start.3
  142.2 6.3 %collective-permute-done.5 = f32[160,256]{1,0:T(8,128)S(1)} collective-permute-done((f32[160,256]{1,0:T(8,128)S(1)}, f32[160,256]{1,0:T(8,128)S(1)}, u32[]{:S(2)}, u32[]{:S(2)}) %collective-permute-start.5) | collective-permute-done | bytes 163872 | tf_op jit(solution)/shard_map/ppermute | solution.py:358
  148.5 0.0 collective-permute-done.4
  148.6 3.5 %collective-permute-done.3 = f32[160,256]{1,0:T(8,128)S(1)} collective-permute-done((f32[160,256]{1,0:T(8,128)S(1)}, f32[160,256]{1,0:T(8,128)S(1)}, u32[]{:S(2)}, u32[]{:S(2)}) %collective-permute-start.3) | collective-permute-done | bytes 163872 | tf_op jit(solution)/shard_map/ppermute | solution.py:358
  152.1 0.9 collective-permute-start.6
  153.1 9.2 %all_to_all.27 = f32[16,4,128]{2,1,0:T(4,128)S(1)} all-to-all(f32[16,4,128]{2,1,0:T(4,128)S(1)} %bitcast.66), channel_id=1, replica_groups=mesh['row'=16,'col'=8] {'row'}, dimensions={0} | all-to-all | bytes 65536 | tf_op jit(solution)/shard_map/all_to_all | solution.py:361
  162.3 16.1 %all_to_all.28 = f32[128,4,128]{2,1,0:T(4,128)S(1)} all-to-all(f32[128,4,128]{2,1,0:T(4,128)S(1)} %broadcast_in_dim.8), channel_id=1, replica_groups=mesh['row'=16,'col'=8] {'row','col'}, dimensions={0} | all-to-all | bytes 524288 | tf_op jit(solution)/shard_map/all_to_all | solution.py:363
  178.5 0.9 copy.27
  179.3 0.8 copy-done.4
  180.2 7.6 %shard_map.30 = (bf16[1280,1536]{1,0:T(8,128)(2,1)}, bf16[768,2560]{1,0:T(8,128)(2,1)}) custom-call(s32[2]{0:T(128)} %pad_add_fusion.place_ref, f32[2,256,1280]{2,1,0:T(8,128)} %bitcast.50, f32[256,1280]{1,0:T(8,128)} %bitcast.48, f32[4,160,256]{2,1,0:T(8,128)} %copy-done.1, f32[4,160,256]{2,1,0:T(8,128)} %copy-done.4, f32[256,256]{1,0:T(8,128)} %get-tuple-element.15.lt_ref, ...), custom_call_target="tpu_custom_call" | custom-call | flops 503316480 | bytes 6553600 | tf_op jit(solution)/shard_map/pallas_call | solution.py:284
  187.8 17.8 %shard_map.31 = f32[1280,2560]{1,0:T(8,128)} custom-call(f32[1280,2560]{1,0:T(8,128)} %a_ref.3, bf16[1280,1536]{1,0:T(8,128)(2,1)} %get-tuple-element.19.left_ref, bf16[768,2560]{1,0:T(8,128)(2,1)} %get-tuple-element.20.right_ref, f32[2560,256]{1,0:T(8,128)} %all-gather.6.cloned.1.call-done.weights_ref), custom_call_target="tpu_custom_call" | custom-call | flops 10066329600 | bytes 26214400 | tf_op jit(solution)/shard_map/pallas_call | solution.py:306
  (19 shorter events, 0.2 us)
Async XLA Ops:
  6.5 84.6 %all-gather.4.cloned.1.call-start = ((), (), s32[]{:S(2)}) async-start(), calls=%async_computation.5 | async-start | bytes 2785280 | tf_op jit(solution)/shard_map/all_gather | solution.py:341
  6.5 26.5 %collective-permute-start = (f32[32,1280]{1,0:T(8,128)}, f32[32,1280]{1,0:T(8,128)S(1)}, u32[]{:S(2)}, u32[]{:S(2)}) collective-permute-start(f32[32,1280]{1,0:T(8,128)} %bitcast.58), channel_id=1, source_target_pairs={{0,0},{1,8},{2,16},{3,24},{4,32},{5,40},{6,48},{7,56},{8,64},{9,72... | collective-permute-start | bytes 491528 | tf_op jit(solution)/shard_map/ppermute | solution.py:335
  33.1 0.7 copy-start.5
  33.8 2.8 %collective-permute-start.1 = (f32[4,32,1280]{2,1,0:T(8,128)S(1)}, f32[4,32,1280]{2,1,0:T(8,128)S(1)}, u32[]{:S(2)}, u32[]{:S(2)}) collective-permute-start(f32[4,32,1280]{2,1,0:T(8,128)S(1)} %bitcast.51), channel_id=1, source_target_pairs={{0,1},{1,0},{2,3},{3,2},{4,5},{5,4},{6,7},{7,6},{8,9},{9,8},{10,11... | collective-permute-start | bytes 1966088 | tf_op jit(solution)/shard_map/ppermute | solution.py:338
  36.7 0.9 copy-start.3
  36.8 13.8 %copy-start = (f32[4,2,32,1280]{3,2,1,0:T(8,128)}, f32[4,2,32,1280]{3,2,1,0:T(8,128)S(1)}, u32[]{:S(2)}) copy-start(f32[4,2,32,1280]{3,2,1,0:T(8,128)S(1)} %pad_maximum_fusion) | copy-start | bytes 3932164
  50.6 19.3 %all-to-all-start.1 = ((f32[128,8,128]{2,1,0:T(8,128)}), f32[128,8,128]{2,1,0:T(8,128)S(1)}, u32[]{:S(2)}, u32[]{:S(2)}) async-start(f32[128,8,128]{2,1,0:T(8,128)} %broadcast_in_dim.7), calls=%async_computation.1 | async-start | bytes 1048576 | tf_op jit(solution)/shard_map/all_to_all | solution.py:346
  56.4 131.4 %all-gather.6.cloned.1.call-start = ((), (), s32[]{:S(2)}) async-start(), calls=%async_computation.6 | async-start | bytes 2785280 | tf_op jit(solution)/shard_map/all_gather | solution.py:356
  102.7 3.2 %collective-permute-start.2 = (f32[4,192,256]{2,1,0:T(8,128)}, f32[4,192,256]{2,1,0:T(8,128)S(1)}, u32[]{:S(2)}, u32[]{:S(2)}) collective-permute-start(f32[4,192,256]{2,1,0:T(8,128)} %get-tuple-element.17), channel_id=1, source_target_pairs={{0,1},{1,0},{2,3},{3,2},{4,5},{5,4},{6,7},{7,6},{8,9},{9,8},{10,11... | collective-permute-start | bytes 2359304 | tf_op jit(solution)/shard_map/ppermute | solution.py:351
  107.2 14.6 %copy-start.2 = (f32[256,256]{1,0:T(8,128)S(1)}, f32[256,256]{1,0:T(8,128)}, u32[]{:S(2)}) copy-start(f32[256,256]{1,0:T(8,128)} %get-tuple-element.18.tt_ref) | copy-start | bytes 786436
  122.3 8.9 %collective-permute-start.7 = (f32[160,256]{1,0:T(8,128)S(1)}, f32[160,256]{1,0:T(8,128)S(1)}, u32[]{:S(2)}, u32[]{:S(2)}) collective-permute-start(f32[160,256]{1,0:T(8,128)S(1)} %fusion), channel_id=1, source_target_pairs={{0,0},{1,8},{2,16},{3,24},{4,32},{5,40},{6,48},{7,56},{8,64},{9,72... | collective-permute-start | bytes 491528 | tf_op jit(solution)/shard_map/ppermute | solution.py:355
  131.2 0.7 copy-start.6
  131.9 16.7 %collective-permute-start.5 = (f32[160,256]{1,0:T(8,128)S(1)}, f32[160,256]{1,0:T(8,128)S(1)}, u32[]{:S(2)}, u32[]{:S(2)}) collective-permute-start(f32[160,256]{1,0:T(8,128)S(1)} %fusion), channel_id=1, source_target_pairs={{0,6},{1,7},{2,0},{3,1},{4,2},{5,3},{6,4},{7,5},{8,14},{9,15},{10,... | collective-permute-start | bytes 491528 | tf_op jit(solution)/shard_map/ppermute | solution.py:358
  141.6 7.0 %collective-permute-start.4 = (f32[160,256]{1,0:T(8,128)S(1)}, f32[160,256]{1,0:T(8,128)S(1)}, u32[]{:S(2)}, u32[]{:S(2)}) collective-permute-start(f32[160,256]{1,0:T(8,128)S(1)} %fusion), channel_id=1, source_target_pairs={{0,4},{1,5},{2,6},{3,7},{4,0},{5,1},{6,2},{7,3},{8,12},{9,13},{10,... | collective-permute-start | bytes 491528 | tf_op jit(solution)/shard_map/ppermute | solution.py:358
  141.6 10.5 %collective-permute-start.3 = (f32[160,256]{1,0:T(8,128)S(1)}, f32[160,256]{1,0:T(8,128)S(1)}, u32[]{:S(2)}, u32[]{:S(2)}) collective-permute-start(f32[160,256]{1,0:T(8,128)S(1)} %fusion), channel_id=1, source_target_pairs={{0,2},{1,3},{2,4},{3,5},{4,6},{5,7},{6,0},{7,1},{8,10},{9,11},{10,... | collective-permute-start | bytes 491528 | tf_op jit(solution)/shard_map/ppermute | solution.py:358
  152.1 27.2 %copy-start.1 = (f32[4,160,256]{2,1,0:T(8,128)}, f32[4,160,256]{2,1,0:T(8,128)S(1)}, u32[]{:S(2)}) copy-start(f32[4,160,256]{2,1,0:T(8,128)S(1)} %pad_maximum_fusion.1.own_ref) | copy-start | bytes 1966084
  152.1 27.2 %collective-permute-start.6 = (f32[4,160,256]{2,1,0:T(8,128)S(1)}, f32[4,160,256]{2,1,0:T(8,128)S(1)}, u32[]{:S(2)}, u32[]{:S(2)}) collective-permute-start(f32[4,160,256]{2,1,0:T(8,128)S(1)} %pad_maximum_fusion.1.own_ref), channel_id=1, source_target_pairs={{0,1},{1,0},{2,3},{3,2},{4,5},{5,4},{6,7},{7,6},{8,9},{9,8},{10,11... | collective-permute-start | bytes 1966088 | tf_op jit(solution)/shard_map/ppermute | solution.py:359
  179.3 0.8 copy-start.4
Sparse Core Ops, SparseCore 0:
  33.9 45.6 all-gather.3
  132.0 54.1 all-gather.5

commit v6 on v5

--- a/solution.py
+++ b/solution.py
@@ -158,10 +158,6 @@
     return x.reshape(rows // 8, 8, cols // H, H).transpose(0, 2, 1, 3).reshape(rows * cols // (8 * H), 8, H)
 
 
-def from_tiles(x, rows, cols):
-    return x.reshape(rows // 8, cols // H, 8, H).transpose(0, 2, 1, 3).reshape(rows, cols)
-
-
 def split(x):
     high = x.astype(jnp.bfloat16)
     return high, (x - high.astype(jnp.float32)).astype(jnp.bfloat16)
@@ -180,7 +176,7 @@
     return lax.dot_general(left, right, (contract, ((), ())), preferred_element_type=jnp.float32)
 
 
-def product_kernel(place_ref, a_ref, cols_ref, rows_ref, lt_ref, keep_ref, send_ref, acc):
+def product_kernel(place_ref, a_ref, cols_ref, rows_ref, lt_ref, keep_ref, send_ref, acc, inner_scr):
     step = pl.program_id(0)
     steps = pl.num_programs(0)
 
@@ -200,19 +196,17 @@
         own = (place_ref[0] == 0).astype(jnp.float32)
         inner = dots(rows_ref[:, :W] + own * lt_ref[...].T, acc[:W], NN)
         inner = inner + dots(rows_ref[:, W:], acc[W:], NN)
-        odd = place_ref[1] % 2 == 1
+        inner_scr[...] = inner
         lines = keep_ref.shape[0]
         part = acc.shape[0] // (2 * lines)
         size = W // (2 * lines)
+        line = place_ref[1] // 2
+        core = place_ref[1] % 2
         for q in range(lines):
-            for k in range(2):
-                i = 2 * q + k
-                for target, mine in ((keep_ref, odd == (k == 1)), (send_ref, odd != (k == 1))):
-
-                    @pl.when(mine)
-                    def _(target=target, i=i, q=q):
-                        target[q, :part] = acc[i * part : (i + 1) * part]
-                        target[q, part:] = inner[i * size : (i + 1) * size]
+            for target, k in ((keep_ref, core), (send_ref, 1 - core)):
+                i = 2 * ((line + q) % lines) + k
+                target[q, :part] = acc[pl.ds(pl.multiple_of(i * part, 8), part)]
+                target[q, part:] = inner_scr[pl.ds(pl.multiple_of(i * size, 8), size)]
 
 
 def product(place, trailing, panel_cols, panel_rows, factor_t, parts):
@@ -234,7 +228,7 @@
             pl.BlockSpec((W, W), lambda i: (0, 0)),
         ],
         out_specs=[out_spec, out_spec],
-        scratch_shapes=[pltpu.VMEM((rows, W), jnp.float32)],
+        scratch_shapes=[pltpu.VMEM((rows, W), jnp.float32), pltpu.VMEM((W, W), jnp.float32)],
         compiler_params=pltpu.CompilerParams(vmem_limit_bytes=VMEM_BYTES),
         cost_estimate=pl.CostEstimate(flops=6 * rows * cols * W, bytes_accessed=4 * rows * cols, transcendentals=0),
     )(place, trailing, panel_cols, panel_rows, factor_t)
@@ -325,7 +319,14 @@
     nr = lax.axis_size("row")
     nc = lax.axis_size("col")
     ratio = nr // nc
-    perm = [(i * nc + j, ((i % ratio) * nc + j) * nc + i // ratio) for i in range(nr) for j in range(nc)]
+
+    def home(i, j):
+        return ((i % ratio) * nc + j) * nc + i // ratio
+
+    def after(j, s):
+        return (j + 2 * s) % nc
+
+    perm = [(i * nc + j, home(i, j)) for i in range(nr) for j in range(nc)]
     pair = [(j, j ^ 1) for j in range(nc)]
     lines = [list(range(k, nc, 2)) for k in range(2)]
     place = jnp.stack([r, c]).astype(jnp.int32)
@@ -349,19 +350,20 @@
     factor_t, coupling_t = factor(full[:, :W], full[:, W:].T)
     keep, send = product(place, trailing, panel_cols, panel_rows, factor_t, nc)
     pieces = keep + lax.ppermute(send, "col", pair)
-    pieces = jnp.sum(lax.all_to_all(pieces, "col", 0, 0, tiled=True, axis_index_groups=lines), axis=0)
+    out = [[(i * nc + j, home(i, after(j, s))) for i in range(nr) for j in range(nc)] for s in range(nc // 2)]
+    back = [[(home(i, j), i * nc + after(j, s)) for i in range(nr) for j in range(nc)] for s in range(nc // 2)]
+    pieces = sum(lax.ppermute(pieces[s], BOTH, out[s]) for s in range(nc // 2))
     mine, inner = pieces[:part], pieces[part:]
     mine = lax.dot_general(mine, coupling_t, (((1,), (1,)), ((), ())), precision=HIGHEST)
-    moved = lax.ppermute(mine, BOTH, perm)
-    weight_cols = lax.all_gather(moved, "row", axis=0, tiled=True)
-    shifts = [[(j, (j + 2 * s) % nc) for j in range(nc)] for s in range(1, nc // 2)]
-    line = jnp.stack([mine] + [lax.ppermute(mine, "col", shift) for shift in shifts])
+    weight_cols = lax.all_gather(mine, "row", axis=0, tiled=True)
+    line = jnp.stack([lax.ppermute(mine, BOTH, back[s]) for s in range(nc // 2)])
     other = lax.ppermute(line, "col", pair)
-    half = (nr, 8 * W * W // (8 * H * nr * nc), H)
-    inner = jnp.sum(lax.all_to_all(to_tiles(inner).reshape(half), "row", 0, 0, tiled=True), axis=0)
-    inner = jnp.broadcast_to(inner[None], (nr * nc,) + inner.shape)
-    inner = lax.all_to_all(inner, BOTH, 0, 0, tiled=True).reshape((nr, nc) + inner.shape[1:])
-    inner = from_tiles(inner.transpose(1, 0, 2, 3).reshape(-1, 8, H), W, W)
+    groups = [[home(i, j) for i in range(nr)] for j in range(nc)]
+    inner = jnp.broadcast_to(inner[None], (nr,) + inner.shape)
+    inner = jnp.sum(lax.all_to_all(inner, BOTH, 0, 0, tiled=True, axis_index_groups=groups), axis=0)
+    inner = jnp.broadcast_to(inner[None], (nc,) + inner.shape)
+    strips = [list(range(h * nc, (h + 1) * nc)) for h in range(ratio)]
+    inner = lax.all_to_all(inner, "row", 0, 0, tiled=True, axis_index_groups=strips).reshape(W, W)
     left, right = prepare(place, panel_cols, panel_rows, line, other, factor_t, coupling_t, inner)
     return update(trailing, left, right, weight_cols)
 

time: 213 us -> 226 us (1.061)
  starting transfers between devices: 27.9 us -> 54.6 us
  blocking collectives: 72.4 us -> 54.5 us
  waiting for transfers between devices: 31.1 us -> 34.6 us
    ppermute x4 -> x8, starting transfers between devices: 13.9 us -> 31.9 us  [the longest x4 16 us: shards(): lax.ppermute(pieces[s], BOTH, out[s])]
    all_to_all x3 -> x1, blocking collectives: 39.9 us -> 22 us  [shards(): lax.all_to_all(inner, 'row', 0, 0, tiled=True, axis_index_groups=strips)]
    all_to_all x0 -> x1, starting transfers between devices: none -> 9.37 us  [shards(): lax.all_to_all(inner, BOTH, 0, 0, tiled=True, axis_index_groups=groups)]
    all_to_all x0 -> x1, waiting for transfers between devices: none -> 3.9 us  [shards(): lax.all_to_all(inner, BOTH, 0, 0, tiled=True, axis_index_groups=groups)]
    ppermute x4 -> x8, waiting for transfers between devices: 15.1 us -> 14.8 us  [the longest x4 8.59 us: shards(): lax.ppermute(pieces[s], BOTH, out[s])]
  transfers between devices with their start and end apart: 11 -> 16, of which waited for: 6 -> 7; matrix products, arithmetic and copies ran while one was open for 3% -> 3% of each run, Pallas kernels for 13% -> 12%
where the time goes in v6:
time: 226 us; the launch traced here: 225 us
  Pallas kernels  56.4 us (25%)
  starting transfers between devices  54.6 us (24%)
  blocking collectives  54.5 us (24%)
  waiting for transfers between devices  34.6 us (15%)
  between operations  13.6 us (6%)
  local copies, waits for them, and re-layouts  5.72 us (3%)
  other arithmetic  3.01 us (1%)
  matrix products  2.31 us (1%)
    all_to_all x1, blocking collectives, shards(): lax.all_to_all(inner, 'row', 0, 0, tiled=True, axis_index_groups=strips)  22 us
    all_gather x1, blocking collectives, shards(): line = lax.all_gather(panel_t, 'col', axis=0, axis_index_groups=lines)  21.6 us
    pallas_call x1, Pallas kernels, factor(): pl.pallas_call(factor_kernel, out_shape=[jax.ShapeDtypeStruct((W, W), jnp...  19.6 us
    pallas_call x1, Pallas kernels, update(): pl.pallas_call(update_kernel, grid=(cols // tile,), out_shape=jax.ShapeDt...  17.8 us
    ppermute x4, starting transfers between devices, shards(): lax.ppermute(pieces[s], BOTH, out[s])  16 us
    ppermute x4, starting transfers between devices, shards(): lax.ppermute(mine, BOTH, back[s])  15.9 us
    all_to_all x1, waiting for transfers between devices, shards(): lax.all_to_all(jnp.broadcast_to(mine[None], (nr * nc,) + mine.shape), BOT...  12.8 us
    pallas_call x1, Pallas kernels, product(): pl.pallas_call(product_kernel, grid=(cols // tile,), out_shape=[out, out]...  11.5 us
  transfers between devices with their start and end apart: 16, of which 7 were waited for; matrix products, arithmetic and copies ran while one was open for 3% of the time, Pallas kernels for 12%

profile of v6, /device:TPU:1, one launch (start us, length us, event | category | flops | bytes accessed | tf_op | source)
XLA Modules:
  0.0 224.8 jit_solution(11713687731368993742)
XLA Ops:
  6.5 4.9 %collective-permute-start = (f32[32,1280]{1,0:T(8,128)}, f32[32,1280]{1,0:T(8,128)S(1)}, u32[]{:S(2)}, u32[]{:S(2)}) collective-permute-start(f32[32,1280]{1,0:T(8,128)} %bitcast.51), channel_id=1, source_target_pairs={{0,0},{1,8},{2,16},{3,24},{4,32},{5,40},{6,48},{7,56},{8,64},{9,72... | collective-permute-start | bytes 491528 | tf_op jit(solution)/shard_map/ppermute | solution.py:336
  11.5 21.6 %all-gather = f32[128,1280]{1,0:T(8,128)S(1)} all-gather(f32[32,1280]{1,0:T(8,128)} %bitcast.52), channel_id=2, replica_groups={{0,2,4,6},{1,3,5,7},{8,10,12,14},{9,11,13,15},{16,18,20,22},{17,19,21,2..., dimensions={0}, use_global_device_ids=true | all-gather | bytes 819200 | tf_op jit(solution)/shard_map/all_gather | solution.py:337
  33.1 0.7 copy-done.5
  33.7 0.0 all-gather.4.cloned.1.call-update
  33.8 1.1 collective-permute-start.1
  34.9 0.8 slice_select_fusion
  35.6 1.0 collective-permute-done.1
  36.6 0.1 select_bitcast_fusion.1
  36.7 0.1 pad_maximum_fusion
  36.8 0.8 copy-done.3
  37.6 1.2 convolution_bitcast_fusion
  38.9 10.9 %all_to_all.20 = f32[16,8,128]{2,1,0:T(8,128)S(1)} all-to-all(f32[16,8,128]{2,1,0:T(8,128)S(1)} %bitcast.54), channel_id=1, replica_groups=mesh['row'=16,'col'=8] {'row'}, dimensions={0} | all-to-all | bytes 131072 | tf_op jit(solution)/shard_map/all_to_all | solution.py:346
  49.8 0.8 broadcast_in_dim.9
  50.6 5.8 %all-to-all-start.1 = ((f32[128,8,128]{2,1,0:T(8,128)}), f32[128,8,128]{2,1,0:T(8,128)S(1)}, u32[]{:S(2)}, u32[]{:S(2)}) async-start(f32[128,8,128]{2,1,0:T(8,128)} %broadcast_in_dim.9), calls=%async_computation.1 | async-start | bytes 1048576 | tf_op jit(solution)/shard_map/all_to_all | solution.py:347
  56.4 0.0 all-gather.6.cloned.1.call-start
  56.5 0.7 pad_add_fusion.place_ref
  57.1 12.8 %all-to-all-done.1 = f32[128,8,128]{2,1,0:T(8,128)S(1)} async-done(((f32[128,8,128]{2,1,0:T(8,128)}), f32[128,8,128]{2,1,0:T(8,128)S(1)}, u32[]{:S(2)}, u32[]{:S(2)}) %all-to-all-start.1) | async-done | bytes 524320 | tf_op jit(solution)/shard_map/all_to_all | solution.py:347
  70.0 0.1 copy.9
  70.0 0.7 fusion.2
  70.8 0.8 copy.11
  71.6 19.6 %shard_map.28 = (f32[256,256]{1,0:T(8,128)}, f32[256,256]{1,0:T(8,128)}) custom-call(f32[256,256]{1,0:T(8,128)} %get-tuple-element.28.gram_ref, f32[256,256]{1,0:T(8,128)} %bitcast.50), custom_call_target="tpu_custom_call" | custom-call | flops 33554432 | bytes 1048576 | tf_op jit(solution)/shard_map/pallas_call | solution.py:146
  91.2 11.5 %shard_map.29 = (f32[4,192,256]{2,1,0:T(8,128)}, f32[4,192,256]{2,1,0:T(8,128)}) custom-call(s32[2]{0:T(128)} %pad_add_fusion.place_ref, f32[1280,2560]{1,0:T(8,128)} %a_ref.3, f32[2,256,1280]{2,1,0:T(8,128)} %bitcast.43, f32[256,1280]{1,0:T(8,128)} %bitcast.41, f32[256,256]{1,0:T(8,128)} %get-tuple-element.15.lt_ref), custom_call_target="tpu_custom_call" | custom-call | flops 5033164800 | bytes 13107200 | tf_op jit(solution)/shard_map/pallas_call | solution.py:219
  102.7 1.1 collective-permute-start.2
  103.8 2.1 collective-permute-done.2
  105.9 1.2 add.17
  107.2 0.1 slice_bitcast_fusion.2
  107.2 2.2 collective-permute-start.4
  109.4 2.5 %collective-permute-start.6 = (f32[192,256]{1,0:T(8,128)S(1)}, f32[192,256]{1,0:T(8,128)S(1)}, u32[]{:S(2)}, u32[]{:S(2)}) collective-permute-start(f32[192,256]{1,0:T(8,128)S(1)} %get-tuple-element.24), channel_id=1, source_target_pairs={{0,48},{1,56},{2,0},{3,8},{4,16},{5,24},{6,32},{7,40},{8,112},{9,1... | collective-permute-start | bytes 589832 | tf_op jit(solution)/shard_map/ppermute | solution.py:355
  112.0 5.3 %collective-permute-start.5 = (f32[192,256]{1,0:T(8,128)S(1)}, f32[192,256]{1,0:T(8,128)S(1)}, u32[]{:S(2)}, u32[]{:S(2)}) collective-permute-start(f32[192,256]{1,0:T(8,128)S(1)} %get-tuple-element.25), channel_id=1, source_target_pairs={{0,32},{1,40},{2,48},{3,56},{4,0},{5,8},{6,16},{7,24},{8,96},{9,10... | collective-permute-start | bytes 589832 | tf_op jit(solution)/shard_map/ppermute | solution.py:355
  117.3 6.0 %collective-permute-start.3 = (f32[192,256]{1,0:T(8,128)S(1)}, f32[192,256]{1,0:T(8,128)S(1)}, u32[]{:S(2)}, u32[]{:S(2)}) collective-permute-start(f32[192,256]{1,0:T(8,128)S(1)} %get-tuple-element.26), channel_id=1, source_target_pairs={{0,0},{1,8},{2,16},{3,24},{4,32},{5,40},{6,48},{7,56},{8,64},{9,72... | collective-permute-start | bytes 589832 | tf_op jit(solution)/shard_map/ppermute | solution.py:355
  123.3 5.9 %collective-permute-done.4 = f32[192,256]{1,0:T(8,128)S(1)} collective-permute-done((f32[192,256]{1,0:T(8,128)S(1)}, f32[192,256]{1,0:T(8,128)S(1)}, u32[]{:S(2)}, u32[]{:S(2)}) %collective-permute-start.4) | collective-permute-done | bytes 196640 | tf_op jit(solution)/shard_map/ppermute | solution.py:355
  129.1 2.7 %collective-permute-done.3 = f32[192,256]{1,0:T(8,128)S(1)} collective-permute-done((f32[192,256]{1,0:T(8,128)S(1)}, f32[192,256]{1,0:T(8,128)S(1)}, u32[]{:S(2)}, u32[]{:S(2)}) %collective-permute-start.3) | collective-permute-done | bytes 196640 | tf_op jit(solution)/shard_map/ppermute | solution.py:355
  131.8 0.1 add_add_fusion
  131.9 1.1 fusion
  133.0 0.0 all-gather.6.cloned.1.call-update
  133.0 11.6 %collective-permute-start.10 = (f32[160,256]{1,0:T(8,128)}, f32[160,256]{1,0:T(8,128)S(1)}, u32[]{:S(2)}, u32[]{:S(2)}) collective-permute-start(f32[160,256]{1,0:T(8,128)} %fusion), channel_id=1, source_target_pairs={{0,6},{8,7},{16,0},{24,1},{32,2},{40,3},{48,4},{56,5},{64,14},{72,... | collective-permute-start | bytes 491528 | tf_op jit(solution)/shard_map/ppermute | solution.py:359
  144.6 0.4 collective-permute-start.9
  145.1 2.0 collective-permute-start.8
  147.1 1.9 collective-permute-start.7
  149.0 0.9 broadcast_in_dim.10
  149.9 9.4 %all-to-all-start.2 = ((f32[16,32,256]{2,1,0:T(8,128)}), f32[16,32,256]{2,1,0:T(8,128)S(1)}, u32[]{:S(2)}, u32[]{:S(2)}) async-start(f32[16,32,256]{2,1,0:T(8,128)} %broadcast_in_dim.10), calls=%async_computation.2 | async-start | bytes 1048576 | tf_op jit(solution)/shard_map/all_to_all | solution.py:363
  159.3 6.2 %collective-permute-done.8 = f32[160,256]{1,0:T(8,128)S(1)} collective-permute-done((f32[160,256]{1,0:T(8,128)}, f32[160,256]{1,0:T(8,128)S(1)}, u32[]{:S(2)}, u32[]{:S(2)}) %collective-permute-start.8) | collective-permute-done | bytes 163872 | tf_op jit(solution)/shard_map/ppermute | solution.py:359
  165.5 0.3 collective-permute-start.11
  165.8 3.9 %all-to-all-done.2 = f32[16,32,256]{2,1,0:T(8,128)S(1)} async-done(((f32[16,32,256]{2,1,0:T(8,128)}), f32[16,32,256]{2,1,0:T(8,128)S(1)}, u32[]{:S(2)}, u32[]{:S(2)}) %all-to-all-start.2) | async-done | bytes 524320 | tf_op jit(solution)/shard_map/all_to_all | solution.py:363
  169.7 22.0 %all_to_all.21 = f32[8,32,256]{2,1,0:T(8,128)} all-to-all(f32[8,32,256]{2,1,0:T(8,128)S(1)} %broadcast_in_dim.11), channel_id=1, replica_groups={{0,8,16,24,32,40,48,56},{64,72,80,88,96,104,112,120},{1,9,17,25,33,41,4..., dimensions={0} | all-to-all | bytes 524288 | tf_op jit(solution)/shard_map/all_to_all | solution.py:366
  191.8 0.8 copy-done.4
  192.6 7.5 %shard_map.30 = (bf16[1280,1536]{1,0:T(8,128)(2,1)}, bf16[768,2560]{1,0:T(8,128)(2,1)}) custom-call(s32[2]{0:T(128)} %pad_add_fusion.place_ref, f32[2,256,1280]{2,1,0:T(8,128)} %bitcast.44, f32[256,1280]{1,0:T(8,128)} %bitcast.42, f32[4,160,256]{2,1,0:T(8,128)} %copy-done.1, f32[4,160,256]{2,1,0:T(8,128)} %copy-done.4, f32[256,256]{1,0:T(8,128)} %get-tuple-element.15.lt_ref, ...), custom_call_target="tpu_custom_call" | custom-call | flops 503316480 | bytes 6553600 | tf_op jit(solution)/shard_map/pallas_call | solution.py:278
  200.1 17.8 %shard_map.31 = f32[1280,2560]{1,0:T(8,128)} custom-call(f32[1280,2560]{1,0:T(8,128)} %a_ref.3, bf16[1280,1536]{1,0:T(8,128)(2,1)} %get-tuple-element.19.left_ref, bf16[768,2560]{1,0:T(8,128)(2,1)} %get-tuple-element.20.right_ref, f32[2560,256]{1,0:T(8,128)} %all-gather.6.cloned.1.call-done.weights_ref), custom_call_target="tpu_custom_call" | custom-call | flops 10066329600 | bytes 26214400 | tf_op jit(solution)/shard_map/pallas_call | solution.py:300
  (25 shorter events, 0.2 us)
Async XLA Ops:
  6.5 84.6 %all-gather.4.cloned.1.call-start = ((), (), s32[]{:S(2)}) async-start(), calls=%async_computation.4 | async-start | bytes 2785280 | tf_op jit(solution)/shard_map/all_gather | solution.py:342
  6.5 26.5 %collective-permute-start = (f32[32,1280]{1,0:T(8,128)}, f32[32,1280]{1,0:T(8,128)S(1)}, u32[]{:S(2)}, u32[]{:S(2)}) collective-permute-start(f32[32,1280]{1,0:T(8,128)} %bitcast.51), channel_id=1, source_target_pairs={{0,0},{1,8},{2,16},{3,24},{4,32},{5,40},{6,48},{7,56},{8,64},{9,72... | collective-permute-start | bytes 491528 | tf_op jit(solution)/shard_map/ppermute | solution.py:336
  33.1 0.7 copy-start.5
  33.8 2.8 %collective-permute-start.1 = (f32[4,32,1280]{2,1,0:T(8,128)S(1)}, f32[4,32,1280]{2,1,0:T(8,128)S(1)}, u32[]{:S(2)}, u32[]{:S(2)}) collective-permute-start(f32[4,32,1280]{2,1,0:T(8,128)S(1)} %bitcast.45), channel_id=1, source_target_pairs={{0,1},{1,0},{2,3},{3,2},{4,5},{5,4},{6,7},{7,6},{8,9},{9,8},{10,11... | collective-permute-start | bytes 1966088 | tf_op jit(solution)/shard_map/ppermute | solution.py:339
  36.7 0.9 copy-start.3
  36.8 13.8 %copy-start = (f32[4,2,32,1280]{3,2,1,0:T(8,128)}, f32[4,2,32,1280]{3,2,1,0:T(8,128)S(1)}, u32[]{:S(2)}) copy-start(f32[4,2,32,1280]{3,2,1,0:T(8,128)S(1)} %pad_maximum_fusion) | copy-start | bytes 3932164
  50.6 19.3 %all-to-all-start.1 = ((f32[128,8,128]{2,1,0:T(8,128)}), f32[128,8,128]{2,1,0:T(8,128)S(1)}, u32[]{:S(2)}, u32[]{:S(2)}) async-start(f32[128,8,128]{2,1,0:T(8,128)} %broadcast_in_dim.9), calls=%async_computation.1 | async-start | bytes 1048576 | tf_op jit(solution)/shard_map/all_to_all | solution.py:347
  56.4 143.7 %all-gather.6.cloned.1.call-start = ((), (), s32[]{:S(2)}) async-start(), calls=%async_computation.5 | async-start | bytes 2785280 | tf_op jit(solution)/shard_map/all_gather | solution.py:358
  102.7 3.2 %collective-permute-start.2 = (f32[4,192,256]{2,1,0:T(8,128)}, f32[4,192,256]{2,1,0:T(8,128)S(1)}, u32[]{:S(2)}, u32[]{:S(2)}) collective-permute-start(f32[4,192,256]{2,1,0:T(8,128)} %get-tuple-element.17), channel_id=1, source_target_pairs={{0,1},{1,0},{2,3},{3,2},{4,5},{5,4},{6,7},{7,6},{8,9},{9,8},{10,11... | collective-permute-start | bytes 2359304 | tf_op jit(solution)/shard_map/ppermute | solution.py:352
  107.2 24.7 %copy-start.2 = (f32[256,256]{1,0:T(8,128)S(1)}, f32[256,256]{1,0:T(8,128)}, u32[]{:S(2)}) copy-start(f32[256,256]{1,0:T(8,128)} %get-tuple-element.18.tt_ref) | copy-start | bytes 786436
  107.2 21.9 %collective-permute-start.4 = (f32[192,256]{1,0:T(8,128)S(1)}, f32[192,256]{1,0:T(8,128)S(1)}, u32[]{:S(2)}, u32[]{:S(2)}) collective-permute-start(f32[192,256]{1,0:T(8,128)S(1)} %get-tuple-element.23), channel_id=1, source_target_pairs={{0,16},{1,24},{2,32},{3,40},{4,48},{5,56},{6,0},{7,8},{8,80},{9,88... | collective-permute-start | bytes 589832 | tf_op jit(solution)/shard_map/ppermute | solution.py:355
  109.4 19.7 %collective-permute-start.6 = (f32[192,256]{1,0:T(8,128)S(1)}, f32[192,256]{1,0:T(8,128)S(1)}, u32[]{:S(2)}, u32[]{:S(2)}) collective-permute-start(f32[192,256]{1,0:T(8,128)S(1)} %get-tuple-element.24), channel_id=1, source_target_pairs={{0,48},{1,56},{2,0},{3,8},{4,16},{5,24},{6,32},{7,40},{8,112},{9,1... | collective-permute-start | bytes 589832 | tf_op jit(solution)/shard_map/ppermute | solution.py:355
  112.0 17.2 %collective-permute-start.5 = (f32[192,256]{1,0:T(8,128)S(1)}, f32[192,256]{1,0:T(8,128)S(1)}, u32[]{:S(2)}, u32[]{:S(2)}) collective-permute-start(f32[192,256]{1,0:T(8,128)S(1)} %get-tuple-element.25), channel_id=1, source_target_pairs={{0,32},{1,40},{2,48},{3,56},{4,0},{5,8},{6,16},{7,24},{8,96},{9,10... | collective-permute-start | bytes 589832 | tf_op jit(solution)/shard_map/ppermute | solution.py:355
  117.3 14.6 %collective-permute-start.3 = (f32[192,256]{1,0:T(8,128)S(1)}, f32[192,256]{1,0:T(8,128)S(1)}, u32[]{:S(2)}, u32[]{:S(2)}) collective-permute-start(f32[192,256]{1,0:T(8,128)S(1)} %get-tuple-element.26), channel_id=1, source_target_pairs={{0,0},{1,8},{2,16},{3,24},{4,32},{5,40},{6,48},{7,56},{8,64},{9,72... | collective-permute-start | bytes 589832 | tf_op jit(solution)/shard_map/ppermute | solution.py:355
  133.0 26.2 %collective-permute-start.10 = (f32[160,256]{1,0:T(8,128)}, f32[160,256]{1,0:T(8,128)S(1)}, u32[]{:S(2)}, u32[]{:S(2)}) collective-permute-start(f32[160,256]{1,0:T(8,128)} %fusion), channel_id=1, source_target_pairs={{0,6},{8,7},{16,0},{24,1},{32,2},{40,3},{48,4},{56,5},{64,14},{72,... | collective-permute-start | bytes 491528 | tf_op jit(solution)/shard_map/ppermute | solution.py:359
  144.6 14.6 %collective-permute-start.9 = (f32[160,256]{1,0:T(8,128)}, f32[160,256]{1,0:T(8,128)S(1)}, u32[]{:S(2)}, u32[]{:S(2)}) collective-permute-start(f32[160,256]{1,0:T(8,128)} %fusion), channel_id=1, source_target_pairs={{0,4},{8,5},{16,6},{24,7},{32,0},{40,1},{48,2},{56,3},{64,12},{72,... | collective-permute-start | bytes 491528 | tf_op jit(solution)/shard_map/ppermute | solution.py:359
  145.1 20.4 %collective-permute-start.8 = (f32[160,256]{1,0:T(8,128)}, f32[160,256]{1,0:T(8,128)S(1)}, u32[]{:S(2)}, u32[]{:S(2)}) collective-permute-start(f32[160,256]{1,0:T(8,128)} %fusion), channel_id=1, source_target_pairs={{0,2},{8,3},{16,4},{24,5},{32,6},{40,7},{48,0},{56,1},{64,10},{72,... | collective-permute-start | bytes 491528 | tf_op jit(solution)/shard_map/ppermute | solution.py:359
  147.1 18.4 %collective-permute-start.7 = (f32[160,256]{1,0:T(8,128)}, f32[160,256]{1,0:T(8,128)S(1)}, u32[]{:S(2)}, u32[]{:S(2)}) collective-permute-start(f32[160,256]{1,0:T(8,128)} %fusion), channel_id=1, source_target_pairs={{0,0},{8,1},{16,2},{24,3},{32,4},{40,5},{48,6},{56,7},{64,8},{72,9... | collective-permute-start | bytes 491528 | tf_op jit(solution)/shard_map/ppermute | solution.py:359
  149.9 19.8 %all-to-all-start.2 = ((f32[16,32,256]{2,1,0:T(8,128)}), f32[16,32,256]{2,1,0:T(8,128)S(1)}, u32[]{:S(2)}, u32[]{:S(2)}) async-start(f32[16,32,256]{2,1,0:T(8,128)} %broadcast_in_dim.10), calls=%async_computation.2 | async-start | bytes 1048576 | tf_op jit(solution)/shard_map/all_to_all | solution.py:363
  165.5 26.3 %copy-start.1 = (f32[4,160,256]{2,1,0:T(8,128)}, f32[4,160,256]{2,1,0:T(8,128)S(1)}, u32[]{:S(2)}) copy-start(f32[4,160,256]{2,1,0:T(8,128)S(1)} %pad_maximum_fusion.1.own_ref) | copy-start | bytes 1966084
  165.5 26.3 %collective-permute-start.11 = (f32[4,160,256]{2,1,0:T(8,128)S(1)}, f32[4,160,256]{2,1,0:T(8,128)S(1)}, u32[]{:S(2)}, u32[]{:S(2)}) collective-permute-start(f32[4,160,256]{2,1,0:T(8,128)S(1)} %pad_maximum_fusion.1.own_ref), channel_id=1, source_target_pairs={{0,1},{1,0},{2,3},{3,2},{4,5},{5,4},{6,7},{7,6},{8,9},{9,8},{10,11... | collective-permute-start | bytes 1966088 | tf_op jit(solution)/shard_map/ppermute | solution.py:360
  191.8 0.8 copy-start.4
Sparse Core Ops, SparseCore 0:
  33.9 45.7 all-gather.3
  133.2 61.3 all-gather.5

commit v7 on v5

--- a/solution.py
+++ b/solution.py
@@ -8,6 +8,7 @@
 W = 256
 H = 128
 PANEL = 8
+STRIPS = 8
 BOTH = ("row", "col")
 HIGHEST = lax.Precision.HIGHEST
 
@@ -41,28 +42,35 @@
     return rows, mods, marks
 
 
-def update_rows(mat, cols, mods):
-    new = mat[...]
+def update_rows(mat, first, cols, mods):
+    new = mat[first:]
     for col, mod in zip(cols, mods):
         new = new - col * mod
-    mat[...] = new
-
-
-def factor_kernel(gram_ref, top_ref, lt_ref, tt_ref, gw, vr, lt, lw, spread):
+    mat[first:] = new
+
+
+def factor_kernel(pieces_ref, lt_ref, tt_ref, gw, vr, lt, lw, spread, whole):
     ri = lax.broadcasted_iota(jnp.int32, (W, W), 0)
     ci = lax.broadcasted_iota(jnp.int32, (W, W), 1)
     li = lax.broadcasted_iota(jnp.int32, (1, H), 1)
-    g = gram_ref[...]
+    across = 2 * W // H
+    strip = W // STRIPS
+    tiles = strip // 8 * across
+    for t in range(tiles):
+        for c in range(STRIPS):
+            row = c * strip + t // across * 8
+            whole[row : row + 8, t % across * H : (t % across + 1) * H] = pieces_ref[t * STRIPS + c]
+    g = whole[:, :W]
     scale = 1.0 / jnp.max(jnp.where(ri == ci, g, 0.0), keepdims=True)
     root = jnp.sqrt(scale)
-    t = top_ref[...] * root
+    t = whole[:, W:].T * root
     g = g * scale
 
     def dot(x, y):
         return jnp.dot(x, y, precision=HIGHEST, preferred_element_type=jnp.float32)
 
-    def chol_panel(at):
-        old = [lane(gw[...], at + k) for k in range(PANEL)]
+    def chol_panel(at, first):
+        old = [lane(gw[first:], at + k) for k in range(PANEL)]
 
         def solo(a, here, row, tops):
             d = tops[a]
@@ -78,7 +86,7 @@
             return mod, ratio, row, (upper, lower, marks)
 
         _, mods, marks = panel_step(solo, gw[pl.ds(at, PANEL), :], at)
-        update_rows(gw, old, mods)
+        update_rows(gw, first, old, mods)
         lt[pl.ds(at, PANEL), :] = jnp.concatenate([m[0] for m in marks], axis=0)
         lw[pl.ds(at, PANEL), :] = jnp.concatenate([m[1] for m in marks], axis=0)
         for a in range(PANEL):
@@ -102,21 +110,22 @@
             return mod, ratio, final, None
 
         rows, mods, _ = panel_step(solo, vr[pl.ds(at, PANEL), :], at)
-        update_rows(vr, old, mods)
+        update_rows(vr, 0, old, mods)
         vr[pl.ds(at, PANEL), :] = rows
 
     def block(gram, top):
         gw[...] = gram
         vr[...] = top
-        chol_panel(0)
-
-        def body(i, _):
-            at = pl.multiple_of(i * PANEL, PANEL)
-            jordan_panel(at - PANEL)
-            chol_panel(at)
-            return 0
-
-        lax.fori_loop(1, H // PANEL, body, 0)
+        chol_panel(0, 0)
+        for first in range(0, H, H // 4):
+
+            def body(i, _, first=first):
+                at = pl.multiple_of(i * PANEL, PANEL)
+                jordan_panel(at - PANEL)
+                chol_panel(at, first)
+                return 0
+
+            lax.fori_loop(max(first // PANEL, 1), (first + H // 4) // PANEL, body, 0)
         jordan_panel(H - PANEL)
         return lt[...], lw[...], vr[...]
 
@@ -141,16 +150,17 @@
     tt_ref[H:, H:] = x22 * scale
 
 
-def factor(gram, top):
+def factor(pieces):
     vmem = pl.BlockSpec(memory_space=pltpu.VMEM)
+    square = pltpu.VMEM((H, H), jnp.float32)
     return pl.pallas_call(
         factor_kernel,
         out_shape=[jax.ShapeDtypeStruct((W, W), jnp.float32)] * 2,
-        in_specs=[vmem] * 2,
+        in_specs=[vmem],
         out_specs=[vmem] * 2,
-        scratch_shapes=[pltpu.VMEM((H, H), jnp.float32)] * 4 + [pltpu.VMEM((PANEL, PANEL + 2, H), jnp.float32)],
+        scratch_shapes=[square] * 4 + [pltpu.VMEM((PANEL, PANEL + 2, H), jnp.float32), pltpu.VMEM((W, 2 * W), jnp.float32)],
         cost_estimate=pl.CostEstimate(flops=2 * W**3, bytes_accessed=16 * W * W, transcendentals=0),
-    )(gram, top)
+    )(pieces)
 
 
 def to_tiles(x):
@@ -180,7 +190,7 @@
     return lax.dot_general(left, right, (contract, ((), ())), preferred_element_type=jnp.float32)
 
 
-def product_kernel(place_ref, a_ref, cols_ref, rows_ref, lt_ref, keep_ref, send_ref, acc):
+def product_kernel(place_ref, a_ref, cols_ref, rows_ref, lt_ref, keep_ref, send_ref, acc, inner_scr):
     step = pl.program_id(0)
     steps = pl.num_programs(0)
 
@@ -200,19 +210,17 @@
         own = (place_ref[0] == 0).astype(jnp.float32)
         inner = dots(rows_ref[:, :W] + own * lt_ref[...].T, acc[:W], NN)
         inner = inner + dots(rows_ref[:, W:], acc[W:], NN)
-        odd = place_ref[1] % 2 == 1
+        inner_scr[...] = inner
         lines = keep_ref.shape[0]
         part = acc.shape[0] // (2 * lines)
         size = W // (2 * lines)
+        line = place_ref[1] // 2
+        core = place_ref[1] % 2
         for q in range(lines):
-            for k in range(2):
-                i = 2 * q + k
-                for target, mine in ((keep_ref, odd == (k == 1)), (send_ref, odd != (k == 1))):
-
-                    @pl.when(mine)
-                    def _(target=target, i=i, q=q):
-                        target[q, :part] = acc[i * part : (i + 1) * part]
-                        target[q, part:] = inner[i * size : (i + 1) * size]
+            for target, k in ((keep_ref, core), (send_ref, 1 - core)):
+                i = 2 * ((line + q) % lines) + k
+                target[q, :part] = acc[pl.ds(pl.multiple_of(i * part, 8), part)]
+                target[q, part:] = inner_scr[pl.ds(pl.multiple_of(i * size, 8), size)]
 
 
 def product(place, trailing, panel_cols, panel_rows, factor_t, parts):
@@ -234,32 +242,49 @@
             pl.BlockSpec((W, W), lambda i: (0, 0)),
         ],
         out_specs=[out_spec, out_spec],
-        scratch_shapes=[pltpu.VMEM((rows, W), jnp.float32)],
+        scratch_shapes=[pltpu.VMEM((rows, W), jnp.float32), pltpu.VMEM((W, W), jnp.float32)],
         compiler_params=pltpu.CompilerParams(vmem_limit_bytes=VMEM_BYTES),
         cost_estimate=pl.CostEstimate(flops=6 * rows * cols * W, bytes_accessed=4 * rows * cols, transcendentals=0),
     )(place, trailing, panel_cols, panel_rows, factor_t)
 
 
-def prepare_kernel(place_ref, cols_ref, rows_ref, own_ref, other_ref, lt_ref, tt_ref, inner_ref, out_ref, right_ref, reflect):
+def parts_kernel(place_ref, cols_ref, rows_ref, lt_ref, left_ref, right_ref):
     half = cols_ref.shape[2]
+    lt = lt_ref[...]
+    for i in range(rows_ref.shape[1] // W):
+        at = slice(i * W, (i + 1) * W)
+        rows = rows_ref[:, at].T
+        if i == 0:
+            rows = rows + lt * (place_ref[0] == 0).astype(jnp.float32)
+        high, low = split(rows)
+        for p, part in enumerate((high, high, low)):
+            left_ref[at, p * W : (p + 1) * W] = part
     for h in range(cols_ref.shape[0]):
         for i in range(half // W):
             cols = cols_ref[h, :, i * W : (i + 1) * W]
             if h == 0 and i == 0:
-                cols = cols + lt_ref[...].T * (place_ref[1] == 0).astype(jnp.float32)
+                cols = cols + lt.T * (place_ref[1] == 0).astype(jnp.float32)
             high, low = split(cols)
             at = slice(h * half + i * W, h * half + (i + 1) * W)
             for p, part in enumerate((high, low, high)):
                 right_ref[p * W : (p + 1) * W, at] = part
-    for i in range(rows_ref.shape[1] // W):
-        at = slice(i * W, (i + 1) * W)
-        rows = rows_ref[:, at].T
-        if i == 0:
-            rows = rows + lt_ref[...] * (place_ref[0] == 0).astype(jnp.float32)
-        high, low = split(rows)
-        both = jnp.concatenate([high, high, low], axis=1)
-        reflect[at] = both
-        out_ref[at, : 3 * W] = both
+
+
+def parts_of(place, panel_cols, panel_rows, factor_t):
+    rows = panel_rows.shape[1]
+    cols = panel_cols.shape[0] * panel_cols.shape[2]
+    vmem = pl.BlockSpec(memory_space=pltpu.VMEM)
+    return pl.pallas_call(
+        parts_kernel,
+        out_shape=[jax.ShapeDtypeStruct(shape, jnp.bfloat16) for shape in ((rows, 3 * W), (3 * W, cols))],
+        in_specs=[pl.BlockSpec(memory_space=pltpu.SMEM)] + [vmem] * 3,
+        out_specs=[vmem] * 2,
+        compiler_params=pltpu.CompilerParams(vmem_limit_bytes=VMEM_BYTES),
+        cost_estimate=pl.CostEstimate(flops=8 * rows * W, bytes_accessed=10 * (rows + cols) * W, transcendentals=0),
+    )(place, panel_cols, panel_rows, factor_t)
+
+
+def correct_kernel(place_ref, left_ref, own_ref, other_ref, tt_ref, inner_ref, out_ref):
     t = tt_ref[...]
     mid = jnp.dot(t, inner_ref[...], precision=HIGHEST, preferred_element_type=jnp.float32)
     square = lax.dot_general(mid, t, (NT, ((), ())), precision=HIGHEST, preferred_element_type=jnp.float32)
@@ -272,35 +297,32 @@
         before = (line + lines - s) % lines
         for ref, k in ((own_ref, core), (other_ref, 1 - core)):
             at = pl.multiple_of((2 * before + k) * part, 16)
-            weights = ref[s] - jnp.dot(reflect[pl.ds(at, part)], right, preferred_element_type=jnp.float32)
+            weights = ref[s] - jnp.dot(left_ref[pl.ds(at, part)], right, preferred_element_type=jnp.float32)
             high, low = split(weights)
-            out_ref[pl.ds(at, part), 3 * W :] = jnp.concatenate([high, high, low], axis=1)
-
-
-def prepare(place, panel_cols, panel_rows, own, other, factor_t, coupling_t, inner):
-    rows = panel_rows.shape[1]
-    cols = panel_cols.shape[0] * panel_cols.shape[2]
+            out_ref[pl.ds(at, part)] = jnp.concatenate([high, high, low], axis=1)
+
+
+def correct(place, left, own, other, coupling_t, inner):
     vmem = pl.BlockSpec(memory_space=pltpu.VMEM)
     return pl.pallas_call(
-        prepare_kernel,
-        out_shape=[jax.ShapeDtypeStruct((rows, 6 * W), jnp.bfloat16), jax.ShapeDtypeStruct((3 * W, cols), jnp.bfloat16)],
-        in_specs=[pl.BlockSpec(memory_space=pltpu.SMEM)] + [vmem] * 7,
-        out_specs=[vmem] * 2,
-        scratch_shapes=[pltpu.VMEM((rows, 3 * W), jnp.bfloat16)],
+        correct_kernel,
+        out_shape=jax.ShapeDtypeStruct(left.shape, jnp.bfloat16),
+        in_specs=[pl.BlockSpec(memory_space=pltpu.SMEM)] + [vmem] * 5,
+        out_specs=vmem,
         compiler_params=pltpu.CompilerParams(vmem_limit_bytes=VMEM_BYTES),
-        cost_estimate=pl.CostEstimate(flops=6 * rows * W * W, bytes_accessed=20 * rows * W, transcendentals=0),
-    )(place, panel_cols, panel_rows, own, other, factor_t, coupling_t, inner)
-
-
-def update_kernel(a_ref, left_ref, right_ref, weights_ref, out_ref):
+        cost_estimate=pl.CostEstimate(flops=2 * left.size * W, bytes_accessed=8 * left.size, transcendentals=0),
+    )(place, left, own, other, coupling_t, inner)
+
+
+def update_kernel(a_ref, left_ref, wleft_ref, right_ref, weights_ref, out_ref):
     high, low = split(weights_ref[...].T)
     right = jnp.concatenate([high, low, high], axis=0)
-    first = jnp.dot(left_ref[:, : 3 * W], right, preferred_element_type=jnp.float32)
-    second = jnp.dot(left_ref[:, 3 * W :], right_ref[...], preferred_element_type=jnp.float32)
+    first = jnp.dot(left_ref[...], right, preferred_element_type=jnp.float32)
+    second = jnp.dot(wleft_ref[...], right_ref[...], preferred_element_type=jnp.float32)
     out_ref[...] = a_ref[...] - (first + second)
 
 
-def update(trailing, left, right, weight_cols):
+def update(trailing, left, weight_left, right, weight_cols):
     rows, cols = trailing.shape
     tile = 512
     return pl.pallas_call(
@@ -309,14 +331,15 @@
         out_shape=jax.ShapeDtypeStruct((rows, cols), jnp.float32),
         in_specs=[
             pl.BlockSpec((rows, tile), lambda i: (0, i)),
-            pl.BlockSpec((rows, 6 * W), lambda i: (0, 0)),
+            pl.BlockSpec((rows, 3 * W), lambda i: (0, 0)),
+            pl.BlockSpec((rows, 3 * W), lambda i: (0, 0)),
             pl.BlockSpec((3 * W, tile), lambda i: (0, i)),
             pl.BlockSpec((tile, W), lambda i: (i, 0)),
         ],
         out_specs=pl.BlockSpec((rows, tile), lambda i: (0, i)),
         compiler_params=pltpu.CompilerParams(vmem_limit_bytes=VMEM_BYTES),
         cost_estimate=pl.CostEstimate(flops=12 * rows * cols * W, bytes_accessed=8 * rows * cols, transcendentals=0),
-    )(trailing, left, right, weight_cols)
+    )(trailing, left, weight_left, right, weight_cols)
 
 
 def shards(trailing, panel_block):
@@ -344,26 +367,28 @@
     pieces = to_tiles(jnp.concatenate([strip, top], axis=1))
     mine = jnp.sum(lax.all_to_all(pieces, "row", 0, 0, tiled=True), axis=0)
     full = lax.all_to_all(jnp.broadcast_to(mine[None], (nr * nc,) + mine.shape), BOTH, 0, 0, tiled=True)
-    tr, tc = width // 8, 2 * W // H
-    full = full.reshape(tr, tc, nc, 8, H).transpose(2, 0, 3, 1, 4).reshape(W, 2 * W)
-    factor_t, coupling_t = factor(full[:, :W], full[:, W:].T)
+    factor_t, coupling_t = factor(full)
     keep, send = product(place, trailing, panel_cols, panel_rows, factor_t, nc)
     pieces = keep + lax.ppermute(send, "col", pair)
-    pieces = jnp.sum(lax.all_to_all(pieces, "col", 0, 0, tiled=True, axis_index_groups=lines), axis=0)
+    shifts = [[(j, (j + 2 * s) % nc) for j in range(nc)] for s in range(1, nc // 2)]
+    pieces = pieces[0] + sum(lax.ppermute(pieces[s + 1], "col", shift) for s, shift in enumerate(shifts))
     mine, inner = pieces[:part], pieces[part:]
     mine = lax.dot_general(mine, coupling_t, (((1,), (1,)), ((), ())), precision=HIGHEST)
+    mine, later = lax.optimization_barrier((mine, panel_rows))
     moved = lax.ppermute(mine, BOTH, perm)
+    left, right = parts_of(place, panel_cols, later, factor_t)
+    moved, left = lax.optimization_barrier((moved, left))
     weight_cols = lax.all_gather(moved, "row", axis=0, tiled=True)
-    shifts = [[(j, (j + 2 * s) % nc) for j in range(nc)] for s in range(1, nc // 2)]
     line = jnp.stack([mine] + [lax.ppermute(mine, "col", shift) for shift in shifts])
-    other = lax.ppermute(line, "col", pair)
     half = (nr, 8 * W * W // (8 * H * nr * nc), H)
     inner = jnp.sum(lax.all_to_all(to_tiles(inner).reshape(half), "row", 0, 0, tiled=True), axis=0)
+    line, inner = lax.optimization_barrier((line, inner))
+    other = lax.ppermute(line, "col", pair)
     inner = jnp.broadcast_to(inner[None], (nr * nc,) + inner.shape)
     inner = lax.all_to_all(inner, BOTH, 0, 0, tiled=True).reshape((nr, nc) + inner.shape[1:])
     inner = from_tiles(inner.transpose(1, 0, 2, 3).reshape(-1, 8, H), W, W)
-    left, right = prepare(place, panel_cols, panel_rows, line, other, factor_t, coupling_t, inner)
-    return update(trailing, left, right, weight_cols)
+    weight_left = correct(place, left, line, other, coupling_t, inner)
+    return update(trailing, left, weight_left, right, weight_cols)
 
 
 def solution(mesh):

time: 213 us -> 204 us (0.958)
  blocking collectives: 72.4 us -> 58.4 us
  starting transfers between devices: 27.9 us -> 31.7 us
    all_to_all x1 -> x0, blocking collectives: 14.6 us -> none  [shards(): lax.all_to_all(pieces, 'col', 0, 0, tiled=True, axis_index_groups=lines)]
    ppermute x0 -> x3, waiting for transfers between devices: none -> 10 us  [shards(): lax.ppermute(pieces[s + 1], 'col', shift)]
    ppermute x3, waiting for transfers between devices: 9.82 us -> 1.08 us  [shards(): lax.ppermute(mine, 'col', shift)]
    all_gather x1, waiting for transfers between devices: 0.01 us -> 4.26 us  [shards(): weight_cols = lax.all_gather(moved, 'row', axis=0, tiled=True)]
    ppermute x1, waiting for transfers between devices: 5.3 us -> 1.1 us  [shards(): moved = lax.ppermute(mine, BOTH, perm)]
    ppermute x0 -> x3, starting transfers between devices: none -> 2.59 us  [shards(): lax.ppermute(pieces[s + 1], 'col', shift)]
    pallas_call x1 -> x2, Pallas kernels: 7.63 us -> 10.2 us  [the longest x1 5.16 us: correct(): pl.pallas_call(correct_kernel, out_shape=jax.ShapeDtypeStruct(left.shape,...]
  transfers between devices with their start and end apart: 11 -> 14, of which waited for: 6 -> 9; matrix products, arithmetic and copies ran while one was open for 3% -> 2% of each run, Pallas kernels for 13% -> 14%
where the time goes in v7:
time: 204 us
  blocking collectives  58.4 us (29%)
  Pallas kernels  57.2 us (28%)
  waiting for transfers between devices  32.4 us (16%)
  starting transfers between devices  31.7 us (16%)
  between operations  13.5 us (7%)
  local copies, waits for them, and re-layouts  5.61 us (3%)
  other arithmetic  3.02 us (1%)
    all_gather x1, blocking collectives, shards(): line = lax.all_gather(panel_t, 'col', axis=0, axis_index_groups=lines)  21.6 us
    pallas_call x1, Pallas kernels, update(): pl.pallas_call(update_kernel, grid=(cols // tile,), out_shape=jax.ShapeDt...  17.8 us
    pallas_call x1, Pallas kernels, factor(): pl.pallas_call(factor_kernel, out_shape=[jax.ShapeDtypeStruct((W, W), jnp...  17.6 us
    all_to_all x1, blocking collectives, shards(): lax.all_to_all(inner, BOTH, 0, 0, tiled=True)  17 us
    all_to_all x1, waiting for transfers between devices, shards(): lax.all_to_all(jnp.broadcast_to(mine[None], (nr * nc,) + mine.shape), BOT...  12.8 us
    pallas_call x1, Pallas kernels, product(): pl.pallas_call(product_kernel, grid=(cols // tile,), out_shape=[out, out]...  11.5 us
    ppermute x3, starting transfers between devices, shards(): lax.ppermute(mine, 'col', shift)  11 us
    all_to_all x1, blocking collectives, shards(): mine = jnp.sum(lax.all_to_all(pieces, 'row', 0, 0, tiled=True), axis=0)  10.9 us
  transfers between devices with their start and end apart: 14, of which 9 were waited for; matrix products, arithmetic and copies ran while one was open for 2% of the time, Pallas kernels for 14%

profile of v7, /device:TPU:1, one launch (start us, length us, event | category | flops | bytes accessed | tf_op | source)
XLA Modules:
  0.0 203.5 jit_solution(16197728816882921154)
XLA Ops:
  6.5 4.9 %collective-permute-start = (f32[32,1280]{1,0:T(8,128)}, f32[32,1280]{1,0:T(8,128)S(1)}, u32[]{:S(2)}, u32[]{:S(2)}) collective-permute-start(f32[32,1280]{1,0:T(8,128)} %bitcast.60), channel_id=1, source_target_pairs={{0,0},{1,8},{2,16},{3,24},{4,32},{5,40},{6,48},{7,56},{8,64},{9,72... | collective-permute-start | bytes 491528 | tf_op jit(solution)/shard_map/ppermute | solution.py:358
  11.5 21.6 %all-gather = f32[128,1280]{1,0:T(8,128)S(1)} all-gather(f32[32,1280]{1,0:T(8,128)} %bitcast.61), channel_id=2, replica_groups={{0,2,4,6},{1,3,5,7},{8,10,12,14},{9,11,13,15},{16,18,20,22},{17,19,21,2..., dimensions={0}, use_global_device_ids=true | all-gather | bytes 819200 | tf_op jit(solution)/shard_map/all_gather | solution.py:359
  33.1 0.7 copy-done.6
  33.7 0.0 all-gather.4.cloned.1.call-update
  33.8 1.1 collective-permute-start.1
  34.9 0.8 slice_select_fusion
  35.6 1.0 collective-permute-done.1
  36.6 0.1 select_bitcast_fusion.1
  36.7 0.1 pad_maximum_fusion
  36.8 0.0 copy-start
  36.8 0.8 copy-done.4
  37.6 1.2 convolution_bitcast_fusion
  38.9 10.9 %all_to_all.20 = f32[16,8,128]{2,1,0:T(8,128)S(1)} all-to-all(f32[16,8,128]{2,1,0:T(8,128)S(1)} %bitcast.64), channel_id=1, replica_groups=mesh['row'=16,'col'=8] {'row'}, dimensions={0} | all-to-all | bytes 131072 | tf_op jit(solution)/shard_map/all_to_all | solution.py:368
  49.8 0.8 broadcast_in_dim.7
  50.6 5.8 %all-to-all-start.1 = ((f32[128,8,128]{2,1,0:T(8,128)}), f32[128,8,128]{2,1,0:T(8,128)S(1)}, u32[]{:S(2)}, u32[]{:S(2)}) async-start(f32[128,8,128]{2,1,0:T(8,128)} %broadcast_in_dim.7), calls=%async_computation.1 | async-start | bytes 1048576 | tf_op jit(solution)/shard_map/all_to_all | solution.py:369
  56.4 0.0 all-gather.6.cloned.1.call-start
  56.5 0.6 pad_add_fusion.place_ref
  57.1 12.8 %all-to-all-done.1.pieces_ref = f32[128,8,128]{2,1,0:T(8,128)S(1)} async-done(((f32[128,8,128]{2,1,0:T(8,128)}), f32[128,8,128]{2,1,0:T(8,128)S(1)}, u32[]{:S(2)}, u32[]{:S(2)}) %all-to-all-start.1) | async-done | bytes 524320 | tf_op jit(solution)/shard_map/all_to_all | solution.py:369
  69.9 0.8 copy-done.2
  70.7 17.6 %shard_map.28 = (f32[256,256]{1,0:T(8,128)}, f32[256,256]{1,0:T(8,128)}) custom-call(f32[128,8,128]{2,1,0:T(8,128)} %copy-done.2), custom_call_target="tpu_custom_call" | custom-call | flops 33554432 | bytes 1048576 | tf_op jit(solution)/shard_map/pallas_call | solution.py:156
  88.4 11.5 %shard_map.29 = (f32[4,192,256]{2,1,0:T(8,128)}, f32[4,192,256]{2,1,0:T(8,128)}) custom-call(s32[2]{0:T(128)} %pad_add_fusion.place_ref, f32[1280,2560]{1,0:T(8,128)} %a_ref.3, f32[2,256,1280]{2,1,0:T(8,128)} %bitcast.54, f32[256,1280]{1,0:T(8,128)} %bitcast.52, f32[256,256]{1,0:T(8,128)} %get-tuple-element.21.lt_ref), custom_call_target="tpu_custom_call" | custom-call | flops 5033164800 | bytes 13107200 | tf_op jit(solution)/shard_map/pallas_call | solution.py:233
  99.9 1.1 collective-permute-start.2
  101.0 2.1 %collective-permute-done.2 = f32[4,192,256]{2,1,0:T(8,128)S(1)} collective-permute-done((f32[4,192,256]{2,1,0:T(8,128)}, f32[4,192,256]{2,1,0:T(8,128)S(1)}, u32[]{:S(2)}, u32[]{:S(2)}) %collective-permute-start.2) | collective-permute-done | bytes 786464 | tf_op jit(solution)/shard_map/ppermute | solution.py:372
  103.2 1.3 add.17
  104.5 0.5 collective-permute-start.4
  105.0 2.1 %collective-permute-start.5 = (f32[192,256]{1,0:T(8,128)S(1)}, f32[192,256]{1,0:T(8,128)S(1)}, u32[]{:S(2)}, u32[]{:S(2)}) collective-permute-start(f32[192,256]{1,0:T(8,128)S(1)} %get-tuple-element.36), channel_id=1, source_target_pairs={{0,6},{1,7},{2,0},{3,1},{4,2},{5,3},{6,4},{7,5},{8,14},{9,15},{10,... | collective-permute-start | bytes 589832 | tf_op jit(solution)/shard_map/ppermute | solution.py:374
  107.1 5.1 %collective-permute-done.4 = f32[192,256]{1,0:T(8,128)S(1)} collective-permute-done((f32[192,256]{1,0:T(8,128)S(1)}, f32[192,256]{1,0:T(8,128)S(1)}, u32[]{:S(2)}, u32[]{:S(2)}) %collective-permute-start.4) | collective-permute-done | bytes 196640 | tf_op jit(solution)/shard_map/ppermute | solution.py:374
  112.2 2.3 %collective-permute-done.5 = f32[192,256]{1,0:T(8,128)S(1)} collective-permute-done((f32[192,256]{1,0:T(8,128)S(1)}, f32[192,256]{1,0:T(8,128)S(1)}, u32[]{:S(2)}, u32[]{:S(2)}) %collective-permute-start.5) | collective-permute-done | bytes 196640 | tf_op jit(solution)/shard_map/ppermute | solution.py:374
  114.5 2.6 %collective-permute-done.3 = f32[192,256]{1,0:T(8,128)S(1)} collective-permute-done((f32[192,256]{1,0:T(8,128)S(1)}, f32[192,256]{1,0:T(8,128)S(1)}, u32[]{:S(2)}, u32[]{:S(2)}) %collective-permute-start.3) | collective-permute-done | bytes 196640 | tf_op jit(solution)/shard_map/ppermute | solution.py:374
  117.1 0.1 fusion
  117.2 0.4 fusion.1
  117.6 2.9 %collective-permute-start.6 = (f32[160,256]{1,0:T(8,128)S(1)}, f32[160,256]{1,0:T(8,128)S(1)}, u32[]{:S(2)}, u32[]{:S(2)}) collective-permute-start(f32[160,256]{1,0:T(8,128)S(1)} %fusion.1), channel_id=1, source_target_pairs={{0,0},{1,8},{2,16},{3,24},{4,32},{5,40},{6,48},{7,56},{8,64},{9,72... | collective-permute-start | bytes 491528 | tf_op jit(solution)/shard_map/ppermute | solution.py:378
  120.5 5.1 %shard_map.30 = (bf16[1280,768]{1,0:T(8,128)(2,1)}, bf16[768,2560]{1,0:T(8,128)(2,1)}) custom-call(s32[2]{0:T(128)} %pad_add_fusion.place_ref, f32[2,256,1280]{2,1,0:T(8,128)} %bitcast.55, f32[256,1280]{1,0:T(8,128)} %bitcast.53, f32[256,256]{1,0:T(8,128)} %get-tuple-element.21.lt_ref), custom_call_target="tpu_custom_call" | custom-call | flops 2621440 | bytes 9830400 | tf_op jit(solution)/shard_map/pallas_call | solution.py:277
  125.6 1.1 collective-permute-done.6
  126.7 0.7 copy-done.7
  127.3 0.0 all-gather.6.cloned.1.call-update
  127.4 10.3 %collective-permute-start.9 = (f32[160,256]{1,0:T(8,128)S(1)}, f32[160,256]{1,0:T(8,128)S(1)}, u32[]{:S(2)}, u32[]{:S(2)}) collective-permute-start(f32[160,256]{1,0:T(8,128)S(1)} %fusion.1), channel_id=1, source_target_pairs={{0,6},{1,7},{2,0},{3,1},{4,2},{5,3},{6,4},{7,5},{8,14},{9,15},{10,... | collective-permute-start | bytes 491528 | tf_op jit(solution)/shard_map/ppermute | solution.py:382
  137.7 0.7 collective-permute-start.7
  138.3 9.0 %all_to_all.21 = f32[16,4,128]{2,1,0:T(4,128)S(1)} all-to-all(f32[16,4,128]{2,1,0:T(4,128)S(1)} %bitcast.68), channel_id=1, replica_groups=mesh['row'=16,'col'=8] {'row'}, dimensions={0} | all-to-all | bytes 65536 | tf_op jit(solution)/shard_map/all_to_all | solution.py:384
  147.4 1.1 collective-permute-done.7
  148.5 0.0 copy-start.1
  148.5 2.2 %collective-permute-start.10 = (f32[4,160,256]{2,1,0:T(8,128)S(1)}, f32[4,160,256]{2,1,0:T(8,128)S(1)}, u32[]{:S(2)}, u32[]{:S(2)}) collective-permute-start(f32[4,160,256]{2,1,0:T(8,128)S(1)} %pad_maximum_fusion.1.own_ref), channel_id=1, source_target_pairs={{0,1},{1,0},{2,3},{3,2},{4,5},{5,4},{6,7},{7,6},{8,9},{9,8},{10,11... | collective-permute-start | bytes 1966088 | tf_op jit(solution)/shard_map/ppermute | solution.py:386
  150.8 17.0 %all_to_all.22 = f32[128,4,128]{2,1,0:T(4,128)S(1)} all-to-all(f32[128,4,128]{2,1,0:T(4,128)S(1)} %broadcast_in_dim.8), channel_id=1, replica_groups=mesh['row'=16,'col'=8] {'row','col'}, dimensions={0} | all-to-all | bytes 524288 | tf_op jit(solution)/shard_map/all_to_all | solution.py:388
  167.8 0.9 copy.9
  168.6 0.9 copy-done.5
  169.5 5.2 %shard_map.31.wleft_ref = bf16[1280,768]{1,0:T(8,128)(2,1)} custom-call(s32[2]{0:T(128)} %pad_add_fusion.place_ref, bf16[1280,768]{1,0:T(8,128)(2,1)} %get-tuple-element.28.left_ref, f32[4,160,256]{2,1,0:T(8,128)} %copy-done.1, f32[4,160,256]{2,1,0:T(8,128)} %copy-done.5, f32[256,256]{1,0:T(8,128)} %get-tuple-element.24.tt_ref, f32[256,256]{1,0:T(8,128)} %bitcast.58), custom_call_target="tpu_custom_call" | custom-call | flops 503316480 | bytes 7864320 | tf_op jit(solution)/shard_map/pallas_call | solution.py:307
  174.7 4.3 %all-gather.6.cloned.1.call-done.weights_ref = f32[2560,256]{1,0:T(8,128)} async-done(((f32[160,256]{1,0:T(8,128)}), f32[2560,256]{1,0:T(8,128)}) %all-gather.6.cloned.1.call-update) | async-done | bytes 2621456 | tf_op jit(solution)/shard_map/all_gather | solution.py:381
  178.9 17.8 %shard_map.32 = f32[1280,2560]{1,0:T(8,128)} custom-call(f32[1280,2560]{1,0:T(8,128)} %a_ref.3, bf16[1280,768]{1,0:T(8,128)(2,1)} %get-tuple-element.28.left_ref, bf16[1280,768]{1,0:T(8,128)(2,1)} %shard_map.31.wleft_ref, bf16[768,2560]{1,0:T(8,128)(2,1)} %get-tuple-element.31.right_ref, f32[2560,256]{1,0:T(8,128)} %all-gather.6.cloned.1.call-done.weights_ref), custom_call_target="tpu_custom_call" | custom-call | flops 10066329600 | bytes 26214400 | tf_op jit(solution)/shard_map/pallas_call | solution.py:328
  (25 shorter events, 0.2 us)
Async XLA Ops:
  6.5 81.9 %all-gather.4.cloned.1.call-start = ((), (), s32[]{:S(2)}) async-start(), calls=%async_computation.4 | async-start | bytes 2785280 | tf_op jit(solution)/shard_map/all_gather | solution.py:364
  6.5 26.5 %collective-permute-start = (f32[32,1280]{1,0:T(8,128)}, f32[32,1280]{1,0:T(8,128)S(1)}, u32[]{:S(2)}, u32[]{:S(2)}) collective-permute-start(f32[32,1280]{1,0:T(8,128)} %bitcast.60), channel_id=1, source_target_pairs={{0,0},{1,8},{2,16},{3,24},{4,32},{5,40},{6,48},{7,56},{8,64},{9,72... | collective-permute-start | bytes 491528 | tf_op jit(solution)/shard_map/ppermute | solution.py:358
  33.1 0.7 copy-start.6
  33.8 2.8 %collective-permute-start.1 = (f32[4,32,1280]{2,1,0:T(8,128)S(1)}, f32[4,32,1280]{2,1,0:T(8,128)S(1)}, u32[]{:S(2)}, u32[]{:S(2)}) collective-permute-start(f32[4,32,1280]{2,1,0:T(8,128)S(1)} %bitcast.56), channel_id=1, source_target_pairs={{0,1},{1,0},{2,3},{3,2},{4,5},{5,4},{6,7},{7,6},{8,9},{9,8},{10,11... | collective-permute-start | bytes 1966088 | tf_op jit(solution)/shard_map/ppermute | solution.py:361
  36.7 0.9 copy-start.4
  36.8 51.6 %copy-start = (f32[4,2,32,1280]{3,2,1,0:T(8,128)}, f32[4,2,32,1280]{3,2,1,0:T(8,128)S(1)}, u32[]{:S(2)}) copy-start(f32[4,2,32,1280]{3,2,1,0:T(8,128)S(1)} %pad_maximum_fusion) | copy-start | bytes 3932164
  50.6 19.3 %all-to-all-start.1 = ((f32[128,8,128]{2,1,0:T(8,128)}), f32[128,8,128]{2,1,0:T(8,128)S(1)}, u32[]{:S(2)}, u32[]{:S(2)}) async-start(f32[128,8,128]{2,1,0:T(8,128)} %broadcast_in_dim.7), calls=%async_computation.1 | async-start | bytes 1048576 | tf_op jit(solution)/shard_map/all_to_all | solution.py:369
  56.4 122.5 %all-gather.6.cloned.1.call-start = ((), (), s32[]{:S(2)}) async-start(), calls=%async_computation.5 | async-start | bytes 2785280 | tf_op jit(solution)/shard_map/all_gather | solution.py:381
  69.9 0.8 copy-start.2
  99.9 3.2 %collective-permute-start.2 = (f32[4,192,256]{2,1,0:T(8,128)}, f32[4,192,256]{2,1,0:T(8,128)S(1)}, u32[]{:S(2)}, u32[]{:S(2)}) collective-permute-start(f32[4,192,256]{2,1,0:T(8,128)} %get-tuple-element.23), channel_id=1, source_target_pairs={{0,1},{1,0},{2,3},{3,2},{4,5},{5,4},{6,7},{7,6},{8,9},{9,8},{10,11... | collective-permute-start | bytes 2359304 | tf_op jit(solution)/shard_map/ppermute | solution.py:372
  103.2 14.0 %copy-start.3 = (f32[256,256]{1,0:T(8,128)S(1)}, f32[256,256]{1,0:T(8,128)}, u32[]{:S(2)}) copy-start(f32[256,256]{1,0:T(8,128)} %get-tuple-element.24.tt_ref) | copy-start | bytes 786436
  104.5 7.7 %collective-permute-start.4 = (f32[192,256]{1,0:T(8,128)S(1)}, f32[192,256]{1,0:T(8,128)S(1)}, u32[]{:S(2)}, u32[]{:S(2)}) collective-permute-start(f32[192,256]{1,0:T(8,128)S(1)} %get-tuple-element.35), channel_id=1, source_target_pairs={{0,4},{1,5},{2,6},{3,7},{4,0},{5,1},{6,2},{7,3},{8,12},{9,13},{10,... | collective-permute-start | bytes 589832 | tf_op jit(solution)/shard_map/ppermute | solution.py:374
  105.0 9.5 %collective-permute-start.5 = (f32[192,256]{1,0:T(8,128)S(1)}, f32[192,256]{1,0:T(8,128)S(1)}, u32[]{:S(2)}, u32[]{:S(2)}) collective-permute-start(f32[192,256]{1,0:T(8,128)S(1)} %get-tuple-element.36), channel_id=1, source_target_pairs={{0,6},{1,7},{2,0},{3,1},{4,2},{5,3},{6,4},{7,5},{8,14},{9,15},{10,... | collective-permute-start | bytes 589832 | tf_op jit(solution)/shard_map/ppermute | solution.py:374
  107.1 10.0 %collective-permute-start.3 = (f32[192,256]{1,0:T(8,128)S(1)}, f32[192,256]{1,0:T(8,128)S(1)}, u32[]{:S(2)}, u32[]{:S(2)}) collective-permute-start(f32[192,256]{1,0:T(8,128)S(1)} %get-tuple-element.37), channel_id=1, source_target_pairs={{0,2},{1,3},{2,4},{3,5},{4,6},{5,7},{6,0},{7,1},{8,10},{9,11},{10,... | collective-permute-start | bytes 589832 | tf_op jit(solution)/shard_map/ppermute | solution.py:374
  117.6 9.1 %collective-permute-start.6 = (f32[160,256]{1,0:T(8,128)S(1)}, f32[160,256]{1,0:T(8,128)S(1)}, u32[]{:S(2)}, u32[]{:S(2)}) collective-permute-start(f32[160,256]{1,0:T(8,128)S(1)} %fusion.1), channel_id=1, source_target_pairs={{0,0},{1,8},{2,16},{3,24},{4,32},{5,40},{6,48},{7,56},{8,64},{9,72... | collective-permute-start | bytes 491528 | tf_op jit(solution)/shard_map/ppermute | solution.py:378
  126.7 0.7 copy-start.7
  127.4 20.0 %collective-permute-start.9 = (f32[160,256]{1,0:T(8,128)S(1)}, f32[160,256]{1,0:T(8,128)S(1)}, u32[]{:S(2)}, u32[]{:S(2)}) collective-permute-start(f32[160,256]{1,0:T(8,128)S(1)} %fusion.1), channel_id=1, source_target_pairs={{0,6},{1,7},{2,0},{3,1},{4,2},{5,3},{6,4},{7,5},{8,14},{9,15},{10,... | collective-permute-start | bytes 491528 | tf_op jit(solution)/shard_map/ppermute | solution.py:382
  137.7 9.7 %collective-permute-start.8 = (f32[160,256]{1,0:T(8,128)S(1)}, f32[160,256]{1,0:T(8,128)S(1)}, u32[]{:S(2)}, u32[]{:S(2)}) collective-permute-start(f32[160,256]{1,0:T(8,128)S(1)} %fusion.1), channel_id=1, source_target_pairs={{0,4},{1,5},{2,6},{3,7},{4,0},{5,1},{6,2},{7,3},{8,12},{9,13},{10,... | collective-permute-start | bytes 491528 | tf_op jit(solution)/shard_map/ppermute | solution.py:382
  137.7 10.8 %collective-permute-start.7 = (f32[160,256]{1,0:T(8,128)S(1)}, f32[160,256]{1,0:T(8,128)S(1)}, u32[]{:S(2)}, u32[]{:S(2)}) collective-permute-start(f32[160,256]{1,0:T(8,128)S(1)} %fusion.1), channel_id=1, source_target_pairs={{0,2},{1,3},{2,4},{3,5},{4,6},{5,7},{6,0},{7,1},{8,10},{9,11},{10,... | collective-permute-start | bytes 491528 | tf_op jit(solution)/shard_map/ppermute | solution.py:382
  148.5 20.1 %copy-start.1 = (f32[4,160,256]{2,1,0:T(8,128)}, f32[4,160,256]{2,1,0:T(8,128)S(1)}, u32[]{:S(2)}) copy-start(f32[4,160,256]{2,1,0:T(8,128)S(1)} %pad_maximum_fusion.1.own_ref) | copy-start | bytes 1966084
  148.5 20.1 %collective-permute-start.10 = (f32[4,160,256]{2,1,0:T(8,128)S(1)}, f32[4,160,256]{2,1,0:T(8,128)S(1)}, u32[]{:S(2)}, u32[]{:S(2)}) collective-permute-start(f32[4,160,256]{2,1,0:T(8,128)S(1)} %pad_maximum_fusion.1.own_ref), channel_id=1, source_target_pairs={{0,1},{1,0},{2,3},{3,2},{4,5},{5,4},{6,7},{7,6},{8,9},{9,8},{10,11... | collective-permute-start | bytes 1966088 | tf_op jit(solution)/shard_map/ppermute | solution.py:386
  168.6 0.9 copy-start.5
Sparse Core Ops, SparseCore 0:
  33.9 45.6 all-gather.3
  127.5 51.3 all-gather.5

commit v8 on v7

--- a/solution.py
+++ b/solution.py
@@ -69,8 +69,8 @@
     def dot(x, y):
         return jnp.dot(x, y, precision=HIGHEST, preferred_element_type=jnp.float32)
 
-    def chol_panel(at, first):
-        old = [lane(gw[first:], at + k) for k in range(PANEL)]
+    def chol_panel(at):
+        old = [lane(gw[at:], at + k) for k in range(PANEL)]
 
         def solo(a, here, row, tops):
             d = tops[a]
@@ -86,7 +86,7 @@
             return mod, ratio, row, (upper, lower, marks)
 
         _, mods, marks = panel_step(solo, gw[pl.ds(at, PANEL), :], at)
-        update_rows(gw, first, old, mods)
+        update_rows(gw, at, old, mods)
         lt[pl.ds(at, PANEL), :] = jnp.concatenate([m[0] for m in marks], axis=0)
         lw[pl.ds(at, PANEL), :] = jnp.concatenate([m[1] for m in marks], axis=0)
         for a in range(PANEL):
@@ -116,16 +116,10 @@
     def block(gram, top):
         gw[...] = gram
         vr[...] = top
-        chol_panel(0, 0)
-        for first in range(0, H, H // 4):
-
-            def body(i, _, first=first):
-                at = pl.multiple_of(i * PANEL, PANEL)
-                jordan_panel(at - PANEL)
-                chol_panel(at, first)
-                return 0
-
-            lax.fori_loop(max(first // PANEL, 1), (first + H // 4) // PANEL, body, 0)
+        chol_panel(0)
+        for at in range(PANEL, H, PANEL):
+            jordan_panel(at - PANEL)
+            chol_panel(at)
         jordan_panel(H - PANEL)
         return lt[...], lw[...], vr[...]
 
@@ -158,6 +152,7 @@
         out_shape=[jax.ShapeDtypeStruct((W, W), jnp.float32)] * 2,
         in_specs=[vmem],
         out_specs=[vmem] * 2,
+        compiler_params=pltpu.CompilerParams(vmem_limit_bytes=8 * 1024 * 1024),
         scratch_shapes=[square] * 4 + [pltpu.VMEM((PANEL, PANEL + 2, H), jnp.float32), pltpu.VMEM((W, 2 * W), jnp.float32)],
         cost_estimate=pl.CostEstimate(flops=2 * W**3, bytes_accessed=16 * W * W, transcendentals=0),
     )(pieces)
@@ -180,6 +175,8 @@
 NN = ((1,), (0,))
 NT = ((1,), (1,))
 VMEM_BYTES = 60 * 1024 * 1024
+TILE = 512
+EARLY = 1
 
 
 def dots(a, b, contract):
@@ -314,32 +311,88 @@
     )(place, left, own, other, coupling_t, inner)
 
 
-def update_kernel(a_ref, left_ref, wleft_ref, right_ref, weights_ref, out_ref):
+def early_kernel(a_ref, left_ref, right_ref, out_ref):
+    out_ref[...] = a_ref[...] - jnp.dot(left_ref[...], right_ref[...], preferred_element_type=jnp.float32)
+
+
+def early(trailing, weight_left, right):
+    rows = trailing.shape[0]
+    return pl.pallas_call(
+        early_kernel,
+        grid=(EARLY,),
+        out_shape=jax.ShapeDtypeStruct((rows, EARLY * TILE), jnp.float32),
+        in_specs=[
+            pl.BlockSpec((rows, TILE), lambda i: (0, i)),
+            pl.BlockSpec((rows, 3 * W), lambda i: (0, 0)),
+            pl.BlockSpec((3 * W, TILE), lambda i: (0, i)),
+        ],
+        out_specs=pl.BlockSpec((rows, TILE), lambda i: (0, i)),
+        compiler_params=pltpu.CompilerParams(vmem_limit_bytes=VMEM_BYTES),
+        cost_estimate=pl.CostEstimate(flops=6 * EARLY * TILE * rows * W, bytes_accessed=8 * EARLY * TILE * rows, transcendentals=0),
+    )(trailing, weight_left, right)
+
+
+def update_kernel(a_ref, early_ref, left_ref, wleft_ref, right_ref, weights_ref, out_ref, wleft, held, copies):
+    step = pl.program_id(0)
+    late = pl.num_programs(0) - EARLY
+    second_left = pltpu.make_async_copy(wleft_ref, wleft, copies.at[EARLY])
+    fetches = [
+        pltpu.make_async_copy(early_ref.at[:, e * TILE : (e + 1) * TILE], held.at[e], copies.at[e]) for e in range(EARLY)
+    ]
+
+    @pl.when(step == 0)
+    def _():
+        second_left.start()
+        for fetch in fetches:
+            fetch.start()
+
     high, low = split(weights_ref[...].T)
     right = jnp.concatenate([high, low, high], axis=0)
     first = jnp.dot(left_ref[...], right, preferred_element_type=jnp.float32)
-    second = jnp.dot(wleft_ref[...], right_ref[...], preferred_element_type=jnp.float32)
-    out_ref[...] = a_ref[...] - (first + second)
-
-
-def update(trailing, left, weight_left, right, weight_cols):
+
+    @pl.when(step == 0)
+    def _():
+        second_left.wait()
+
+    @pl.when(step < late)
+    def _():
+        second = jnp.dot(wleft[...], right_ref[...], preferred_element_type=jnp.float32)
+        out_ref[...] = a_ref[...] - (first + second)
+
+    for e in range(EARLY):
+
+        @pl.when(step == late + e)
+        def _(e=e):
+            fetches[e].wait()
+            out_ref[...] = held[e] - first
+
+
+def update(trailing, early_cols, left, weight_left, right, weight_cols):
     rows, cols = trailing.shape
-    tile = 512
+    steps = cols // TILE
+    late = steps - EARLY
+    anywhere = pl.BlockSpec(memory_space=pl.ANY)
     return pl.pallas_call(
         update_kernel,
-        grid=(cols // tile,),
+        grid=(steps,),
         out_shape=jax.ShapeDtypeStruct((rows, cols), jnp.float32),
         in_specs=[
-            pl.BlockSpec((rows, tile), lambda i: (0, i)),
+            pl.BlockSpec((rows, TILE), lambda i: (0, EARLY + jnp.minimum(i, late - 1))),
+            anywhere,
             pl.BlockSpec((rows, 3 * W), lambda i: (0, 0)),
-            pl.BlockSpec((rows, 3 * W), lambda i: (0, 0)),
-            pl.BlockSpec((3 * W, tile), lambda i: (0, i)),
-            pl.BlockSpec((tile, W), lambda i: (i, 0)),
+            anywhere,
+            pl.BlockSpec((3 * W, TILE), lambda i: (0, EARLY + jnp.minimum(i, late - 1))),
+            pl.BlockSpec((TILE, W), lambda i: ((i + EARLY) % steps, 0)),
         ],
-        out_specs=pl.BlockSpec((rows, tile), lambda i: (0, i)),
+        out_specs=pl.BlockSpec((rows, TILE), lambda i: (0, (i + EARLY) % steps)),
+        scratch_shapes=[
+            pltpu.VMEM((rows, 3 * W), jnp.bfloat16),
+            pltpu.VMEM((EARLY, rows, TILE), jnp.float32),
+            pltpu.SemaphoreType.DMA((EARLY + 1,)),
+        ],
         compiler_params=pltpu.CompilerParams(vmem_limit_bytes=VMEM_BYTES),
         cost_estimate=pl.CostEstimate(flops=12 * rows * cols * W, bytes_accessed=8 * rows * cols, transcendentals=0),
-    )(trailing, left, weight_left, right, weight_cols)
+    )(trailing, early_cols, left, weight_left, right, weight_cols)
 
 
 def shards(trailing, panel_block):
@@ -388,7 +441,8 @@
     inner = lax.all_to_all(inner, BOTH, 0, 0, tiled=True).reshape((nr, nc) + inner.shape[1:])
     inner = from_tiles(inner.transpose(1, 0, 2, 3).reshape(-1, 8, H), W, W)
     weight_left = correct(place, left, line, other, coupling_t, inner)
-    return update(trailing, left, weight_left, right, weight_cols)
+    early_cols = early(trailing, weight_left, right)
+    return update(trailing, early_cols, left, weight_left, right, weight_cols)
 
 
 def solution(mesh):

time: 204 us -> 201 us (0.985)
  waiting for transfers between devices: 32.4 us -> 27.9 us
    pallas_call x1 -> x2, Pallas kernels: 17.8 us -> 22.8 us  [the longest x1 17.5 us: update(): pl.pallas_call(update_kernel, grid=(steps,), out_shape=jax.ShapeDtypeStru...]
    all_gather x1, waiting for transfers between devices: 4.26 us -> 0.01 us  [shards(): weight_cols = lax.all_gather(moved, 'row', axis=0, tiled=True)]
    pallas_call x1, Pallas kernels: 17.6 us -> 13.9 us  [factor(): pl.pallas_call(factor_kernel, out_shape=[jax.ShapeDtypeStruct((W, W), jnp...]
  transfers between devices with their start and end apart: 14 -> 14, of which waited for: 9 -> 8; matrix products, arithmetic and copies ran while one was open for 2% -> 2% of each run, Pallas kernels for 14% -> 15%
where the time goes in v8:
time: 201 us; the launch traced here: 200 us
  blocking collectives  58.6 us (29%)
  Pallas kernels  58.5 us (29%)
  starting transfers between devices  31.9 us (16%)
  waiting for transfers between devices  27.9 us (14%)
  between operations  13.6 us (7%)
  local copies, waits for them, and re-layouts  5.47 us (3%)
  other arithmetic  2.92 us (1%)
    all_gather x1, blocking collectives, shards(): line = lax.all_gather(panel_t, 'col', axis=0, axis_index_groups=lines)  21.6 us
    pallas_call x1, Pallas kernels, update(): pl.pallas_call(update_kernel, grid=(steps,), out_shape=jax.ShapeDtypeStru...  17.5 us
    all_to_all x1, blocking collectives, shards(): lax.all_to_all(inner, BOTH, 0, 0, tiled=True)  17 us
    pallas_call x1, Pallas kernels, factor(): pl.pallas_call(factor_kernel, out_shape=[jax.ShapeDtypeStruct((W, W), jnp...  13.9 us
    all_to_all x1, waiting for transfers between devices, shards(): lax.all_to_all(jnp.broadcast_to(mine[None], (nr * nc,) + mine.shape), BOT...  12.7 us
    pallas_call x1, Pallas kernels, product(): pl.pallas_call(product_kernel, grid=(cols // tile,), out_shape=[out, out]...  11.6 us
    ppermute x3, starting transfers between devices, shards(): lax.ppermute(mine, 'col', shift)  11 us
    all_to_all x1, blocking collectives, shards(): mine = jnp.sum(lax.all_to_all(pieces, 'row', 0, 0, tiled=True), axis=0)  10.9 us
  transfers between devices with their start and end apart: 14, of which 8 were waited for; matrix products, arithmetic and copies ran while one was open for 2% of the time, Pallas kernels for 15%

profile of v8, /device:TPU:1, one launch (start us, length us, event | category | flops | bytes accessed | tf_op | source)
XLA Modules:
  0.0 200.5 jit_solution(17228984375638704832)
XLA Ops:
  6.5 4.9 %collective-permute-start = (f32[32,1280]{1,0:T(8,128)}, f32[32,1280]{1,0:T(8,128)S(1)}, u32[]{:S(2)}, u32[]{:S(2)}) collective-permute-start(f32[32,1280]{1,0:T(8,128)} %bitcast.60), channel_id=1, source_target_pairs={{0,0},{1,8},{2,16},{3,24},{4,32},{5,40},{6,48},{7,56},{8,64},{9,72... | collective-permute-start | bytes 491528 | tf_op jit(solution)/shard_map/ppermute | solution.py:411
  11.5 21.6 %all-gather = f32[128,1280]{1,0:T(8,128)S(1)} all-gather(f32[32,1280]{1,0:T(8,128)} %bitcast.61), channel_id=2, replica_groups={{0,2,4,6},{1,3,5,7},{8,10,12,14},{9,11,13,15},{16,18,20,22},{17,19,21,2..., dimensions={0}, use_global_device_ids=true | all-gather | bytes 819200 | tf_op jit(solution)/shard_map/all_gather | solution.py:412
  33.1 0.7 copy-done.6
  33.8 0.0 all-gather.4.cloned.1.call-update
  33.8 1.1 collective-permute-start.1
  34.9 0.8 slice_select_fusion
  35.6 1.0 collective-permute-done.1
  36.6 0.1 select_bitcast_fusion.1
  36.7 0.0 copy-start.4
  36.7 0.1 pad_maximum_fusion
  36.8 0.0 copy-start.2
  36.8 0.8 copy-done.4
  37.6 1.2 convolution_bitcast_fusion
  38.9 10.9 %all_to_all.20 = f32[16,8,128]{2,1,0:T(8,128)S(1)} all-to-all(f32[16,8,128]{2,1,0:T(8,128)S(1)} %bitcast.64), channel_id=1, replica_groups=mesh['row'=16,'col'=8] {'row'}, dimensions={0} | all-to-all | bytes 131072 | tf_op jit(solution)/shard_map/all_to_all | solution.py:421
  49.8 0.8 broadcast_in_dim.7
  50.6 5.8 %all-to-all-start.1 = ((f32[128,8,128]{2,1,0:T(8,128)}), f32[128,8,128]{2,1,0:T(8,128)S(1)}, u32[]{:S(2)}, u32[]{:S(2)}) async-start(f32[128,8,128]{2,1,0:T(8,128)} %broadcast_in_dim.7), calls=%async_computation.1 | async-start | bytes 1048576 | tf_op jit(solution)/shard_map/all_to_all | solution.py:422
  56.4 0.2 all-gather.6.cloned.1.call-start
  56.7 0.6 pad_add_fusion.place_ref
  57.2 12.7 %all-to-all-done.1.pieces_ref = f32[128,8,128]{2,1,0:T(8,128)S(1)} async-done(((f32[128,8,128]{2,1,0:T(8,128)}), f32[128,8,128]{2,1,0:T(8,128)S(1)}, u32[]{:S(2)}, u32[]{:S(2)}) %all-to-all-start.1) | async-done | bytes 524320 | tf_op jit(solution)/shard_map/all_to_all | solution.py:422
  70.0 13.9 %shard_map.28 = (f32[256,256]{1,0:T(8,128)S(1)}, f32[256,256]{1,0:T(8,128)S(1)}) custom-call(f32[128,8,128]{2,1,0:T(8,128)S(1)} %all-to-all-done.1.pieces_ref), custom_call_target="tpu_custom_call" | custom-call | flops 33554432 | bytes 1048576 | tf_op jit(solution)/shard_map/pallas_call | solution.py:150
  83.8 0.7 copy-done.1
  84.5 11.6 %shard_map.29 = (f32[4,192,256]{2,1,0:T(8,128)}, f32[4,192,256]{2,1,0:T(8,128)}) custom-call(s32[2]{0:T(128)} %pad_add_fusion.place_ref, f32[1280,2560]{1,0:T(8,128)} %a_ref.5, f32[2,256,1280]{2,1,0:T(8,128)} %bitcast.54, f32[256,1280]{1,0:T(8,128)} %bitcast.52, f32[256,256]{1,0:T(8,128)} %copy-done.1), custom_call_target="tpu_custom_call" | custom-call | flops 5033164800 | bytes 13107200 | tf_op jit(solution)/shard_map/pallas_call | solution.py:230
  96.1 1.1 collective-permute-start.2
  97.3 2.1 %collective-permute-done.2 = f32[4,192,256]{2,1,0:T(8,128)S(1)} collective-permute-done((f32[4,192,256]{2,1,0:T(8,128)}, f32[4,192,256]{2,1,0:T(8,128)S(1)}, u32[]{:S(2)}, u32[]{:S(2)}) %collective-permute-start.2) | collective-permute-done | bytes 786464 | tf_op jit(solution)/shard_map/ppermute | solution.py:425
  99.4 1.2 add.17
  100.7 0.5 collective-permute-start.4
  101.2 2.1 %collective-permute-start.5 = (f32[192,256]{1,0:T(8,128)S(1)}, f32[192,256]{1,0:T(8,128)S(1)}, u32[]{:S(2)}, u32[]{:S(2)}) collective-permute-start(f32[192,256]{1,0:T(8,128)S(1)} %get-tuple-element.36), channel_id=1, source_target_pairs={{0,6},{1,7},{2,0},{3,1},{4,2},{5,3},{6,4},{7,5},{8,14},{9,15},{10,... | collective-permute-start | bytes 589832 | tf_op jit(solution)/shard_map/ppermute | solution.py:427
  103.2 5.1 %collective-permute-done.4 = f32[192,256]{1,0:T(8,128)S(1)} collective-permute-done((f32[192,256]{1,0:T(8,128)S(1)}, f32[192,256]{1,0:T(8,128)S(1)}, u32[]{:S(2)}, u32[]{:S(2)}) %collective-permute-start.4) | collective-permute-done | bytes 196640 | tf_op jit(solution)/shard_map/ppermute | solution.py:427
  108.4 2.3 %collective-permute-done.5 = f32[192,256]{1,0:T(8,128)S(1)} collective-permute-done((f32[192,256]{1,0:T(8,128)S(1)}, f32[192,256]{1,0:T(8,128)S(1)}, u32[]{:S(2)}, u32[]{:S(2)}) %collective-permute-start.5) | collective-permute-done | bytes 196640 | tf_op jit(solution)/shard_map/ppermute | solution.py:427
  110.6 2.6 %collective-permute-done.3 = f32[192,256]{1,0:T(8,128)S(1)} collective-permute-done((f32[192,256]{1,0:T(8,128)S(1)}, f32[192,256]{1,0:T(8,128)S(1)}, u32[]{:S(2)}, u32[]{:S(2)}) %collective-permute-start.3) | collective-permute-done | bytes 196640 | tf_op jit(solution)/shard_map/ppermute | solution.py:427
  113.3 0.1 fusion
  113.3 0.4 fusion.1
  113.8 2.9 %collective-permute-start.6 = (f32[160,256]{1,0:T(8,128)S(1)}, f32[160,256]{1,0:T(8,128)S(1)}, u32[]{:S(2)}, u32[]{:S(2)}) collective-permute-start(f32[160,256]{1,0:T(8,128)S(1)} %fusion.1), channel_id=1, source_target_pairs={{0,0},{1,8},{2,16},{3,24},{4,32},{5,40},{6,48},{7,56},{8,64},{9,72... | collective-permute-start | bytes 491528 | tf_op jit(solution)/shard_map/ppermute | solution.py:431
  116.7 5.1 %shard_map.30 = (bf16[1280,768]{1,0:T(8,128)(2,1)}, bf16[768,2560]{1,0:T(8,128)(2,1)}) custom-call(s32[2]{0:T(128)} %pad_add_fusion.place_ref, f32[2,256,1280]{2,1,0:T(8,128)} %bitcast.55, f32[256,1280]{1,0:T(8,128)} %bitcast.53, f32[256,256]{1,0:T(8,128)} %copy-done.1), custom_call_target="tpu_custom_call" | custom-call | flops 2621440 | bytes 9830400 | tf_op jit(solution)/shard_map/pallas_call | solution.py:274
  121.7 1.1 collective-permute-done.6
  122.8 0.7 copy-done.7
  123.5 0.0 all-gather.6.cloned.1.call-update
  123.5 10.3 %collective-permute-start.9 = (f32[160,256]{1,0:T(8,128)S(1)}, f32[160,256]{1,0:T(8,128)S(1)}, u32[]{:S(2)}, u32[]{:S(2)}) collective-permute-start(f32[160,256]{1,0:T(8,128)S(1)} %fusion.1), channel_id=1, source_target_pairs={{0,6},{1,7},{2,0},{3,1},{4,2},{5,3},{6,4},{7,5},{8,14},{9,15},{10,... | collective-permute-start | bytes 491528 | tf_op jit(solution)/shard_map/ppermute | solution.py:435
  133.8 0.7 collective-permute-start.7
  134.5 9.1 %all_to_all.21 = f32[16,4,128]{2,1,0:T(4,128)S(1)} all-to-all(f32[16,4,128]{2,1,0:T(4,128)S(1)} %bitcast.68), channel_id=1, replica_groups=mesh['row'=16,'col'=8] {'row'}, dimensions={0} | all-to-all | bytes 65536 | tf_op jit(solution)/shard_map/all_to_all | solution.py:437
  143.6 0.9 collective-permute-done.7
  144.6 2.3 %collective-permute-start.10 = (f32[4,160,256]{2,1,0:T(8,128)S(1)}, f32[4,160,256]{2,1,0:T(8,128)S(1)}, u32[]{:S(2)}, u32[]{:S(2)}) collective-permute-start(f32[4,160,256]{2,1,0:T(8,128)S(1)} %pad_maximum_fusion.1.own_ref), channel_id=1, source_target_pairs={{0,1},{1,0},{2,3},{3,2},{4,5},{5,4},{6,7},{7,6},{8,9},{9,8},{10,11... | collective-permute-start | bytes 1966088 | tf_op jit(solution)/shard_map/ppermute | solution.py:439
  146.9 17.0 %all_to_all.22 = f32[128,4,128]{2,1,0:T(4,128)S(1)} all-to-all(f32[128,4,128]{2,1,0:T(4,128)S(1)} %broadcast_in_dim.8), channel_id=1, replica_groups=mesh['row'=16,'col'=8] {'row','col'}, dimensions={0} | all-to-all | bytes 524288 | tf_op jit(solution)/shard_map/all_to_all | solution.py:441
  163.9 0.9 copy.9
  164.8 0.8 copy-done.5
  165.6 5.2 %shard_map.31.left_ref.wleft_ref = bf16[1280,768]{1,0:T(8,128)(2,1)} custom-call(s32[2]{0:T(128)} %pad_add_fusion.place_ref, bf16[1280,768]{1,0:T(8,128)(2,1)} %get-tuple-element.28.left_ref, f32[4,160,256]{2,1,0:T(8,128)} %copy-done.3, f32[4,160,256]{2,1,0:T(8,128)} %copy-done.5, f32[256,256]{1,0:T(8,128)} %copy-done, f32[256,256]{1,0:T(8,128)} %bitcast.58), custom_call_target="tpu_custom_call" | custom-call | flops 503316480 | bytes 7864320 | tf_op jit(solution)/shard_map/pallas_call | solution.py:304
  170.8 5.3 %shard_map.32.early_ref = f32[1280,512]{1,0:T(8,128)} custom-call(f32[1280,2560]{1,0:T(8,128)} %a_ref.5, bf16[1280,768]{1,0:T(8,128)(2,1)} %shard_map.31.left_ref.wleft_ref, bf16[768,2560]{1,0:T(8,128)(2,1)} %get-tuple-element.31.right_ref), custom_call_target="tpu_custom_call" | custom-call | flops 1006632960 | bytes 5242880 | tf_op jit(solution)/shard_map/pallas_call | solution.py:320
  176.2 17.5 %shard_map.33 = f32[1280,2560]{1,0:T(8,128)} custom-call(f32[1280,2560]{1,0:T(8,128)} %a_ref.5, f32[1280,512]{1,0:T(8,128)} %shard_map.32.early_ref, bf16[1280,768]{1,0:T(8,128)(2,1)} %get-tuple-element.28.left_ref, bf16[1280,768]{1,0:T(8,128)(2,1)} %shard_map.31.left_ref.wleft_ref, bf16[768,2560]{1,0:T(8,128)(2,1)} %get-tuple-element.31.right_ref, ...), custom_call_target="tpu_custom_call" | custom-call | flops 10066329600 | bytes 26214400 | tf_op jit(solution)/shard_map/pallas_call | solution.py:375
  (26 shorter events, 0.2 us)
Async XLA Ops:
  6.5 78.0 %all-gather.4.cloned.1.call-start = ((), (), s32[]{:S(2)}) async-start(), calls=%async_computation.4 | async-start | bytes 2785280 | tf_op jit(solution)/shard_map/all_gather | solution.py:417
  6.5 26.5 %collective-permute-start = (f32[32,1280]{1,0:T(8,128)}, f32[32,1280]{1,0:T(8,128)S(1)}, u32[]{:S(2)}, u32[]{:S(2)}) collective-permute-start(f32[32,1280]{1,0:T(8,128)} %bitcast.60), channel_id=1, source_target_pairs={{0,0},{1,8},{2,16},{3,24},{4,32},{5,40},{6,48},{7,56},{8,64},{9,72... | collective-permute-start | bytes 491528 | tf_op jit(solution)/shard_map/ppermute | solution.py:411
  33.1 0.7 copy-start.6
  33.8 2.8 %collective-permute-start.1 = (f32[4,32,1280]{2,1,0:T(8,128)S(1)}, f32[4,32,1280]{2,1,0:T(8,128)S(1)}, u32[]{:S(2)}, u32[]{:S(2)}) collective-permute-start(f32[4,32,1280]{2,1,0:T(8,128)S(1)} %bitcast.56), channel_id=1, source_target_pairs={{0,1},{1,0},{2,3},{3,2},{4,5},{5,4},{6,7},{7,6},{8,9},{9,8},{10,11... | collective-permute-start | bytes 1966088 | tf_op jit(solution)/shard_map/ppermute | solution.py:414
  36.7 0.9 copy-start.4
  36.8 47.0 %copy-start.2 = (f32[4,2,32,1280]{3,2,1,0:T(8,128)}, f32[4,2,32,1280]{3,2,1,0:T(8,128)S(1)}, u32[]{:S(2)}) copy-start(f32[4,2,32,1280]{3,2,1,0:T(8,128)S(1)} %pad_maximum_fusion) | copy-start | bytes 3932164
  50.6 19.3 %all-to-all-start.1 = ((f32[128,8,128]{2,1,0:T(8,128)}), f32[128,8,128]{2,1,0:T(8,128)S(1)}, u32[]{:S(2)}, u32[]{:S(2)}) async-start(f32[128,8,128]{2,1,0:T(8,128)} %broadcast_in_dim.7), calls=%async_computation.1 | async-start | bytes 1048576 | tf_op jit(solution)/shard_map/all_to_all | solution.py:422
  56.4 119.7 %all-gather.6.cloned.1.call-start = ((), (), s32[]{:S(2)}) async-start(), calls=%async_computation.5 | async-start | bytes 2785280 | tf_op jit(solution)/shard_map/all_gather | solution.py:434
  83.8 0.7 copy-start.1
  84.5 28.8 %copy-start = (f32[256,256]{1,0:T(8,128)}, f32[256,256]{1,0:T(8,128)S(1)}, u32[]{:S(2)}) copy-start(f32[256,256]{1,0:T(8,128)S(1)} %get-tuple-element.24.tt_ref) | copy-start | bytes 786436
  96.1 3.2 %collective-permute-start.2 = (f32[4,192,256]{2,1,0:T(8,128)}, f32[4,192,256]{2,1,0:T(8,128)S(1)}, u32[]{:S(2)}, u32[]{:S(2)}) collective-permute-start(f32[4,192,256]{2,1,0:T(8,128)} %get-tuple-element.23), channel_id=1, source_target_pairs={{0,1},{1,0},{2,3},{3,2},{4,5},{5,4},{6,7},{7,6},{8,9},{9,8},{10,11... | collective-permute-start | bytes 2359304 | tf_op jit(solution)/shard_map/ppermute | solution.py:425
  100.7 7.7 %collective-permute-start.4 = (f32[192,256]{1,0:T(8,128)S(1)}, f32[192,256]{1,0:T(8,128)S(1)}, u32[]{:S(2)}, u32[]{:S(2)}) collective-permute-start(f32[192,256]{1,0:T(8,128)S(1)} %get-tuple-element.35), channel_id=1, source_target_pairs={{0,4},{1,5},{2,6},{3,7},{4,0},{5,1},{6,2},{7,3},{8,12},{9,13},{10,... | collective-permute-start | bytes 589832 | tf_op jit(solution)/shard_map/ppermute | solution.py:427
  101.2 9.5 %collective-permute-start.5 = (f32[192,256]{1,0:T(8,128)S(1)}, f32[192,256]{1,0:T(8,128)S(1)}, u32[]{:S(2)}, u32[]{:S(2)}) collective-permute-start(f32[192,256]{1,0:T(8,128)S(1)} %get-tuple-element.36), channel_id=1, source_target_pairs={{0,6},{1,7},{2,0},{3,1},{4,2},{5,3},{6,4},{7,5},{8,14},{9,15},{10,... | collective-permute-start | bytes 589832 | tf_op jit(solution)/shard_map/ppermute | solution.py:427
  103.2 10.0 %collective-permute-start.3 = (f32[192,256]{1,0:T(8,128)S(1)}, f32[192,256]{1,0:T(8,128)S(1)}, u32[]{:S(2)}, u32[]{:S(2)}) collective-permute-start(f32[192,256]{1,0:T(8,128)S(1)} %get-tuple-element.37), channel_id=1, source_target_pairs={{0,2},{1,3},{2,4},{3,5},{4,6},{5,7},{6,0},{7,1},{8,10},{9,11},{10,... | collective-permute-start | bytes 589832 | tf_op jit(solution)/shard_map/ppermute | solution.py:427
  113.8 9.0 %collective-permute-start.6 = (f32[160,256]{1,0:T(8,128)S(1)}, f32[160,256]{1,0:T(8,128)S(1)}, u32[]{:S(2)}, u32[]{:S(2)}) collective-permute-start(f32[160,256]{1,0:T(8,128)S(1)} %fusion.1), channel_id=1, source_target_pairs={{0,0},{1,8},{2,16},{3,24},{4,32},{5,40},{6,48},{7,56},{8,64},{9,72... | collective-permute-start | bytes 491528 | tf_op jit(solution)/shard_map/ppermute | solution.py:431
  122.8 0.7 copy-start.7
  123.5 20.1 %collective-permute-start.9 = (f32[160,256]{1,0:T(8,128)S(1)}, f32[160,256]{1,0:T(8,128)S(1)}, u32[]{:S(2)}, u32[]{:S(2)}) collective-permute-start(f32[160,256]{1,0:T(8,128)S(1)} %fusion.1), channel_id=1, source_target_pairs={{0,6},{1,7},{2,0},{3,1},{4,2},{5,3},{6,4},{7,5},{8,14},{9,15},{10,... | collective-permute-start | bytes 491528 | tf_op jit(solution)/shard_map/ppermute | solution.py:435
  133.8 9.8 %collective-permute-start.8 = (f32[160,256]{1,0:T(8,128)S(1)}, f32[160,256]{1,0:T(8,128)S(1)}, u32[]{:S(2)}, u32[]{:S(2)}) collective-permute-start(f32[160,256]{1,0:T(8,128)S(1)} %fusion.1), channel_id=1, source_target_pairs={{0,4},{1,5},{2,6},{3,7},{4,0},{5,1},{6,2},{7,3},{8,12},{9,13},{10,... | collective-permute-start | bytes 491528 | tf_op jit(solution)/shard_map/ppermute | solution.py:435
  133.8 10.8 %collective-permute-start.7 = (f32[160,256]{1,0:T(8,128)S(1)}, f32[160,256]{1,0:T(8,128)S(1)}, u32[]{:S(2)}, u32[]{:S(2)}) collective-permute-start(f32[160,256]{1,0:T(8,128)S(1)} %fusion.1), channel_id=1, source_target_pairs={{0,2},{1,3},{2,4},{3,5},{4,6},{5,7},{6,0},{7,1},{8,10},{9,11},{10,... | collective-permute-start | bytes 491528 | tf_op jit(solution)/shard_map/ppermute | solution.py:435
  144.6 20.2 %copy-start.3 = (f32[4,160,256]{2,1,0:T(8,128)}, f32[4,160,256]{2,1,0:T(8,128)S(1)}, u32[]{:S(2)}) copy-start(f32[4,160,256]{2,1,0:T(8,128)S(1)} %pad_maximum_fusion.1.own_ref) | copy-start | bytes 1966084
  144.6 20.2 %collective-permute-start.10 = (f32[4,160,256]{2,1,0:T(8,128)S(1)}, f32[4,160,256]{2,1,0:T(8,128)S(1)}, u32[]{:S(2)}, u32[]{:S(2)}) collective-permute-start(f32[4,160,256]{2,1,0:T(8,128)S(1)} %pad_maximum_fusion.1.own_ref), channel_id=1, source_target_pairs={{0,1},{1,0},{2,3},{3,2},{4,5},{5,4},{6,7},{7,6},{8,9},{9,8},{10,11... | collective-permute-start | bytes 1966088 | tf_op jit(solution)/shard_map/ppermute | solution.py:439
  164.8 0.8 copy-start.5
Sparse Core Ops, SparseCore 0:
  33.9 45.6 all-gather.3
  123.6 51.4 all-gather.5

commit v9 on v8

--- a/solution.py
+++ b/solution.py
@@ -187,12 +187,14 @@
     return lax.dot_general(left, right, (contract, ((), ())), preferred_element_type=jnp.float32)
 
 
-def product_kernel(place_ref, a_ref, cols_ref, rows_ref, lt_ref, keep_ref, send_ref, acc, inner_scr):
+def product_kernel(place_ref, a_ref, cols_ref, rows_ref, lt_ref, keep_ref, send_ref, acc, inner_scr, panel, arrived):
     step = pl.program_id(0)
     steps = pl.num_programs(0)
+    fetch = pltpu.make_async_copy(rows_ref, panel, arrived)
 
     @pl.when(step == 0)
     def _():
+        fetch.start()
         own = (place_ref[1] == 0).astype(jnp.float32)
         cols = cols_ref[0]
         cols = jnp.concatenate([cols[:, :W] + own * lt_ref[...].T, cols[:, W:]], axis=1)
@@ -204,9 +206,10 @@
 
     @pl.when(step == steps - 1)
     def _():
+        fetch.wait()
         own = (place_ref[0] == 0).astype(jnp.float32)
-        inner = dots(rows_ref[:, :W] + own * lt_ref[...].T, acc[:W], NN)
-        inner = inner + dots(rows_ref[:, W:], acc[W:], NN)
+        inner = dots(panel[:, :W] + own * lt_ref[...].T, acc[:W], NN)
+        inner = inner + dots(panel[:, W:], acc[W:], NN)
         inner_scr[...] = inner
         lines = keep_ref.shape[0]
         part = acc.shape[0] // (2 * lines)
@@ -235,11 +238,16 @@
             pl.BlockSpec(memory_space=pltpu.SMEM),
             pl.BlockSpec((rows, tile), lambda i: (0, i)),
             pl.BlockSpec((1, W, tile), lambda i: (i // per, 0, i % per)),
-            pl.BlockSpec((W, rows), lambda i: (0, 0)),
+            pl.BlockSpec(memory_space=pl.ANY),
             pl.BlockSpec((W, W), lambda i: (0, 0)),
         ],
         out_specs=[out_spec, out_spec],
-        scratch_shapes=[pltpu.VMEM((rows, W), jnp.float32), pltpu.VMEM((W, W), jnp.float32)],
+        scratch_shapes=[
+            pltpu.VMEM((rows, W), jnp.float32),
+            pltpu.VMEM((W, W), jnp.float32),
+            pltpu.VMEM((W, rows), jnp.float32),
+            pltpu.SemaphoreType.DMA,
+        ],
         compiler_params=pltpu.CompilerParams(vmem_limit_bytes=VMEM_BYTES),
         cost_estimate=pl.CostEstimate(flops=6 * rows * cols * W, bytes_accessed=4 * rows * cols, transcendentals=0),
     )(place, trailing, panel_cols, panel_rows, factor_t)
@@ -263,8 +271,8 @@
                 cols = cols + lt.T * (place_ref[1] == 0).astype(jnp.float32)
             high, low = split(cols)
             at = slice(h * half + i * W, h * half + (i + 1) * W)
-            for p, part in enumerate((high, low, high)):
-                right_ref[p * W : (p + 1) * W, at] = part
+            right_ref[:W, at] = high
+            right_ref[W:, at] = low
 
 
 def parts_of(place, panel_cols, panel_rows, factor_t):
@@ -273,7 +281,7 @@
     vmem = pl.BlockSpec(memory_space=pltpu.VMEM)
     return pl.pallas_call(
         parts_kernel,
-        out_shape=[jax.ShapeDtypeStruct(shape, jnp.bfloat16) for shape in ((rows, 3 * W), (3 * W, cols))],
+        out_shape=[jax.ShapeDtypeStruct(shape, jnp.bfloat16) for shape in ((rows, 3 * W), (2 * W, cols))],
         in_specs=[pl.BlockSpec(memory_space=pltpu.SMEM)] + [vmem] * 3,
         out_specs=[vmem] * 2,
         compiler_params=pltpu.CompilerParams(vmem_limit_bytes=VMEM_BYTES),
@@ -311,8 +319,13 @@
     )(place, left, own, other, coupling_t, inner)
 
 
+def stacked(ref):
+    high = ref[:W]
+    return jnp.concatenate([high, ref[W:], high], axis=0)
+
+
 def early_kernel(a_ref, left_ref, right_ref, out_ref):
-    out_ref[...] = a_ref[...] - jnp.dot(left_ref[...], right_ref[...], preferred_element_type=jnp.float32)
+    out_ref[...] = a_ref[...] - jnp.dot(left_ref[...], stacked(right_ref), preferred_element_type=jnp.float32)
 
 
 def early(trailing, weight_left, right):
@@ -324,7 +337,7 @@
         in_specs=[
             pl.BlockSpec((rows, TILE), lambda i: (0, i)),
             pl.BlockSpec((rows, 3 * W), lambda i: (0, 0)),
-            pl.BlockSpec((3 * W, TILE), lambda i: (0, i)),
+            pl.BlockSpec((2 * W, TILE), lambda i: (0, i)),
         ],
         out_specs=pl.BlockSpec((rows, TILE), lambda i: (0, i)),
         compiler_params=pltpu.CompilerParams(vmem_limit_bytes=VMEM_BYTES),
@@ -356,7 +369,7 @@
 
     @pl.when(step < late)
     def _():
-        second = jnp.dot(wleft[...], right_ref[...], preferred_element_type=jnp.float32)
+        second = jnp.dot(wleft[...], stacked(right_ref), preferred_element_type=jnp.float32)
         out_ref[...] = a_ref[...] - (first + second)
 
     for e in range(EARLY):
@@ -381,7 +394,7 @@
             anywhere,
             pl.BlockSpec((rows, 3 * W), lambda i: (0, 0)),
             anywhere,
-            pl.BlockSpec((3 * W, TILE), lambda i: (0, EARLY + jnp.minimum(i, late - 1))),
+            pl.BlockSpec((2 * W, TILE), lambda i: (0, EARLY + jnp.minimum(i, late - 1))),
             pl.BlockSpec((TILE, W), lambda i: ((i + EARLY) % steps, 0)),
         ],
         out_specs=pl.BlockSpec((rows, TILE), lambda i: (0, (i + EARLY) % steps)),

time: 201 us -> 200 us (level)
  no operation moved by 1% of the time
where the time goes in v9:
time: 200 us
  blocking collectives  58.6 us (29%)
  Pallas kernels  57.5 us (29%)
  starting transfers between devices  32 us (16%)
  waiting for transfers between devices  28 us (14%)
  between operations  13.6 us (7%)
  local copies, waits for them, and re-layouts  5.52 us (3%)
  other arithmetic  2.94 us (1%)
    all_gather x1, blocking collectives, shards(): line = lax.all_gather(panel_t, 'col', axis=0, axis_index_groups=lines)  21.6 us
    pallas_call x1, Pallas kernels, update(): pl.pallas_call(update_kernel, grid=(steps,), out_shape=jax.ShapeDtypeStru...  17.2 us
    all_to_all x1, blocking collectives, shards(): lax.all_to_all(inner, BOTH, 0, 0, tiled=True)  17 us
    pallas_call x1, Pallas kernels, factor(): pl.pallas_call(factor_kernel, out_shape=[jax.ShapeDtypeStruct((W, W), jnp...  13.9 us
    all_to_all x1, waiting for transfers between devices, shards(): lax.all_to_all(jnp.broadcast_to(mine[None], (nr * nc,) + mine.shape), BOT...  12.7 us
    pallas_call x1, Pallas kernels, product(): pl.pallas_call(product_kernel, grid=(cols // tile,), out_shape=[out, out]...  11.2 us
    ppermute x3, starting transfers between devices, shards(): lax.ppermute(mine, 'col', shift)  11 us
    all_to_all x1, blocking collectives, shards(): mine = jnp.sum(lax.all_to_all(pieces, 'row', 0, 0, tiled=True), axis=0)  10.9 us
  transfers between devices with their start and end apart: 14, of which 8 were waited for; matrix products, arithmetic and copies ran while one was open for 2% of the time, Pallas kernels for 15%

profile of v9, /device:TPU:1, one launch (start us, length us, event | category | flops | bytes accessed | tf_op | source)
XLA Modules:
  0.0 199.8 jit_solution(3623208156286864104)
XLA Ops:
  6.5 4.9 %collective-permute-start = (f32[32,1280]{1,0:T(8,128)}, f32[32,1280]{1,0:T(8,128)S(1)}, u32[]{:S(2)}, u32[]{:S(2)}) collective-permute-start(f32[32,1280]{1,0:T(8,128)} %bitcast.60), channel_id=1, source_target_pairs={{0,0},{1,8},{2,16},{3,24},{4,32},{5,40},{6,48},{7,56},{8,64},{9,72... | collective-permute-start | bytes 491528 | tf_op jit(solution)/shard_map/ppermute | solution.py:424
  11.5 21.6 %all-gather = f32[128,1280]{1,0:T(8,128)S(1)} all-gather(f32[32,1280]{1,0:T(8,128)} %bitcast.61), channel_id=2, replica_groups={{0,2,4,6},{1,3,5,7},{8,10,12,14},{9,11,13,15},{16,18,20,22},{17,19,21,2..., dimensions={0}, use_global_device_ids=true | all-gather | bytes 819200 | tf_op jit(solution)/shard_map/all_gather | solution.py:425
  33.1 0.7 copy-done.6
  33.8 0.0 all-gather.4.cloned.1.call-update
  33.8 1.1 collective-permute-start.1
  34.9 0.8 slice_select_fusion
  35.6 1.0 collective-permute-done.1
  36.6 0.1 select_bitcast_fusion.1
  36.7 0.1 pad_maximum_fusion
  36.8 0.0 copy-start.2
  36.8 0.8 copy-done.4
  37.6 1.2 convolution_bitcast_fusion
  38.9 10.9 %all_to_all.20 = f32[16,8,128]{2,1,0:T(8,128)S(1)} all-to-all(f32[16,8,128]{2,1,0:T(8,128)S(1)} %bitcast.64), channel_id=1, replica_groups=mesh['row'=16,'col'=8] {'row'}, dimensions={0} | all-to-all | bytes 131072 | tf_op jit(solution)/shard_map/all_to_all | solution.py:434
  49.8 0.8 broadcast_in_dim.7
  50.6 5.8 %all-to-all-start.1 = ((f32[128,8,128]{2,1,0:T(8,128)}), f32[128,8,128]{2,1,0:T(8,128)S(1)}, u32[]{:S(2)}, u32[]{:S(2)}) async-start(f32[128,8,128]{2,1,0:T(8,128)} %broadcast_in_dim.7), calls=%async_computation.1 | async-start | bytes 1048576 | tf_op jit(solution)/shard_map/all_to_all | solution.py:435
  56.4 0.2 all-gather.6.cloned.1.call-start
  56.7 0.6 pad_add_fusion.place_ref
  57.3 12.7 %all-to-all-done.1.pieces_ref = f32[128,8,128]{2,1,0:T(8,128)S(1)} async-done(((f32[128,8,128]{2,1,0:T(8,128)}), f32[128,8,128]{2,1,0:T(8,128)S(1)}, u32[]{:S(2)}, u32[]{:S(2)}) %all-to-all-start.1) | async-done | bytes 524320 | tf_op jit(solution)/shard_map/all_to_all | solution.py:435
  70.0 13.9 %shard_map.28 = (f32[256,256]{1,0:T(8,128)S(1)}, f32[256,256]{1,0:T(8,128)S(1)}) custom-call(f32[128,8,128]{2,1,0:T(8,128)S(1)} %all-to-all-done.1.pieces_ref), custom_call_target="tpu_custom_call" | custom-call | flops 33554432 | bytes 1048576 | tf_op jit(solution)/shard_map/pallas_call | solution.py:150
  83.8 0.7 copy-done.1
  84.6 11.2 %shard_map.29 = (f32[4,192,256]{2,1,0:T(8,128)}, f32[4,192,256]{2,1,0:T(8,128)}) custom-call(s32[2]{0:T(128)} %pad_add_fusion.place_ref, f32[1280,2560]{1,0:T(8,128)} %a_ref.5, f32[2,256,1280]{2,1,0:T(8,128)} %bitcast.54, f32[256,1280]{1,0:T(8,128)} %bitcast.52, f32[256,256]{1,0:T(8,128)} %copy-done.1), custom_call_target="tpu_custom_call" | custom-call | flops 5033164800 | bytes 13107200 | tf_op jit(solution)/shard_map/pallas_call | solution.py:233
  95.8 1.2 collective-permute-start.2
  97.0 2.1 %collective-permute-done.2 = f32[4,192,256]{2,1,0:T(8,128)S(1)} collective-permute-done((f32[4,192,256]{2,1,0:T(8,128)}, f32[4,192,256]{2,1,0:T(8,128)S(1)}, u32[]{:S(2)}, u32[]{:S(2)}) %collective-permute-start.2) | collective-permute-done | bytes 786464 | tf_op jit(solution)/shard_map/ppermute | solution.py:438
  99.1 1.2 add.17
  100.4 0.5 collective-permute-start.4
  100.9 2.1 %collective-permute-start.5 = (f32[192,256]{1,0:T(8,128)S(1)}, f32[192,256]{1,0:T(8,128)S(1)}, u32[]{:S(2)}, u32[]{:S(2)}) collective-permute-start(f32[192,256]{1,0:T(8,128)S(1)} %get-tuple-element.36), channel_id=1, source_target_pairs={{0,6},{1,7},{2,0},{3,1},{4,2},{5,3},{6,4},{7,5},{8,14},{9,15},{10,... | collective-permute-start | bytes 589832 | tf_op jit(solution)/shard_map/ppermute | solution.py:440
  103.0 5.1 %collective-permute-done.4 = f32[192,256]{1,0:T(8,128)S(1)} collective-permute-done((f32[192,256]{1,0:T(8,128)S(1)}, f32[192,256]{1,0:T(8,128)S(1)}, u32[]{:S(2)}, u32[]{:S(2)}) %collective-permute-start.4) | collective-permute-done | bytes 196640 | tf_op jit(solution)/shard_map/ppermute | solution.py:440
  108.1 2.3 %collective-permute-done.5 = f32[192,256]{1,0:T(8,128)S(1)} collective-permute-done((f32[192,256]{1,0:T(8,128)S(1)}, f32[192,256]{1,0:T(8,128)S(1)}, u32[]{:S(2)}, u32[]{:S(2)}) %collective-permute-start.5) | collective-permute-done | bytes 196640 | tf_op jit(solution)/shard_map/ppermute | solution.py:440
  110.4 2.6 %collective-permute-done.3 = f32[192,256]{1,0:T(8,128)S(1)} collective-permute-done((f32[192,256]{1,0:T(8,128)S(1)}, f32[192,256]{1,0:T(8,128)S(1)}, u32[]{:S(2)}, u32[]{:S(2)}) %collective-permute-start.3) | collective-permute-done | bytes 196640 | tf_op jit(solution)/shard_map/ppermute | solution.py:440
  113.0 0.1 fusion
  113.1 0.4 fusion.1
  113.5 2.9 %collective-permute-start.6 = (f32[160,256]{1,0:T(8,128)S(1)}, f32[160,256]{1,0:T(8,128)S(1)}, u32[]{:S(2)}, u32[]{:S(2)}) collective-permute-start(f32[160,256]{1,0:T(8,128)S(1)} %fusion.1), channel_id=1, source_target_pairs={{0,0},{1,8},{2,16},{3,24},{4,32},{5,40},{6,48},{7,56},{8,64},{9,72... | collective-permute-start | bytes 491528 | tf_op jit(solution)/shard_map/ppermute | solution.py:444
  116.4 4.9 %shard_map.30 = (bf16[1280,768]{1,0:T(8,128)(2,1)}, bf16[512,2560]{1,0:T(8,128)(2,1)}) custom-call(s32[2]{0:T(128)} %pad_add_fusion.place_ref, f32[2,256,1280]{2,1,0:T(8,128)} %bitcast.55, f32[256,1280]{1,0:T(8,128)} %bitcast.53, f32[256,256]{1,0:T(8,128)} %copy-done.1), custom_call_target="tpu_custom_call" | custom-call | flops 2621440 | bytes 9830400 | tf_op jit(solution)/shard_map/pallas_call | solution.py:282
  121.3 1.2 collective-permute-done.6
  122.5 0.7 copy-done.7
  123.2 0.0 all-gather.6.cloned.1.call-update
  123.2 10.3 %collective-permute-start.9 = (f32[160,256]{1,0:T(8,128)S(1)}, f32[160,256]{1,0:T(8,128)S(1)}, u32[]{:S(2)}, u32[]{:S(2)}) collective-permute-start(f32[160,256]{1,0:T(8,128)S(1)} %fusion.1), channel_id=1, source_target_pairs={{0,6},{1,7},{2,0},{3,1},{4,2},{5,3},{6,4},{7,5},{8,14},{9,15},{10,... | collective-permute-start | bytes 491528 | tf_op jit(solution)/shard_map/ppermute | solution.py:448
  133.5 0.7 collective-permute-start.7
  134.2 9.1 %all_to_all.21 = f32[16,4,128]{2,1,0:T(4,128)S(1)} all-to-all(f32[16,4,128]{2,1,0:T(4,128)S(1)} %bitcast.68), channel_id=1, replica_groups=mesh['row'=16,'col'=8] {'row'}, dimensions={0} | all-to-all | bytes 65536 | tf_op jit(solution)/shard_map/all_to_all | solution.py:450
  143.4 1.0 collective-permute-done.7
  144.4 0.0 copy-start.3
  144.4 2.3 %collective-permute-start.10 = (f32[4,160,256]{2,1,0:T(8,128)S(1)}, f32[4,160,256]{2,1,0:T(8,128)S(1)}, u32[]{:S(2)}, u32[]{:S(2)}) collective-permute-start(f32[4,160,256]{2,1,0:T(8,128)S(1)} %pad_maximum_fusion.1.own_ref), channel_id=1, source_target_pairs={{0,1},{1,0},{2,3},{3,2},{4,5},{5,4},{6,7},{7,6},{8,9},{9,8},{10,11... | collective-permute-start | bytes 1966088 | tf_op jit(solution)/shard_map/ppermute | solution.py:452
  146.7 17.0 %all_to_all.22 = f32[128,4,128]{2,1,0:T(4,128)S(1)} all-to-all(f32[128,4,128]{2,1,0:T(4,128)S(1)} %broadcast_in_dim.8), channel_id=1, replica_groups=mesh['row'=16,'col'=8] {'row','col'}, dimensions={0} | all-to-all | bytes 524288 | tf_op jit(solution)/shard_map/all_to_all | solution.py:454
  163.7 0.9 copy.9
  164.6 0.8 copy-done.5
  165.4 5.1 %shard_map.31.left_ref.wleft_ref = bf16[1280,768]{1,0:T(8,128)(2,1)} custom-call(s32[2]{0:T(128)} %pad_add_fusion.place_ref, bf16[1280,768]{1,0:T(8,128)(2,1)} %get-tuple-element.28.left_ref, f32[4,160,256]{2,1,0:T(8,128)} %copy-done.3, f32[4,160,256]{2,1,0:T(8,128)} %copy-done.5, f32[256,256]{1,0:T(8,128)} %copy-done, f32[256,256]{1,0:T(8,128)} %bitcast.58), custom_call_target="tpu_custom_call" | custom-call | flops 503316480 | bytes 7864320 | tf_op jit(solution)/shard_map/pallas_call | solution.py:312
  170.5 5.2 %shard_map.32.early_ref = f32[1280,512]{1,0:T(8,128)} custom-call(f32[1280,2560]{1,0:T(8,128)} %a_ref.5, bf16[1280,768]{1,0:T(8,128)(2,1)} %shard_map.31.left_ref.wleft_ref, bf16[512,2560]{1,0:T(8,128)(2,1)} %get-tuple-element.31.right_ref), custom_call_target="tpu_custom_call" | custom-call | flops 1006632960 | bytes 5242880 | tf_op jit(solution)/shard_map/pallas_call | solution.py:333
  175.7 17.2 %shard_map.33 = f32[1280,2560]{1,0:T(8,128)} custom-call(f32[1280,2560]{1,0:T(8,128)} %a_ref.5, f32[1280,512]{1,0:T(8,128)} %shard_map.32.early_ref, bf16[1280,768]{1,0:T(8,128)(2,1)} %get-tuple-element.28.left_ref, bf16[1280,768]{1,0:T(8,128)(2,1)} %shard_map.31.left_ref.wleft_ref, bf16[512,2560]{1,0:T(8,128)(2,1)} %get-tuple-element.31.right_ref, ...), custom_call_target="tpu_custom_call" | custom-call | flops 10066329600 | bytes 26214400 | tf_op jit(solution)/shard_map/pallas_call | solution.py:388
  (26 shorter events, 0.2 us)
Async XLA Ops:
  6.5 78.0 %all-gather.4.cloned.1.call-start = ((), (), s32[]{:S(2)}) async-start(), calls=%async_computation.4 | async-start | bytes 2785280 | tf_op jit(solution)/shard_map/all_gather | solution.py:430
  6.5 26.5 %collective-permute-start = (f32[32,1280]{1,0:T(8,128)}, f32[32,1280]{1,0:T(8,128)S(1)}, u32[]{:S(2)}, u32[]{:S(2)}) collective-permute-start(f32[32,1280]{1,0:T(8,128)} %bitcast.60), channel_id=1, source_target_pairs={{0,0},{1,8},{2,16},{3,24},{4,32},{5,40},{6,48},{7,56},{8,64},{9,72... | collective-permute-start | bytes 491528 | tf_op jit(solution)/shard_map/ppermute | solution.py:424
  33.1 0.7 copy-start.6
  33.8 2.8 %collective-permute-start.1 = (f32[4,32,1280]{2,1,0:T(8,128)S(1)}, f32[4,32,1280]{2,1,0:T(8,128)S(1)}, u32[]{:S(2)}, u32[]{:S(2)}) collective-permute-start(f32[4,32,1280]{2,1,0:T(8,128)S(1)} %bitcast.56), channel_id=1, source_target_pairs={{0,1},{1,0},{2,3},{3,2},{4,5},{5,4},{6,7},{7,6},{8,9},{9,8},{10,11... | collective-permute-start | bytes 1966088 | tf_op jit(solution)/shard_map/ppermute | solution.py:427
  36.7 0.9 copy-start.4
  36.8 47.0 %copy-start.2 = (f32[4,2,32,1280]{3,2,1,0:T(8,128)}, f32[4,2,32,1280]{3,2,1,0:T(8,128)S(1)}, u32[]{:S(2)}) copy-start(f32[4,2,32,1280]{3,2,1,0:T(8,128)S(1)} %pad_maximum_fusion) | copy-start | bytes 3932164
  50.6 19.3 %all-to-all-start.1 = ((f32[128,8,128]{2,1,0:T(8,128)}), f32[128,8,128]{2,1,0:T(8,128)S(1)}, u32[]{:S(2)}, u32[]{:S(2)}) async-start(f32[128,8,128]{2,1,0:T(8,128)} %broadcast_in_dim.7), calls=%async_computation.1 | async-start | bytes 1048576 | tf_op jit(solution)/shard_map/all_to_all | solution.py:435
  56.4 119.2 %all-gather.6.cloned.1.call-start = ((), (), s32[]{:S(2)}) async-start(), calls=%async_computation.5 | async-start | bytes 2785280 | tf_op jit(solution)/shard_map/all_gather | solution.py:447
  83.8 0.7 copy-start.1
  84.6 28.5 %copy-start = (f32[256,256]{1,0:T(8,128)}, f32[256,256]{1,0:T(8,128)S(1)}, u32[]{:S(2)}) copy-start(f32[256,256]{1,0:T(8,128)S(1)} %get-tuple-element.24.tt_ref) | copy-start | bytes 786436
  95.8 3.3 %collective-permute-start.2 = (f32[4,192,256]{2,1,0:T(8,128)}, f32[4,192,256]{2,1,0:T(8,128)S(1)}, u32[]{:S(2)}, u32[]{:S(2)}) collective-permute-start(f32[4,192,256]{2,1,0:T(8,128)} %get-tuple-element.23), channel_id=1, source_target_pairs={{0,1},{1,0},{2,3},{3,2},{4,5},{5,4},{6,7},{7,6},{8,9},{9,8},{10,11... | collective-permute-start | bytes 2359304 | tf_op jit(solution)/shard_map/ppermute | solution.py:438
  100.4 7.7 %collective-permute-start.4 = (f32[192,256]{1,0:T(8,128)S(1)}, f32[192,256]{1,0:T(8,128)S(1)}, u32[]{:S(2)}, u32[]{:S(2)}) collective-permute-start(f32[192,256]{1,0:T(8,128)S(1)} %get-tuple-element.35), channel_id=1, source_target_pairs={{0,4},{1,5},{2,6},{3,7},{4,0},{5,1},{6,2},{7,3},{8,12},{9,13},{10,... | collective-permute-start | bytes 589832 | tf_op jit(solution)/shard_map/ppermute | solution.py:440
  100.9 9.5 %collective-permute-start.5 = (f32[192,256]{1,0:T(8,128)S(1)}, f32[192,256]{1,0:T(8,128)S(1)}, u32[]{:S(2)}, u32[]{:S(2)}) collective-permute-start(f32[192,256]{1,0:T(8,128)S(1)} %get-tuple-element.36), channel_id=1, source_target_pairs={{0,6},{1,7},{2,0},{3,1},{4,2},{5,3},{6,4},{7,5},{8,14},{9,15},{10,... | collective-permute-start | bytes 589832 | tf_op jit(solution)/shard_map/ppermute | solution.py:440
  103.0 10.0 %collective-permute-start.3 = (f32[192,256]{1,0:T(8,128)S(1)}, f32[192,256]{1,0:T(8,128)S(1)}, u32[]{:S(2)}, u32[]{:S(2)}) collective-permute-start(f32[192,256]{1,0:T(8,128)S(1)} %get-tuple-element.37), channel_id=1, source_target_pairs={{0,2},{1,3},{2,4},{3,5},{4,6},{5,7},{6,0},{7,1},{8,10},{9,11},{10,... | collective-permute-start | bytes 589832 | tf_op jit(solution)/shard_map/ppermute | solution.py:440
  113.5 9.0 %collective-permute-start.6 = (f32[160,256]{1,0:T(8,128)S(1)}, f32[160,256]{1,0:T(8,128)S(1)}, u32[]{:S(2)}, u32[]{:S(2)}) collective-permute-start(f32[160,256]{1,0:T(8,128)S(1)} %fusion.1), channel_id=1, source_target_pairs={{0,0},{1,8},{2,16},{3,24},{4,32},{5,40},{6,48},{7,56},{8,64},{9,72... | collective-permute-start | bytes 491528 | tf_op jit(solution)/shard_map/ppermute | solution.py:444
  122.5 0.7 copy-start.7
  123.2 20.1 %collective-permute-start.9 = (f32[160,256]{1,0:T(8,128)S(1)}, f32[160,256]{1,0:T(8,128)S(1)}, u32[]{:S(2)}, u32[]{:S(2)}) collective-permute-start(f32[160,256]{1,0:T(8,128)S(1)} %fusion.1), channel_id=1, source_target_pairs={{0,6},{1,7},{2,0},{3,1},{4,2},{5,3},{6,4},{7,5},{8,14},{9,15},{10,... | collective-permute-start | bytes 491528 | tf_op jit(solution)/shard_map/ppermute | solution.py:448
  133.5 9.8 %collective-permute-start.8 = (f32[160,256]{1,0:T(8,128)S(1)}, f32[160,256]{1,0:T(8,128)S(1)}, u32[]{:S(2)}, u32[]{:S(2)}) collective-permute-start(f32[160,256]{1,0:T(8,128)S(1)} %fusion.1), channel_id=1, source_target_pairs={{0,4},{1,5},{2,6},{3,7},{4,0},{5,1},{6,2},{7,3},{8,12},{9,13},{10,... | collective-permute-start | bytes 491528 | tf_op jit(solution)/shard_map/ppermute | solution.py:448
  133.5 10.8 %collective-permute-start.7 = (f32[160,256]{1,0:T(8,128)S(1)}, f32[160,256]{1,0:T(8,128)S(1)}, u32[]{:S(2)}, u32[]{:S(2)}) collective-permute-start(f32[160,256]{1,0:T(8,128)S(1)} %fusion.1), channel_id=1, source_target_pairs={{0,2},{1,3},{2,4},{3,5},{4,6},{5,7},{6,0},{7,1},{8,10},{9,11},{10,... | collective-permute-start | bytes 491528 | tf_op jit(solution)/shard_map/ppermute | solution.py:448
  144.4 20.2 %copy-start.3 = (f32[4,160,256]{2,1,0:T(8,128)}, f32[4,160,256]{2,1,0:T(8,128)S(1)}, u32[]{:S(2)}) copy-start(f32[4,160,256]{2,1,0:T(8,128)S(1)} %pad_maximum_fusion.1.own_ref) | copy-start | bytes 1966084
  144.4 20.2 %collective-permute-start.10 = (f32[4,160,256]{2,1,0:T(8,128)S(1)}, f32[4,160,256]{2,1,0:T(8,128)S(1)}, u32[]{:S(2)}, u32[]{:S(2)}) collective-permute-start(f32[4,160,256]{2,1,0:T(8,128)S(1)} %pad_maximum_fusion.1.own_ref), channel_id=1, source_target_pairs={{0,1},{1,0},{2,3},{3,2},{4,5},{5,4},{6,7},{7,6},{8,9},{9,8},{10,11... | collective-permute-start | bytes 1966088 | tf_op jit(solution)/shard_map/ppermute | solution.py:452
  164.6 0.8 copy-start.5
Sparse Core Ops, SparseCore 0:
  33.9 45.6 all-gather.3
  123.3 51.4 all-gather.5
